TPU v7x, 32 devices: a whole 2x2x4 slice. The times are simulated.
32 devices in a mesh: blk: 16 (over z, y, x), grp: 2 (over core).
Axes of the slice: x: 2, y: 2, z: 4, core: 2. Of those that a mesh axis runs over, the one named last changes fastest.
Arguments:
- image_emb: bfloat16 [8192, 1152], P(('blk', 'grp')), may hold values from -8 to 8
- text_emb: bfloat16 [8192, 1152], P(('blk', 'grp')), may hold values from -8 to 8
- log_temp: float32 [1], replicated, may hold values from 1.6 to 2.8
- bias: float32 [1], replicated, may hold values from -3 to -1
Outputs:
- grad_image: float32 [8192, 1152], P(('blk', 'grp'))
- grad_text: float32 [8192, 1152], P(('blk', 'grp'))
- statistics: float32 [3], replicated
All inputs are finite; a program needn't handle non-finite values.
Results may differ from a plain program's by a relative error of at most 0.00032.
Values may be sent and summed in bfloat16 or wider, within the bound.
No kernel may reach another device: no remote copies, remote signals or barrier semaphores. Data moves between devices by JAX's collectives and lax.ppermute only.
A program may use at most 64 MiB of HBM per device.

v0:
```python
import jax
import jax.numpy as jnp
from jax import lax
from jax.sharding import PartitionSpec as P

REACH = 2


def passed_along(block, axis, distance):
    devices = range(lax.axis_size(axis))
    route = [((i - distance) % len(devices), i) for i in devices]
    return lax.ppermute(block, axis, route)


def normalize(raw_rows):
    widened = raw_rows.astype(jnp.float32)
    inverse = 1.0 / jnp.sqrt(jnp.sum(widened * widened, axis=1, keepdims=True) + 1e-06)
    return (widened * inverse, inverse)


def tile_slope(img_unit, visitor, temper, offset_bias, diagonal):
    row_count = img_unit.shape[0]
    similar = lax.dot_general(
        img_unit, visitor, (((1,), (1,)), ((), ())), preferred_element_type=jnp.float32
    )
    logits = temper * similar + offset_bias
    if diagonal:
        ident = lax.broadcasted_iota(jnp.int32, (row_count, row_count), 0) == lax.broadcasted_iota(
            jnp.int32, (row_count, row_count), 1
        )
        labels = jnp.where(ident, 1.0, -1.0).astype(jnp.float32)
    else:
        labels = -jnp.ones((row_count, row_count), jnp.float32)
    margin = -labels * logits
    slope = -labels * jax.nn.sigmoid(margin)
    totals = (jnp.sum(jax.nn.softplus(margin)), jnp.sum(slope * temper * similar), jnp.sum(slope))
    scaled = (temper * slope).astype(jnp.bfloat16)
    return (totals, scaled)


def image_side(scaled, visitor):
    return jnp.dot(scaled, visitor, preferred_element_type=jnp.float32)


def text_side(scaled, img_unit):
    return lax.dot_general(
        scaled, img_unit, (((0,), (0,)), ((), ())), preferred_element_type=jnp.float32
    )


def pair_tile(img_unit, visitor, temper, offset_bias, diagonal):
    totals, scaled = tile_slope(img_unit, visitor, temper, offset_bias, diagonal)
    return (totals, image_side(scaled, visitor), text_side(scaled, img_unit))


def relay_text(visitor, heading):
    return passed_along(visitor, "blk", heading)


def relay_acc(carried, heading):
    return passed_along(carried, "blk", heading)


def send_home(carried, distance):
    return passed_along(carried, "blk", distance)


def on_device(image_emb, text_emb, log_temp, bias):
    row_count = image_emb.shape[0]
    reach_steps = REACH
    img_wide, img_inv = normalize(image_emb)
    txt_wide, txt_inv = normalize(text_emb)
    img_unit = img_wide.astype(jnp.bfloat16)
    txt_unit = txt_wide.astype(jnp.bfloat16)
    temper = jnp.exp(log_temp[0])
    offset_bias = bias[0]
    totals, grad_img, grad_txt = pair_tile(img_unit, txt_unit, temper, offset_bias, True)
    for heading in (1, -1):
        visitor = txt_unit
        carried = jnp.zeros_like(grad_txt)
        for relay_step in range(reach_steps):
            visitor = relay_text(visitor, heading)
            if relay_step > 0:
                carried = relay_acc(carried, heading)
            part_totals, part_img, part_txt = pair_tile(
                img_unit, visitor, temper, offset_bias, False
            )
            totals = tuple((a + b for a, b in zip(totals, part_totals)))
            grad_img = grad_img + part_img
            carried = carried + part_txt
        grad_txt = grad_txt + send_home(carried, -heading * reach_steps)
    summed = lax.psum((totals[0], totals[1], totals[2]), ("blk", "grp"))
    pair_count = jnp.float32(
        row_count * row_count * (2 * reach_steps + 1) * lax.axis_size("blk") * lax.axis_size("grp")
    )
    statistics = jnp.stack([summed[0], summed[1], summed[2]]) / pair_count
    grad_image = img_inv * (
        grad_img - img_wide * jnp.sum(img_wide * grad_img, axis=1, keepdims=True)
    )
    grad_text = txt_inv * (
        grad_txt - txt_wide * jnp.sum(txt_wide * grad_txt, axis=1, keepdims=True)
    )
    return (grad_image, grad_text, statistics)


def solution(mesh):
    placed = (P(("blk", "grp"), None), P(("blk", "grp"), None), P(), P())
    return jax.shard_map(
        on_device,
        mesh=mesh,
        in_specs=placed,
        out_specs=(P(("blk", "grp"), None), P(("blk", "grp"), None), P()),
        check_vma=False,
    )
```

profile of v0, /device:TPU:0, one launch (start us, length us, event | category | flops | bytes accessed | tf_op | source)
XLA Modules:
  0.0 222.9 jit_solution(4804532491303277277)
XLA Ops:
  0.6 0.0 copy-start
  0.6 1.3 fusion.14
  2.0 1.2 fusion.3
  3.2 7.0 %collective-permute-start.2 = (bf16[256,1152]{1,0:T(8,128)(2,1)S(1)}, bf16[256,1152]{1,0:T(8,128)(2,1)}, u32[]{:S(2)}, u32[]{:S(2)}) collective-permute-start(bf16[256,1152]{1,0:T(8,128)(2,1)S(1)} %fusion.3), channel_id=1, source_target_pairs={{2,0},{4,2},{6,4},{8,6},{10,8},{12,10},{14,12},{16,14},{18,16},{20... | collective-permute-start | bytes 1769480 | tf_op jit(solution)/shard_map/ppermute | solution.py:12
  10.2 0.0 collective-permute-start
  10.2 0.0 copy-done
  10.2 0.2 fusion.10
  11.8 1.3 fusion.15
  13.0 0.0 copy-start.4
  13.0 0.4 fusion.21
  13.4 9.4 %collective-permute-done.2 = bf16[256,1152]{1,0:T(8,128)(2,1)} collective-permute-done((bf16[256,1152]{1,0:T(8,128)(2,1)S(1)}, bf16[256,1152]{1,0:T(8,128)(2,1)}, u32[]{:S(2)}, u32[]{:S(2)}) %collective-permute-start.2) | collective-permute-done | bytes 589856 | tf_op jit(solution)/shard_map/ppermute | solution.py:12
  22.8 2.3 %fusion.18 = (f32[]{:T(128)}, f32[]{:T(128)}, f32[]{:T(128)}, f32[256,256]{1,0:T(8,128)S(1)}) fusion(f32[]{:T(128)} %bitcast.18, f32[]{:T(128)} %bitcast, bf16[256,1152]{1,0:T(8,128)(2,1)} %collective-permute-done.2, bf16[256,1152]{1,0:T(8,128)(2,1)S(1)} %copy-done, f32[256]{0:T(256)S(1)} %add_rsqrt_fusion.1), kind=kOutput, calls=%fused_computation.33 | convolution fusion | flops 152928256 | bytes 1442836 | tf_op jit(solution)/shard_map/dot_general | solution.py:23
  25.1 0.0 copy-done.4
  25.1 1.4 fusion.23
  26.5 13.2 %collective-permute-start.6 = (f32[256,1152]{1,0:T(8,128)}, f32[256,1152]{1,0:T(8,128)}, u32[]{:S(2)}, u32[]{:S(2)}) collective-permute-start(f32[256,1152]{1,0:T(8,128)} %fusion.23), channel_id=1, source_target_pairs={{2,0},{4,2},{6,4},{8,6},{10,8},{12,10},{14,12},{16,14},{18,16},{20... | collective-permute-start | bytes 3538952 | tf_op jit(solution)/shard_map/ppermute | solution.py:12
  39.7 0.0 collective-permute-done
  39.7 0.0 collective-permute-start.1
  39.7 2.3 %fusion.16 = (f32[]{:T(128)}, f32[]{:T(128)}, f32[]{:T(128)}, f32[256,256]{1,0:T(8,128)S(1)}) fusion(f32[]{:T(128)} %bitcast.20, f32[]{:T(128)} %bitcast, bf16[256,1152]{1,0:T(8,128)(2,1)} %collective-permute-done, bf16[256,1152]{1,0:T(8,128)(2,1)S(1)} %copy-done, f32[256]{0:T(256)S(1)} %add_rsqrt_fusion.1), kind=kOutput, calls=%fused_computation.31 | convolution fusion | flops 152928256 | bytes 1442836 | tf_op jit(solution)/shard_map/dot_general | solution.py:23
  42.0 0.0 copy-done.6
  42.0 1.4 fusion.22
  43.5 0.0 collective-permute-start.4
  43.5 5.6 %collective-permute-start.3 = (bf16[256,1152]{1,0:T(8,128)(2,1)}, bf16[256,1152]{1,0:T(8,128)(2,1)}, u32[]{:S(2)}, u32[]{:S(2)}) collective-permute-start(bf16[256,1152]{1,0:T(8,128)(2,1)} %collective-permute-done.2), channel_id=1, source_target_pairs={{2,0},{4,2},{6,4},{8,6},{10,8},{12,10},{14,12},{16,14},{18,16},{20... | collective-permute-start | bytes 1769480 | tf_op jit(solution)/shard_map/ppermute | solution.py:12
  49.1 1.4 convolution_add_fusion.4
  54.2 1.5 fusion.24
  55.7 31.9 %collective-permute-done.1 = bf16[256,1152]{1,0:T(8,128)(2,1)S(1)} collective-permute-done((bf16[256,1152]{1,0:T(8,128)(2,1)}, bf16[256,1152]{1,0:T(8,128)(2,1)S(1)}, u32[]{:S(2)}, u32[]{:S(2)}) %collective-permute-start.1) | collective-permute-done | bytes 589856 | tf_op jit(solution)/shard_map/ppermute | solution.py:12
  87.6 0.8 copy-done.2
  88.4 2.3 %fusion.17 = (f32[]{:T(128)}, f32[]{:T(128)}, f32[]{:T(128)}, f32[256,256]{1,0:T(8,128)S(1)}) fusion(f32[]{:T(128)} %bitcast.19, f32[]{:T(128)} %bitcast, bf16[256,1152]{1,0:T(8,128)(2,1)} %copy-done.2, bf16[256,1152]{1,0:T(8,128)(2,1)S(1)} %copy-done, f32[256]{0:T(256)S(1)} %add_rsqrt_fusion.1), kind=kOutput, calls=%fused_computation.32 | convolution fusion | flops 152928256 | bytes 1442836 | tf_op jit(solution)/shard_map/dot_general | solution.py:23
  92.0 16.1 %collective-permute-done.3 = bf16[256,1152]{1,0:T(8,128)(2,1)} collective-permute-done((bf16[256,1152]{1,0:T(8,128)(2,1)}, bf16[256,1152]{1,0:T(8,128)(2,1)}, u32[]{:S(2)}, u32[]{:S(2)}) %collective-permute-start.3) | collective-permute-done | bytes 589856 | tf_op jit(solution)/shard_map/ppermute | solution.py:12
  108.1 2.3 %fusion.19 = (f32[]{:T(128)}, f32[]{:T(128)}, f32[]{:T(128)}, f32[256,256]{1,0:T(8,128)S(1)}) fusion(f32[]{:T(128)} %bitcast.17, f32[]{:T(128)} %bitcast, bf16[256,1152]{1,0:T(8,128)(2,1)} %collective-permute-done.3, bf16[256,1152]{1,0:T(8,128)(2,1)S(1)} %copy-done, f32[256]{0:T(256)S(1)} %add_rsqrt_fusion.1), kind=kOutput, calls=%fused_computation.34 | convolution fusion | flops 152928256 | bytes 1442836 | tf_op jit(solution)/shard_map/dot_general | solution.py:23
  114.8 46.9 %all-reduce = (f32[1]{0:T(128)}, f32[1]{0:T(128)}, f32[1]{0:T(128)}) all-reduce(f32[1]{0:T(128)} %bitcast.4, f32[1]{0:T(128)} %bitcast.3, f32[1]{0:T(128)} %bitcast.2), channel_id=1, replica_groups=mesh['blk'=16,'grp'=2] {'blk','grp'}, use_global_device_ids=true, to_apply=%region_21.22 | all-reduce | flops 3 | bytes 24 | tf_op jit(solution)/shard_map/psum | solution.py:92
  161.7 2.3 %maximum_multiply_fusion = f32[3]{0:T(128)} fusion(f32[1]{0:T(128)} %get-tuple-element.18, f32[1]{0:T(128)} %get-tuple-element.19, f32[1]{0:T(128)} %get-tuple-element.20), kind=kLoop, calls=%fused_computation.64 | loop fusion | flops 9 | bytes 24 | tf_op jit(solution)/shard_map/div | solution.py:96
  164.0 0.0 collective-permute-done.6
  164.0 1.7 convolution_add_fusion
  165.7 2.5 %collective-permute-start.7 = (f32[256,1152]{1,0:T(8,128)S(1)}, f32[256,1152]{1,0:T(8,128)S(1)}, u32[]{:S(2)}, u32[]{:S(2)}) collective-permute-start(f32[256,1152]{1,0:T(8,128)S(1)} %convolution_add_fusion), channel_id=1, source_target_pairs={{28,0},{30,2},{0,4},{2,6},{4,8},{6,10},{8,12},{10,14},{12,16},{14,... | collective-permute-start | bytes 3538952 | tf_op jit(solution)/shard_map/ppermute | solution.py:12
  168.2 0.0 collective-permute-done.4
  168.2 1.7 convolution_add_fusion.1
  170.0 2.3 %collective-permute-start.5 = (f32[256,1152]{1,0:T(8,128)S(1)}, f32[256,1152]{1,0:T(8,128)S(1)}, u32[]{:S(2)}, u32[]{:S(2)}) collective-permute-start(f32[256,1152]{1,0:T(8,128)S(1)} %convolution_add_fusion.1), channel_id=1, source_target_pairs={{4,0},{6,2},{8,4},{10,6},{12,8},{14,10},{16,12},{18,14},{20,16},{2... | collective-permute-start | bytes 3538952 | tf_op jit(solution)/shard_map/ppermute | solution.py:12
  172.3 0.0 copy-done.3
  172.3 0.4 fusion
  172.7 1.5 fusion.7
  174.2 0.0 copy-start.5
  174.2 1.3 fusion.9
  175.5 42.9 %collective-permute-done.7 = f32[256,1152]{1,0:T(8,128)S(1)} collective-permute-done((f32[256,1152]{1,0:T(8,128)S(1)}, f32[256,1152]{1,0:T(8,128)S(1)}, u32[]{:S(2)}, u32[]{:S(2)}) %collective-permute-start.7) | collective-permute-done | bytes 1179680 | tf_op jit(solution)/shard_map/ppermute | solution.py:12
  218.4 2.5 %collective-permute-done.5 = f32[256,1152]{1,0:T(8,128)S(1)} collective-permute-done((f32[256,1152]{1,0:T(8,128)S(1)}, f32[256,1152]{1,0:T(8,128)S(1)}, u32[]{:S(2)}, u32[]{:S(2)}) %collective-permute-start.5) | collective-permute-done | bytes 1179680 | tf_op jit(solution)/shard_map/ppermute | solution.py:12
  220.8 0.0 copy-done.1
  220.8 0.0 copy-done.5
  220.8 0.6 fusion.11
  221.5 1.4 fusion.13
  (6 shorter events, 0.0 us)
Async XLA Ops:
  0.6 9.6 %copy-start = (bf16[256,1152]{1,0:T(8,128)(2,1)S(1)}, bf16[256,1152]{1,0:T(8,128)(2,1)}, u32[]{:S(2)}) copy-start(bf16[256,1152]{1,0:T(8,128)(2,1)} %param.4) | copy-start | bytes 1769476
  3.2 19.6 %collective-permute-start.2 = (bf16[256,1152]{1,0:T(8,128)(2,1)S(1)}, bf16[256,1152]{1,0:T(8,128)(2,1)}, u32[]{:S(2)}, u32[]{:S(2)}) collective-permute-start(bf16[256,1152]{1,0:T(8,128)(2,1)S(1)} %fusion.3), channel_id=1, source_target_pairs={{2,0},{4,2},{6,4},{8,6},{10,8},{12,10},{14,12},{16,14},{18,16},{20... | collective-permute-start | bytes 1769480 | tf_op jit(solution)/shard_map/ppermute | solution.py:12
  10.2 29.5 %collective-permute-start = (bf16[256,1152]{1,0:T(8,128)(2,1)S(1)}, bf16[256,1152]{1,0:T(8,128)(2,1)}, u32[]{:S(2)}, u32[]{:S(2)}) collective-permute-start(bf16[256,1152]{1,0:T(8,128)(2,1)S(1)} %fusion.3), channel_id=1, source_target_pairs={{30,0},{0,2},{2,4},{4,6},{6,8},{8,10},{10,12},{12,14},{14,16},{16,... | collective-permute-start | bytes 1769480 | tf_op jit(solution)/shard_map/ppermute | solution.py:12
  13.0 12.1 %copy-start.4 = (f32[256,256]{1,0:T(8,128)}, f32[256,256]{1,0:T(8,128)S(1)}, u32[]{:S(2)}) copy-start(f32[256,256]{1,0:T(8,128)S(1)} %get-tuple-element.25) | copy-start | bytes 786436
  25.1 16.9 %copy-start.6 = (f32[256,256]{1,0:T(8,128)}, f32[256,256]{1,0:T(8,128)S(1)}, u32[]{:S(2)}) copy-start(f32[256,256]{1,0:T(8,128)S(1)} %get-tuple-element.28) | copy-start | bytes 786436
  26.5 137.5 %collective-permute-start.6 = (f32[256,1152]{1,0:T(8,128)}, f32[256,1152]{1,0:T(8,128)}, u32[]{:S(2)}, u32[]{:S(2)}) collective-permute-start(f32[256,1152]{1,0:T(8,128)} %fusion.23), channel_id=1, source_target_pairs={{2,0},{4,2},{6,4},{8,6},{10,8},{12,10},{14,12},{16,14},{18,16},{20... | collective-permute-start | bytes 3538952 | tf_op jit(solution)/shard_map/ppermute | solution.py:12
  39.7 47.9 %collective-permute-start.1 = (bf16[256,1152]{1,0:T(8,128)(2,1)}, bf16[256,1152]{1,0:T(8,128)(2,1)S(1)}, u32[]{:S(2)}, u32[]{:S(2)}) collective-permute-start(bf16[256,1152]{1,0:T(8,128)(2,1)} %collective-permute-done), channel_id=1, source_target_pairs={{30,0},{0,2},{2,4},{4,6},{6,8},{8,10},{10,12},{12,14},{14,16},{16,... | collective-permute-start | bytes 1769480 | tf_op jit(solution)/shard_map/ppermute | solution.py:12
  43.5 124.8 %collective-permute-start.4 = (f32[256,1152]{1,0:T(8,128)}, f32[256,1152]{1,0:T(8,128)}, u32[]{:S(2)}, u32[]{:S(2)}) collective-permute-start(f32[256,1152]{1,0:T(8,128)} %fusion.22), channel_id=1, source_target_pairs={{30,0},{0,2},{2,4},{4,6},{6,8},{8,10},{10,12},{12,14},{14,16},{16,... | collective-permute-start | bytes 3538952 | tf_op jit(solution)/shard_map/ppermute | solution.py:12
  43.5 64.6 %collective-permute-start.3 = (bf16[256,1152]{1,0:T(8,128)(2,1)}, bf16[256,1152]{1,0:T(8,128)(2,1)}, u32[]{:S(2)}, u32[]{:S(2)}) collective-permute-start(bf16[256,1152]{1,0:T(8,128)(2,1)} %collective-permute-done.2), channel_id=1, source_target_pairs={{2,0},{4,2},{6,4},{8,6},{10,8},{12,10},{14,12},{16,14},{18,16},{20... | collective-permute-start | bytes 1769480 | tf_op jit(solution)/shard_map/ppermute | solution.py:12
  87.6 0.8 copy-start.2
  165.7 52.7 %collective-permute-start.7 = (f32[256,1152]{1,0:T(8,128)S(1)}, f32[256,1152]{1,0:T(8,128)S(1)}, u32[]{:S(2)}, u32[]{:S(2)}) collective-permute-start(f32[256,1152]{1,0:T(8,128)S(1)} %convolution_add_fusion), channel_id=1, source_target_pairs={{28,0},{30,2},{0,4},{2,6},{4,8},{6,10},{8,12},{10,14},{12,16},{14,... | collective-permute-start | bytes 3538952 | tf_op jit(solution)/shard_map/ppermute | solution.py:12
  168.2 4.1 %copy-start.3 = (bf16[256,1152]{1,0:T(8,128)(2,1)S(1)}, bf16[256,1152]{1,0:T(8,128)(2,1)}, u32[]{:S(2)}) copy-start(bf16[256,1152]{1,0:T(8,128)(2,1)} %copy-done.2) | copy-start | bytes 1769476
  170.0 50.8 %collective-permute-start.5 = (f32[256,1152]{1,0:T(8,128)S(1)}, f32[256,1152]{1,0:T(8,128)S(1)}, u32[]{:S(2)}, u32[]{:S(2)}) collective-permute-start(f32[256,1152]{1,0:T(8,128)S(1)} %convolution_add_fusion.1), channel_id=1, source_target_pairs={{4,0},{6,2},{8,4},{10,6},{12,8},{14,10},{16,12},{18,14},{20,16},{2... | collective-permute-start | bytes 3538952 | tf_op jit(solution)/shard_map/ppermute | solution.py:12
  174.2 46.7 %copy-start.1 = (bf16[256,1152]{1,0:T(8,128)(2,1)S(1)}, bf16[256,1152]{1,0:T(8,128)(2,1)}, u32[]{:S(2)}) copy-start(bf16[256,1152]{1,0:T(8,128)(2,1)} %param.5) | copy-start | bytes 1769476
  174.2 46.7 %copy-start.5 = (f32[256,256]{1,0:T(8,128)S(1)}, f32[256,256]{1,0:T(8,128)}, u32[]{:S(2)}) copy-start(f32[256,256]{1,0:T(8,128)} %copy-done.4) | copy-start | bytes 786436
where the time goes:
time: 224 us; the launch traced here: 223 us
  waiting for transfers between devices  103 us (46%)
  blocking collectives  46.9 us (21%)
  starting transfers between devices  30.6 us (14%)
  matrix products  22.7 us (10%)
  between operations  11.4 us (5%)
  other arithmetic  7.72 us (3%)
    ppermute x8, waiting for transfers between devices, passed_along(): return lax.ppermute(block, axis, route)  103 us
    psum x1, blocking collectives, on_device(): summed = lax.psum((totals[0], totals[1], totals[2]), ('blk', 'grp'))  46.9 us
    ppermute x8, starting transfers between devices, passed_along(): return lax.ppermute(block, axis, route)  30.6 us
    dot_general x5, matrix products, tile_slope(): lax.dot_general(img_unit, visitor, (((1,), (1,)), ((), ())), preferred_el...  10.5 us
    dot_general x5, matrix products, text_side(): lax.dot_general(scaled, img_unit, (((0,), (0,)), ((), ())), preferred_ele...  6.93 us
    dot_general x5, matrix products, image_side(): return jnp.dot(scaled, visitor, preferred_element_type=jnp.float32)  5.18 us
  transfers between devices with their start and end apart: 8, of which 5 were waited for; matrix products, arithmetic and copies ran while one was open for 12% of the time, Pallas kernels for 0%

commit v1 on v0

v1 whole, which is shorter than its diff:
```python
import functools

import jax
import jax.numpy as jnp
from jax import lax
from jax.experimental import pallas as pl
from jax.experimental.pallas import tpu as pltpu
from jax.sharding import PartitionSpec as P

REACH = 2
QUAD = 4
VMEM_LIMIT = 48 * 1024 * 1024
IN_VMEM = pl.BlockSpec(memory_space=pltpu.VMEM)
IN_SMEM = pl.BlockSpec(memory_space=pltpu.SMEM)


def unit_rows(raw):
    wide = raw.astype(jnp.float32)
    inverse = 1.0 / jnp.sqrt(jnp.sum(wide * wide, axis=1, keepdims=True) + 1e-06)
    return wide * inverse, inverse


def slopes(similar, temper, offset_bias, diagonal):
    logits = temper * similar + offset_bias
    tail = jnp.exp(-jnp.abs(logits))
    upper = jnp.where(logits >= 0, 1.0, tail) / (1.0 + tail)
    if not diagonal:
        return logits, tail, upper, logits
    lower = jnp.where(logits >= 0, tail, 1.0) / (1.0 + tail)
    same = lax.broadcasted_iota(jnp.int32, similar.shape, 0) == lax.broadcasted_iota(
        jnp.int32, similar.shape, 1
    )
    return logits, tail, jnp.where(same, -lower, upper), jnp.where(same, -logits, logits)


def fold(tile):
    rows, columns = tile.shape
    part = jnp.sum(tile.reshape(rows // 8, 8, columns), axis=0)
    return sum(part[:, c : c + 128] for c in range(0, columns, 128))


def tallies(margin, tail, slope, logits_part):
    pair_loss = jnp.maximum(margin, 0.0) + jnp.log1p(tail)
    return jnp.concatenate([fold(pair_loss), fold(slope * logits_part), fold(slope)], axis=0)


def across(left, right):
    return lax.dot_general(
        left, right, (((1,), (1,)), ((), ())), preferred_element_type=jnp.float32
    )


def own_kernel(scalars, image, text, img_unit, txt_unit, img_inv, txt_inv, gx, gy, stats):
    temper, offset_bias = scalars[0], scalars[1]
    x_wide, x_inv = unit_rows(image[...])
    y_wide, y_inv = unit_rows(text[...])
    x, y = x_wide.astype(jnp.bfloat16), y_wide.astype(jnp.bfloat16)
    img_unit[...] = x
    txt_unit[...] = y
    img_inv[...] = jnp.broadcast_to(x_inv, img_inv.shape)
    txt_inv[...] = jnp.broadcast_to(y_inv, txt_inv.shape)
    similar = across(x, y)
    _, tail, slope, margin = slopes(similar, temper, offset_bias, True)
    stats[...] = tallies(margin, tail, slope, temper * similar)
    scaled = (temper * slope).astype(jnp.bfloat16)
    gx[...] = jnp.dot(scaled, y, preferred_element_type=jnp.float32)
    _, _, slope, _ = slopes(across(y, x), temper, offset_bias, True)
    scaled = (temper * slope).astype(jnp.bfloat16)
    gy[...] = jnp.dot(scaled, x, preferred_element_type=jnp.float32)


def visit_kernel(counted, last, *refs):
    refs = list(refs)
    scalars, own, visitor = refs.pop(0), refs.pop(0), refs.pop(0)
    other = refs.pop(0) if last else None
    acc = refs.pop(0)
    stats = refs.pop(0) if counted else None
    raw, inverse = (refs.pop(0), refs.pop(0)) if last else (None, None)
    out = refs.pop(0)
    temper, offset_bias = scalars[0], scalars[1]
    block = visitor[...].astype(jnp.float32)
    if last:
        block = jnp.where(scalars[2] > 0.5, block, other[...].astype(jnp.float32))
    unit = unit_rows(block)[0].astype(jnp.bfloat16)
    similar = across(own[...], unit)
    logits, tail, slope, _ = slopes(similar, temper, offset_bias, False)
    scaled = (temper * slope).astype(jnp.bfloat16)
    grad = acc[...] + jnp.dot(scaled, unit, preferred_element_type=jnp.float32)
    if last:
        inv = inverse[:, :1]
        wide = raw[...].astype(jnp.float32) * inv
        grad = inv * (grad - wide * jnp.sum(wide * grad, axis=1, keepdims=True))
    out[...] = grad
    if counted:
        tally = stats[...] + tallies(logits, tail, slope, temper * similar)
        if last:
            lane = lax.broadcasted_iota(jnp.int32, (8, 128), 1)
            sums = [jnp.sum(tally[8 * i : 8 * i + 8]) for i in range(3)]
            row = jnp.where(lane == 0, sums[0], jnp.where(lane == 1, sums[1], sums[2]))
            refs[0][...] = jnp.broadcast_to(row[None], refs[0].shape)
        else:
            refs[0][...] = tally


def cost(rows, width, tiles):
    return pl.CostEstimate(
        flops=4 * tiles * rows * rows * width,
        bytes_accessed=12 * rows * width,
        transcendentals=tiles * rows * rows,
    )


def call(kernel, operands, shapes, rows, width, tiles):
    return pl.pallas_call(
        kernel,
        out_shape=shapes,
        in_specs=[IN_SMEM] + [IN_VMEM] * (len(operands) - 1),
        out_specs=tuple(IN_VMEM for _ in shapes),
        compiler_params=pltpu.CompilerParams(vmem_limit_bytes=VMEM_LIMIT),
        cost_estimate=cost(rows, width, tiles),
    )(*operands)


def visit(scalars, own, visitor, acc, stats=None, other=None, finish=None, devices=0):
    rows, width = own.shape
    last = finish is not None
    counted = stats is not None
    operands = [scalars, own, visitor]
    if last:
        operands.append(other)
    operands.append(acc)
    if counted:
        operands.append(stats)
    if last:
        operands += list(finish)
    shapes = [jax.ShapeDtypeStruct((rows, width), jnp.float32)]
    if counted:
        shape = (devices, 8, 128) if last else (24, 128)
        shapes.append(jax.ShapeDtypeStruct(shape, jnp.float32))
    return call(functools.partial(visit_kernel, counted, last), operands, tuple(shapes), rows, width, 1)


def on_device(image, text, log_temp, bias):
    rows, width = image.shape
    blocks = lax.axis_size("blk")
    devices = blocks * lax.axis_size("grp")
    place = lax.axis_index("blk") % QUAD
    everyone = range(blocks)
    f32 = jnp.float32
    scalars = jnp.stack(
        [jnp.exp(log_temp[0]), bias[0], jnp.where((place == 0) | (place == 3), 1.0, 0.0).astype(f32)]
    )

    def send(block, route):
        return lax.ppermute(block, "blk", route)

    beside = [(b, b ^ 1) for b in everyone]
    above = [(b, b ^ 2) for b in everyone]
    beyond = [(b, (b + QUAD if b % QUAD < 2 else b - QUAD) % blocks) for b in everyone]
    corner = [(b, b ^ 1) for b in everyone if b % QUAD in (1, 2)]
    middle_x = [(b, b ^ 1) for b in everyone if b % QUAD in (0, 3)]
    middle_y = [(b, b ^ 2) for b in everyone if b % QUAD in (0, 3)]

    txt_y = send(text, above)
    txt_x = send(text, beside)
    img_y = send(image, above)
    img_x = send(image, beside)

    tile = jax.ShapeDtypeStruct((rows, width), f32)
    unit = jax.ShapeDtypeStruct((rows, width), jnp.bfloat16)
    column = jax.ShapeDtypeStruct((rows, 128), f32)
    img_unit, txt_unit, img_inv, txt_inv, gx, gy, stats = call(
        own_kernel,
        [scalars, image, text],
        (unit, unit, column, column, tile, tile, jax.ShapeDtypeStruct((24, 128), f32)),
        rows,
        width,
        2,
    )

    txt_z = send(txt_y, beyond)
    img_z = send(img_y, beyond)
    txt_z, img_x = lax.optimization_barrier((txt_z, img_x))
    txt_c = send(txt_z, corner)
    txt_m = send(txt_y, middle_x)
    img_m = send(img_x, middle_y)
    img_c = send(img_z, corner)

    gx, stats = visit(scalars, img_unit, txt_y, gx, stats)
    gx, stats = visit(scalars, img_unit, txt_x, gx, stats)
    (gy,) = visit(scalars, txt_unit, img_y, gy)
    (gy,) = visit(scalars, txt_unit, img_x, gy)
    gx, stats = visit(scalars, img_unit, txt_z, gx, stats)
    (gy,) = visit(scalars, txt_unit, img_z, gy)
    grad_image, sums = visit(
        scalars, img_unit, txt_c, gx, stats, txt_m, (image, img_inv), devices
    )
    (grad_text,) = visit(scalars, txt_unit, img_c, gy, None, img_m, (text, txt_inv))
    seen = lax.all_to_all(sums, ("blk", "grp"), 0, 0)
    pairs = jnp.float32(rows * rows * (2 * REACH + 1) * devices)
    statistics = jnp.sum(seen[:, 0, :3], axis=0) / pairs
    return grad_image, grad_text, statistics


def solution(mesh):
    placed = P(("blk", "grp"), None)
    return jax.shard_map(
        on_device,
        mesh=mesh,
        in_specs=(placed, placed, P(), P()),
        out_specs=(placed, placed, P()),
        check_vma=False,
    )
```

time: 224 us -> 83.1 us (0.37)
  waiting for transfers between devices: 103 us -> 22.8 us
  blocking collectives: 46.9 us -> 0 us
  matrix products: 22.7 us -> 0 us
  Pallas kernels: 0 us -> 21.9 us
  between operations: 11.4 us -> 2.16 us
  other arithmetic: 7.72 us -> 1.55 us
  local copies, waits for them, and re-layouts: 0.84 us -> 3.62 us
    ppermute x8 -> x10, waiting for transfers between devices: 103 us -> 22.8 us  [send(): return lax.ppermute(block, 'blk', route)]
    psum x1 -> x0, blocking collectives: 46.9 us -> none  [on_device(): summed = lax.psum((totals[0], totals[1], totals[2]), ('blk', 'grp'))]
    dot_general x15 -> x0, matrix products: 22.7 us -> none  [the longest x5 10.5 us: tile_slope(): lax.dot_general(img_unit, visitor, (((1,), (1,)), ((), ())), preferred_el...]
    pallas_call x0 -> x9, Pallas kernels: none -> 21.9 us  [call(): pl.pallas_call(kernel, out_shape=shapes, in_specs=[IN_SMEM] + [IN_VMEM] *...]
    ppermute x8 -> x10, starting transfers between devices: 30.6 us -> 24.7 us  [send(): return lax.ppermute(block, 'blk', route)]
    all_to_all x0 -> x1, starting transfers between devices: none -> 5.8 us  [on_device(): seen = lax.all_to_all(sums, ('blk', 'grp'), 0, 0)]
    unnamed x14 -> x16, local copies, waits for them, and re-layouts: 0.84 us -> 3.62 us
    mul x2 -> x0, other arithmetic: 2.67 us -> none  [the longest x1 1.4 us: on_device(): txt_inv * (grad_txt - txt_wide * jnp.sum(txt_wide * grad_txt, axis=1, kee...]
  transfers between devices with their start and end apart: 8 -> 11, of which waited for: 5 -> 3; matrix products, arithmetic and copies ran while one was open for 12% -> 0% of each run, Pallas kernels for 0% -> 27%
where the time goes in v1:
time: 83.1 us; the launch traced here: 82.5 us
  starting transfers between devices  30.5 us (37%)
  waiting for transfers between devices  22.8 us (27%)
  Pallas kernels  21.9 us (26%)
  local copies, waits for them, and re-layouts  3.62 us (4%)
  between operations  2.16 us (3%)
  other arithmetic  1.55 us (2%)
    ppermute x10, starting transfers between devices, send(): return lax.ppermute(block, 'blk', route)  24.7 us
    ppermute x10, waiting for transfers between devices, send(): return lax.ppermute(block, 'blk', route)  22.8 us
    pallas_call x9, Pallas kernels, call(): pl.pallas_call(kernel, out_shape=shapes, in_specs=[IN_SMEM] + [IN_VMEM] *...  21.9 us
    all_to_all x1, starting transfers between devices, on_device(): seen = lax.all_to_all(sums, ('blk', 'grp'), 0, 0)  5.8 us
    unnamed x16, local copies, waits for them, and re-layouts  3.62 us
  transfers between devices with their start and end apart: 11, of which 3 were waited for; matrix products, arithmetic and copies ran while one was open for 0% of the time, Pallas kernels for 27%

profile of v1, /device:TPU:0, one launch (start us, length us, event | category | flops | bytes accessed | tf_op | source)
XLA Modules:
  0.0 82.5 jit_solution(15622819984279003611)
XLA Ops:
  0.6 3.0 %collective-permute-start = (bf16[256,1152]{1,0:T(8,128)(2,1)}, bf16[256,1152]{1,0:T(8,128)(2,1)S(1)}, u32[]{:S(2)}, u32[]{:S(2)}) collective-permute-start(bf16[256,1152]{1,0:T(8,128)(2,1)} %refs_5_.1), channel_id=1, source_target_pairs={{0,4},{2,6},{4,0},{6,2},{8,12},{10,14},{12,8},{14,10},{16,20},{18,... | collective-permute-start | bytes 1769480 | tf_op jit(solution)/shard_map/ppermute | solution.py:155
  3.7 0.1 collective-permute-start.6
  3.7 1.9 %collective-permute-start.2 = (bf16[256,1152]{1,0:T(8,128)(2,1)}, bf16[256,1152]{1,0:T(8,128)(2,1)}, u32[]{:S(2)}, u32[]{:S(2)}) collective-permute-start(bf16[256,1152]{1,0:T(8,128)(2,1)} %refs_6_.1), channel_id=1, source_target_pairs={{0,2},{2,0},{4,6},{6,4},{8,10},{10,8},{12,14},{14,12},{16,18},{18,... | collective-permute-start | bytes 1769480 | tf_op jit(solution)/shard_map/ppermute | solution.py:155
  5.7 12.4 %collective-permute-done.refs_2_ = bf16[256,1152]{1,0:T(8,128)(2,1)S(1)} collective-permute-done((bf16[256,1152]{1,0:T(8,128)(2,1)}, bf16[256,1152]{1,0:T(8,128)(2,1)S(1)}, u32[]{:S(2)}, u32[]{:S(2)}) %collective-permute-start) | collective-permute-done | bytes 589856 | tf_op jit(solution)/shard_map/ppermute | solution.py:155
  18.0 2.1 %collective-permute-start.1 = (bf16[256,1152]{1,0:T(8,128)(2,1)S(1)}, bf16[256,1152]{1,0:T(8,128)(2,1)}, u32[]{:S(2)}, u32[]{:S(2)}) collective-permute-start(bf16[256,1152]{1,0:T(8,128)(2,1)S(1)} %collective-permute-done.refs_2_), channel_id=1, source_target_pairs={{0,8},{2,10},{4,28},{6,30},{8,16},{10,18},{12,4},{14,6},{16,24},{1... | collective-permute-start | bytes 1769480 | tf_op jit(solution)/shard_map/ppermute | solution.py:155
  20.1 9.7 %collective-permute-done.6.refs_2_ = bf16[256,1152]{1,0:T(8,128)(2,1)S(1)} collective-permute-done((bf16[256,1152]{1,0:T(8,128)(2,1)}, bf16[256,1152]{1,0:T(8,128)(2,1)S(1)}, u32[]{:S(2)}, u32[]{:S(2)}) %collective-permute-start.6) | collective-permute-done | bytes 589856 | tf_op jit(solution)/shard_map/ppermute | solution.py:155
  29.8 1.8 %collective-permute-start.7 = (bf16[256,1152]{1,0:T(8,128)(2,1)S(1)}, bf16[256,1152]{1,0:T(8,128)(2,1)}, u32[]{:S(2)}, u32[]{:S(2)}) collective-permute-start(bf16[256,1152]{1,0:T(8,128)(2,1)S(1)} %collective-permute-done.6.refs_2_), channel_id=1, source_target_pairs={{0,8},{2,10},{4,28},{6,30},{8,16},{10,18},{12,4},{14,6},{16,24},{1... | collective-permute-start | bytes 1769480 | tf_op jit(solution)/shard_map/ppermute | solution.py:155
  31.6 0.0 copy-start.3
  31.6 0.8 copy-done.3
  32.5 1.5 %collective-permute-start.5 = (bf16[256,1152]{1,0:T(8,128)(2,1)}, bf16[256,1152]{1,0:T(8,128)(2,1)}, u32[]{:S(2)}, u32[]{:S(2)}) collective-permute-start(bf16[256,1152]{1,0:T(8,128)(2,1)} %refs_5_.1), channel_id=1, source_target_pairs={{0,2},{2,0},{4,6},{6,4},{8,10},{10,8},{12,14},{14,12},{16,18},{18,... | collective-permute-start | bytes 1769480 | tf_op jit(solution)/shard_map/ppermute | solution.py:155
  33.9 3.3 %collective-permute-start.4 = (bf16[256,1152]{1,0:T(8,128)(2,1)S(1)}, bf16[256,1152]{1,0:T(8,128)(2,1)}, u32[]{:S(2)}, u32[]{:S(2)}) collective-permute-start(bf16[256,1152]{1,0:T(8,128)(2,1)S(1)} %collective-permute-done.refs_2_), channel_id=1, source_target_pairs={{0,2},{6,4},{8,10},{14,12},{16,18},{22,20},{24,26},{30,28},{1,3},{... | collective-permute-start | bytes 1769480 | tf_op jit(solution)/shard_map/ppermute | solution.py:155
  37.2 0.0 collective-permute-done.2.refs_2_
  37.2 0.0 collective-permute-done.1.refs_2_
  37.2 1.3 %collective-permute-start.3 = (bf16[256,1152]{1,0:T(8,128)(2,1)}, bf16[256,1152]{1,0:T(8,128)(2,1)}, u32[]{:S(2)}, u32[]{:S(2)}) collective-permute-start(bf16[256,1152]{1,0:T(8,128)(2,1)} %collective-permute-done.1.refs_2_), channel_id=1, source_target_pairs={{2,0},{4,6},{10,8},{12,14},{18,16},{20,22},{26,24},{28,30},{3,1},{... | collective-permute-start | bytes 1769480 | tf_op jit(solution)/shard_map/ppermute | solution.py:155
  38.5 8.4 %collective-permute-start.9 = (bf16[256,1152]{1,0:T(8,128)(2,1)}, bf16[256,1152]{1,0:T(8,128)(2,1)S(1)}, u32[]{:S(2)}, u32[]{:S(2)}) collective-permute-start(bf16[256,1152]{1,0:T(8,128)(2,1)} %collective-permute-done.2.refs_2_), channel_id=1, source_target_pairs={{0,4},{6,2},{8,12},{14,10},{16,20},{22,18},{24,28},{30,26},{1,5},{... | collective-permute-start | bytes 1769480 | tf_op jit(solution)/shard_map/ppermute | solution.py:155
  46.9 0.0 collective-permute-done.7.refs_2_
  46.9 1.3 %collective-permute-start.8 = (bf16[256,1152]{1,0:T(8,128)(2,1)}, bf16[256,1152]{1,0:T(8,128)(2,1)S(1)}, u32[]{:S(2)}, u32[]{:S(2)}) collective-permute-start(bf16[256,1152]{1,0:T(8,128)(2,1)} %collective-permute-done.7.refs_2_), channel_id=1, source_target_pairs={{2,0},{4,6},{10,8},{12,14},{18,16},{20,22},{26,24},{28,30},{3,1},{... | collective-permute-start | bytes 1769480 | tf_op jit(solution)/shard_map/ppermute | solution.py:155
  49.6 0.1 pad_maximum_fusion.scalars.refs_0_
  49.6 0.0 copy-start
  49.6 1.1 %copy-done = bf16[256,1152]{1,0:T(8,128)(2,1)S(1)} copy-done((bf16[256,1152]{1,0:T(8,128)(2,1)S(1)}, bf16[256,1152]{1,0:T(8,128)(2,1)}, u32[]{:S(2)}) %copy-start) | copy-done | bytes 589848
  50.7 0.0 copy-start.2
  50.7 1.1 %copy-done.2 = bf16[256,1152]{1,0:T(8,128)(2,1)S(1)} copy-done((bf16[256,1152]{1,0:T(8,128)(2,1)S(1)}, bf16[256,1152]{1,0:T(8,128)(2,1)}, u32[]{:S(2)}) %copy-start.2) | copy-done | bytes 589848
  51.8 2.7 %shard_map.67 = (bf16[256,1152]{1,0:T(8,128)(2,1)S(1)}, bf16[256,1152]{1,0:T(8,128)(2,1)S(1)}, f32[256,128]{1,0:T(8,128)S(1)}, f32[256,128]{1,0:T(8,128)S(1)}, f...) custom-call(f32[3]{0:T(128)S(1)} %pad_maximum_fusion.scalars.refs_0_, ...), custom_call_target="tpu_custom_call" | custom-call | flops 603979776 | bytes 3538944 | tf_op jit(solution)/shard_map/pallas_call | solution.py:114
  54.5 0.0 copy-start.5
  54.5 1.8 %shard_map.68 = (f32[256,1152]{1,0:T(8,128)S(1)}, f32[24,128]{1,0:T(8,128)S(1)}) custom-call(f32[3]{0:T(128)S(1)} %pad_maximum_fusion.scalars.refs_0_, bf16[256,1152]{1,0:T(8,128)(2,1)S(1)} %get-tuple-element.20.refs_1_, bf16[256,1152]{1,0:T(8,128)(2,1)S(1)} %collective-permute-done.refs_2_, f32[256,1152]{1,0:T(8,128)S(1)} %get-tuple-element.22.refs_3_, ...), custom_call_target="tpu_custom_call" | custom-call | flops 301989888 | bytes 3538944 | tf_op jit(solution)/shard_map/pallas_call | solution.py:114
  56.3 0.0 copy-done.5
  56.3 0.0 collective-permute-done.5.refs_2_
  56.3 2.3 %shard_map.69 = (f32[256,1152]{1,0:T(8,128)S(1)}, f32[24,128]{1,0:T(8,128)S(1)}) custom-call(f32[3]{0:T(128)S(1)} %pad_maximum_fusion.scalars.refs_0_, bf16[256,1152]{1,0:T(8,128)(2,1)S(1)} %get-tuple-element.20.refs_1_, bf16[256,1152]{1,0:T(8,128)(2,1)} %collective-permute-done.5.refs_2_, f32[256,1152]{1,0:T(8,128)S(1)} %get-tuple-element.24.refs_3_, ...), custom_call_target="tpu_custom_call" | custom-call | flops 301989888 | bytes 3538944 | tf_op jit(solution)/shard_map/pallas_call | solution.py:114
  58.6 2.3 %shard_map.70 = (f32[256,1152]{1,0:T(8,128)S(1)}, f32[24,128]{1,0:T(8,128)S(1)}) custom-call(f32[3]{0:T(128)S(1)} %pad_maximum_fusion.scalars.refs_0_, bf16[256,1152]{1,0:T(8,128)(2,1)S(1)} %get-tuple-element.20.refs_1_, bf16[256,1152]{1,0:T(8,128)(2,1)} %collective-permute-done.1.refs_2_, f32[256,1152]{1,0:T(8,128)S(1)} %get-tuple-element.26.refs_3_, ...), custom_call_target="tpu_custom_call" | custom-call | flops 301989888 | bytes 3538944 | tf_op jit(solution)/shard_map/pallas_call | solution.py:114
  60.9 0.0 collective-permute-done.4.refs_3_
  60.9 0.8 collective-permute-done.3.refs_2_
  61.7 3.8 %shard_map.71 = (f32[256,1152]{1,0:T(8,128)}, f32[32,8,128]{2,1,0:T(8,128)S(1)}) custom-call(f32[3]{0:T(128)S(1)} %pad_maximum_fusion.scalars.refs_0_, bf16[256,1152]{1,0:T(8,128)(2,1)S(1)} %get-tuple-element.20.refs_1_, bf16[256,1152]{1,0:T(8,128)(2,1)} %collective-permute-done.3.refs_2_, bf16[256,1152]{1,0:T(8,128)(2,1)} %collective-permute-done.4.refs_3_, ...), custom_call_target="tpu_custom_call" | custom-call | flops 301989888 | bytes 3538944 | tf_op jit(solution)/shard_map/pallas_call | solution.py:114
  65.5 0.7 copy-done.7
  66.2 5.8 %all-to-all-start = ((f32[32,8,128]{2,1,0:T(8,128)}), f32[32,8,128]{2,1,0:T(8,128)}, u32[]{:S(2)}, u32[]{:S(2)}) async-start(f32[32,8,128]{2,1,0:T(8,128)} %copy-done.7), calls=%async_computation | async-start | bytes 262144 | tf_op jit(solution)/shard_map/all_to_all | solution.py:199
  72.0 0.0 copy-done.4
  72.0 1.6 %shard_map.72.refs_3_ = f32[256,1152]{1,0:T(8,128)S(1)} custom-call(f32[3]{0:T(128)S(1)} %pad_maximum_fusion.scalars.refs_0_, bf16[256,1152]{1,0:T(8,128)(2,1)S(1)} %get-tuple-element.32.refs_1_, bf16[256,1152]{1,0:T(8,128)(2,1)S(1)} %copy-done.4, f32[256,1152]{1,0:T(8,128)S(1)} %get-tuple-element.34.refs_3_), custom_call_target="tpu_custom_call" | custom-call | flops 301989888 | bytes 3538944 | tf_op jit(solution)/shard_map/pallas_call | solution.py:114
  73.6 2.2 %shard_map.73.refs_3_ = f32[256,1152]{1,0:T(8,128)S(1)} custom-call(f32[3]{0:T(128)S(1)} %pad_maximum_fusion.scalars.refs_0_, bf16[256,1152]{1,0:T(8,128)(2,1)S(1)} %get-tuple-element.32.refs_1_, bf16[256,1152]{1,0:T(8,128)(2,1)} %collective-permute-done.2.refs_2_, f32[256,1152]{1,0:T(8,128)S(1)} %shard_map.72.refs_3_), custom_call_target="tpu_custom_call" | custom-call | flops 301989888 | bytes 3538944 | tf_op jit(solution)/shard_map/pallas_call | solution.py:114
  75.8 0.0 copy-start.1
  75.8 0.0 copy-start.6
  75.8 2.2 %shard_map.74.refs_4_ = f32[256,1152]{1,0:T(8,128)S(1)} custom-call(f32[3]{0:T(128)S(1)} %pad_maximum_fusion.scalars.refs_0_, bf16[256,1152]{1,0:T(8,128)(2,1)S(1)} %get-tuple-element.32.refs_1_, bf16[256,1152]{1,0:T(8,128)(2,1)} %collective-permute-done.7.refs_2_, f32[256,1152]{1,0:T(8,128)S(1)} %shard_map.73.refs_3_), custom_call_target="tpu_custom_call" | custom-call | flops 301989888 | bytes 3538944 | tf_op jit(solution)/shard_map/pallas_call | solution.py:114
  78.1 0.0 collective-permute-done.9.refs_3_
  78.1 0.0 collective-permute-done.8.refs_2_
  78.1 0.0 copy-done.1
  78.1 0.0 copy-done.6
  78.1 2.9 %shard_map.75 = f32[256,1152]{1,0:T(8,128)} custom-call(f32[3]{0:T(128)S(1)} %pad_maximum_fusion.scalars.refs_0_, bf16[256,1152]{1,0:T(8,128)(2,1)S(1)} %get-tuple-element.32.refs_1_, bf16[256,1152]{1,0:T(8,128)(2,1)S(1)} %collective-permute-done.8.refs_2_, bf16[256,1152]{1,0:T(8,128)(2,1)S(1)} %collective-permute-done.9.refs_3_, ...), custom_call_target="tpu_custom_call" | custom-call | flops 301989888 | bytes 3538944 | tf_op jit(solution)/shard_map/pallas_call | solution.py:114
  81.1 0.0 all-to-all-done
  81.1 1.0 %slice_reduce_fusion = f32[3]{0:T(128)S(1)} fusion(f32[32,8,128]{2,1,0:T(8,128)} %all-to-all-done), kind=kLoop, calls=%fused_computation | loop fusion | flops 93 | bytes 396 | tf_op jit(solution)/shard_map/reduce_sum | solution.py:201
  82.0 0.5 broadcast_multiply_fusion
  (2 shorter events, 0.0 us)
Async XLA Ops:
  0.6 17.4 %collective-permute-start = (bf16[256,1152]{1,0:T(8,128)(2,1)}, bf16[256,1152]{1,0:T(8,128)(2,1)S(1)}, u32[]{:S(2)}, u32[]{:S(2)}) collective-permute-start(bf16[256,1152]{1,0:T(8,128)(2,1)} %refs_5_.1), channel_id=1, source_target_pairs={{0,4},{2,6},{4,0},{6,2},{8,12},{10,14},{12,8},{14,10},{16,20},{18,... | collective-permute-start | bytes 1769480 | tf_op jit(solution)/shard_map/ppermute | solution.py:155
  3.7 26.2 %collective-permute-start.6 = (bf16[256,1152]{1,0:T(8,128)(2,1)}, bf16[256,1152]{1,0:T(8,128)(2,1)S(1)}, u32[]{:S(2)}, u32[]{:S(2)}) collective-permute-start(bf16[256,1152]{1,0:T(8,128)(2,1)} %refs_6_.1), channel_id=1, source_target_pairs={{0,4},{2,6},{4,0},{6,2},{8,12},{10,14},{12,8},{14,10},{16,20},{18,... | collective-permute-start | bytes 1769480 | tf_op jit(solution)/shard_map/ppermute | solution.py:155
  3.7 33.5 %collective-permute-start.2 = (bf16[256,1152]{1,0:T(8,128)(2,1)}, bf16[256,1152]{1,0:T(8,128)(2,1)}, u32[]{:S(2)}, u32[]{:S(2)}) collective-permute-start(bf16[256,1152]{1,0:T(8,128)(2,1)} %refs_6_.1), channel_id=1, source_target_pairs={{0,2},{2,0},{4,6},{6,4},{8,10},{10,8},{12,14},{14,12},{16,18},{18,... | collective-permute-start | bytes 1769480 | tf_op jit(solution)/shard_map/ppermute | solution.py:155
  18.0 19.2 %collective-permute-start.1 = (bf16[256,1152]{1,0:T(8,128)(2,1)S(1)}, bf16[256,1152]{1,0:T(8,128)(2,1)}, u32[]{:S(2)}, u32[]{:S(2)}) collective-permute-start(bf16[256,1152]{1,0:T(8,128)(2,1)S(1)} %collective-permute-done.refs_2_), channel_id=1, source_target_pairs={{0,8},{2,10},{4,28},{6,30},{8,16},{10,18},{12,4},{14,6},{16,24},{1... | collective-permute-start | bytes 1769480 | tf_op jit(solution)/shard_map/ppermute | solution.py:155
  29.8 17.1 %collective-permute-start.7 = (bf16[256,1152]{1,0:T(8,128)(2,1)S(1)}, bf16[256,1152]{1,0:T(8,128)(2,1)}, u32[]{:S(2)}, u32[]{:S(2)}) collective-permute-start(bf16[256,1152]{1,0:T(8,128)(2,1)S(1)} %collective-permute-done.6.refs_2_), channel_id=1, source_target_pairs={{0,8},{2,10},{4,28},{6,30},{8,16},{10,18},{12,4},{14,6},{16,24},{1... | collective-permute-start | bytes 1769480 | tf_op jit(solution)/shard_map/ppermute | solution.py:155
  31.6 0.8 copy-start.3
  32.5 23.9 %collective-permute-start.5 = (bf16[256,1152]{1,0:T(8,128)(2,1)}, bf16[256,1152]{1,0:T(8,128)(2,1)}, u32[]{:S(2)}, u32[]{:S(2)}) collective-permute-start(bf16[256,1152]{1,0:T(8,128)(2,1)} %refs_5_.1), channel_id=1, source_target_pairs={{0,2},{2,0},{4,6},{6,4},{8,10},{10,8},{12,14},{14,12},{16,18},{18,... | collective-permute-start | bytes 1769480 | tf_op jit(solution)/shard_map/ppermute | solution.py:155
  33.9 27.0 %collective-permute-start.4 = (bf16[256,1152]{1,0:T(8,128)(2,1)S(1)}, bf16[256,1152]{1,0:T(8,128)(2,1)}, u32[]{:S(2)}, u32[]{:S(2)}) collective-permute-start(bf16[256,1152]{1,0:T(8,128)(2,1)S(1)} %collective-permute-done.refs_2_), channel_id=1, source_target_pairs={{0,2},{6,4},{8,10},{14,12},{16,18},{22,20},{24,26},{30,28},{1,3},{... | collective-permute-start | bytes 1769480 | tf_op jit(solution)/shard_map/ppermute | solution.py:155
  37.2 24.5 %collective-permute-start.3 = (bf16[256,1152]{1,0:T(8,128)(2,1)}, bf16[256,1152]{1,0:T(8,128)(2,1)}, u32[]{:S(2)}, u32[]{:S(2)}) collective-permute-start(bf16[256,1152]{1,0:T(8,128)(2,1)} %collective-permute-done.1.refs_2_), channel_id=1, source_target_pairs={{2,0},{4,6},{10,8},{12,14},{18,16},{20,22},{26,24},{28,30},{3,1},{... | collective-permute-start | bytes 1769480 | tf_op jit(solution)/shard_map/ppermute | solution.py:155
  38.5 39.6 %collective-permute-start.9 = (bf16[256,1152]{1,0:T(8,128)(2,1)}, bf16[256,1152]{1,0:T(8,128)(2,1)S(1)}, u32[]{:S(2)}, u32[]{:S(2)}) collective-permute-start(bf16[256,1152]{1,0:T(8,128)(2,1)} %collective-permute-done.2.refs_2_), channel_id=1, source_target_pairs={{0,4},{6,2},{8,12},{14,10},{16,20},{22,18},{24,28},{30,26},{1,5},{... | collective-permute-start | bytes 1769480 | tf_op jit(solution)/shard_map/ppermute | solution.py:155
  46.9 31.2 %collective-permute-start.8 = (bf16[256,1152]{1,0:T(8,128)(2,1)}, bf16[256,1152]{1,0:T(8,128)(2,1)S(1)}, u32[]{:S(2)}, u32[]{:S(2)}) collective-permute-start(bf16[256,1152]{1,0:T(8,128)(2,1)} %collective-permute-done.7.refs_2_), channel_id=1, source_target_pairs={{2,0},{4,6},{10,8},{12,14},{18,16},{20,22},{26,24},{28,30},{3,1},{... | collective-permute-start | bytes 1769480 | tf_op jit(solution)/shard_map/ppermute | solution.py:155
  49.6 1.1 %copy-start = (bf16[256,1152]{1,0:T(8,128)(2,1)S(1)}, bf16[256,1152]{1,0:T(8,128)(2,1)}, u32[]{:S(2)}) copy-start(bf16[256,1152]{1,0:T(8,128)(2,1)} %refs_5_.1) | copy-start | bytes 1769476
  50.7 1.1 %copy-start.2 = (bf16[256,1152]{1,0:T(8,128)(2,1)S(1)}, bf16[256,1152]{1,0:T(8,128)(2,1)}, u32[]{:S(2)}) copy-start(bf16[256,1152]{1,0:T(8,128)(2,1)} %refs_6_.1) | copy-start | bytes 1769476
  54.5 1.8 %copy-start.5 = (f32[256,128]{1,0:T(8,128)}, f32[256,128]{1,0:T(8,128)S(1)}, u32[]{:S(2)}) copy-start(f32[256,128]{1,0:T(8,128)S(1)} %get-tuple-element.35.refs_6_) | copy-start | bytes 393220
  61.7 10.3 %copy-start.4 = (bf16[256,1152]{1,0:T(8,128)(2,1)S(1)}, bf16[256,1152]{1,0:T(8,128)(2,1)}, u32[]{:S(2)}) copy-start(bf16[256,1152]{1,0:T(8,128)(2,1)} %copy-done.3) | copy-start | bytes 1769476
  65.5 0.7 copy-start.7
  66.2 14.9 %all-to-all-start = ((f32[32,8,128]{2,1,0:T(8,128)}), f32[32,8,128]{2,1,0:T(8,128)}, u32[]{:S(2)}, u32[]{:S(2)}) async-start(f32[32,8,128]{2,1,0:T(8,128)} %copy-done.7), calls=%async_computation | async-start | bytes 262144 | tf_op jit(solution)/shard_map/all_to_all | solution.py:199
  75.8 2.3 %copy-start.1 = (bf16[256,1152]{1,0:T(8,128)(2,1)S(1)}, bf16[256,1152]{1,0:T(8,128)(2,1)}, u32[]{:S(2)}) copy-start(bf16[256,1152]{1,0:T(8,128)(2,1)} %refs_5_.1) | copy-start | bytes 1769476
  75.8 2.3 %copy-start.6 = (f32[256,128]{1,0:T(8,128)S(1)}, f32[256,128]{1,0:T(8,128)}, u32[]{:S(2)}) copy-start(f32[256,128]{1,0:T(8,128)} %copy-done.5) | copy-start | bytes 393220

commit v2 on v1

--- a/solution.py
+++ b/solution.py
@@ -140,6 +140,10 @@
     return call(functools.partial(visit_kernel, counted, last), operands, tuple(shapes), rows, width, 1)
 
 
+def tied(*values):
+    return lax.optimization_barrier(values)
+
+
 def on_device(image, text, log_temp, bias):
     rows, width = image.shape
     blocks = lax.axis_size("blk")
@@ -178,27 +182,30 @@
         2,
     )
 
+    txt_y, txt_x, gx, gy = tied(txt_y, txt_x, gx, gy)
     txt_z = send(txt_y, beyond)
-    img_z = send(img_y, beyond)
-    txt_z, img_x = lax.optimization_barrier((txt_z, img_x))
-    txt_c = send(txt_z, corner)
     txt_m = send(txt_y, middle_x)
-    img_m = send(img_x, middle_y)
-    img_c = send(img_z, corner)
-
     gx, stats = visit(scalars, img_unit, txt_y, gx, stats)
     gx, stats = visit(scalars, img_unit, txt_x, gx, stats)
+    img_y, img_x, gx = tied(img_y, img_x, gx)
+    img_z = send(img_y, beyond)
+    img_m = send(img_x, middle_y)
     (gy,) = visit(scalars, txt_unit, img_y, gy)
+    txt_z, gy = tied(txt_z, gy)
+    txt_c = send(txt_z, corner)
     (gy,) = visit(scalars, txt_unit, img_x, gy)
     gx, stats = visit(scalars, img_unit, txt_z, gx, stats)
+    img_z, gx, gy = tied(img_z, gx, gy)
+    img_c = send(img_z, corner)
     (gy,) = visit(scalars, txt_unit, img_z, gy)
+    img_m, gx = tied(img_m, gx)
     grad_image, sums = visit(
         scalars, img_unit, txt_c, gx, stats, txt_m, (image, img_inv), devices
     )
-    (grad_text,) = visit(scalars, txt_unit, img_c, gy, None, img_m, (text, txt_inv))
     seen = lax.all_to_all(sums, ("blk", "grp"), 0, 0)
     pairs = jnp.float32(rows * rows * (2 * REACH + 1) * devices)
     statistics = jnp.sum(seen[:, 0, :3], axis=0) / pairs
+    (grad_text,) = visit(scalars, txt_unit, img_c, gy, None, img_m, (text, txt_inv))
     return grad_image, grad_text, statistics
 
 

time: 83.1 us -> 73.7 us (0.89)
  starting transfers between devices: 30.5 us -> 19.4 us
  waiting for transfers between devices: 22.8 us -> 28.1 us
  Pallas kernels: 21.9 us -> 20.2 us
  other arithmetic: 1.55 us -> 0.64 us
    ppermute x10, starting transfers between devices: 24.7 us -> 16.6 us  [send(): return lax.ppermute(block, 'blk', route)]
    ppermute x10, waiting for transfers between devices: 22.8 us -> 27.1 us  [send(): return lax.ppermute(block, 'blk', route)]
    all_to_all x1, starting transfers between devices: 5.8 us -> 2.81 us  [on_device(): seen = lax.all_to_all(sums, ('blk', 'grp'), 0, 0)]
    pallas_call x9, Pallas kernels: 21.9 us -> 20.2 us  [call(): pl.pallas_call(kernel, out_shape=shapes, in_specs=[IN_SMEM] + [IN_VMEM] *...]
    all_to_all x1, waiting for transfers between devices: 0.01 us -> 0.99 us  [on_device(): seen = lax.all_to_all(sums, ('blk', 'grp'), 0, 0)]
    reduce_sum x1, other arithmetic: 0.95 us -> 0.05 us  [on_device(): statistics = jnp.sum(seen[:, 0, :3], axis=0) / pairs]
    unnamed x16 -> x10, local copies, waits for them, and re-layouts: 3.62 us -> 2.79 us
  transfers between devices with their start and end apart: 11 -> 11, of which waited for: 3 -> 9; matrix products, arithmetic and copies ran while one was open for 0% -> 0% of each run, Pallas kernels for 27% -> 28%
where the time goes in v2:
time: 73.7 us; the launch traced here: 73.3 us
  waiting for transfers between devices  28.1 us (38%)
  Pallas kernels  20.2 us (27%)
  starting transfers between devices  19.4 us (26%)
  local copies, waits for them, and re-layouts  2.79 us (4%)
  between operations  2.09 us (3%)
    ppermute x10, waiting for transfers between devices, send(): return lax.ppermute(block, 'blk', route)  27.1 us
    pallas_call x9, Pallas kernels, call(): pl.pallas_call(kernel, out_shape=shapes, in_specs=[IN_SMEM] + [IN_VMEM] *...  20.2 us
    ppermute x10, starting transfers between devices, send(): return lax.ppermute(block, 'blk', route)  16.6 us
    all_to_all x1, starting transfers between devices, on_device(): seen = lax.all_to_all(sums, ('blk', 'grp'), 0, 0)  2.81 us
    unnamed x10, local copies, waits for them, and re-layouts  2.79 us
  transfers between devices with their start and end apart: 11, of which 9 were waited for; matrix products, arithmetic and copies ran while one was open for 0% of the time, Pallas kernels for 28%

profile of v2, /device:TPU:0, one launch (start us, length us, event | category | flops | bytes accessed | tf_op | source)
XLA Modules:
  0.0 73.3 jit_solution(4034114112267221106)
XLA Ops:
  0.6 3.0 %collective-permute-start = (bf16[256,1152]{1,0:T(8,128)(2,1)}, bf16[256,1152]{1,0:T(8,128)(2,1)S(1)}, u32[]{:S(2)}, u32[]{:S(2)}) collective-permute-start(bf16[256,1152]{1,0:T(8,128)(2,1)} %refs_5_.1), channel_id=1, source_target_pairs={{0,4},{2,6},{4,0},{6,2},{8,12},{10,14},{12,8},{14,10},{16,20},{18,... | collective-permute-start | bytes 1769480 | tf_op jit(solution)/shard_map/ppermute | solution.py:159
  3.7 1.5 %collective-permute-start.1 = (bf16[256,1152]{1,0:T(8,128)(2,1)}, bf16[256,1152]{1,0:T(8,128)(2,1)S(1)}, u32[]{:S(2)}, u32[]{:S(2)}) collective-permute-start(bf16[256,1152]{1,0:T(8,128)(2,1)} %refs_5_.1), channel_id=1, source_target_pairs={{0,2},{2,0},{4,6},{6,4},{8,10},{10,8},{12,14},{14,12},{16,18},{18,... | collective-permute-start | bytes 1769480 | tf_op jit(solution)/shard_map/ppermute | solution.py:159
  5.2 0.5 collective-permute-start.3
  5.7 0.1 collective-permute-start.4
  7.1 0.1 pad_maximum_fusion.scalars.refs_0_
  7.2 0.0 copy-start
  7.2 1.1 %copy-done = bf16[256,1152]{1,0:T(8,128)(2,1)S(1)} copy-done((bf16[256,1152]{1,0:T(8,128)(2,1)S(1)}, bf16[256,1152]{1,0:T(8,128)(2,1)}, u32[]{:S(2)}) %copy-start) | copy-done | bytes 589848
  8.3 0.0 copy-start.2
  8.3 1.1 %copy-done.2 = bf16[256,1152]{1,0:T(8,128)(2,1)S(1)} copy-done((bf16[256,1152]{1,0:T(8,128)(2,1)S(1)}, bf16[256,1152]{1,0:T(8,128)(2,1)}, u32[]{:S(2)}) %copy-start.2) | copy-done | bytes 589848
  9.3 2.8 %shard_map.67 = (bf16[256,1152]{1,0:T(8,128)(2,1)S(1)}, bf16[256,1152]{1,0:T(8,128)(2,1)S(1)}, f32[256,128]{1,0:T(8,128)S(1)}, f32[256,128]{1,0:T(8,128)S(1)}, f...) custom-call(f32[3]{0:T(128)S(1)} %pad_maximum_fusion.scalars.refs_0_, ...), custom_call_target="tpu_custom_call" | custom-call | flops 603979776 | bytes 3538944 | tf_op jit(solution)/shard_map/pallas_call | solution.py:114
  12.1 0.0 copy-start.3
  12.1 0.6 copy-done.3
  12.7 5.3 %collective-permute-done.refs_2_ = bf16[256,1152]{1,0:T(8,128)(2,1)S(1)} collective-permute-done((bf16[256,1152]{1,0:T(8,128)(2,1)}, bf16[256,1152]{1,0:T(8,128)(2,1)S(1)}, u32[]{:S(2)}, u32[]{:S(2)}) %collective-permute-start) | collective-permute-done | bytes 589856 | tf_op jit(solution)/shard_map/ppermute | solution.py:159
  18.0 2.1 %collective-permute-done.1.refs_2_ = bf16[256,1152]{1,0:T(8,128)(2,1)S(1)} collective-permute-done((bf16[256,1152]{1,0:T(8,128)(2,1)}, bf16[256,1152]{1,0:T(8,128)(2,1)S(1)}, u32[]{:S(2)}, u32[]{:S(2)}) %collective-permute-start.1) | collective-permute-done | bytes 589856 | tf_op jit(solution)/shard_map/ppermute | solution.py:159
  20.1 1.6 %collective-permute-start.2 = (bf16[256,1152]{1,0:T(8,128)(2,1)S(1)}, bf16[256,1152]{1,0:T(8,128)(2,1)S(1)}, u32[]{:S(2)}, u32[]{:S(2)}) collective-permute-start(bf16[256,1152]{1,0:T(8,128)(2,1)S(1)} %collective-permute-done.refs_2_), channel_id=1, source_target_pairs={{0,8},{2,10},{4,28},{6,30},{8,16},{10,18},{12,4},{14,6},{16,24},{1... | collective-permute-start | bytes 1769480 | tf_op jit(solution)/shard_map/ppermute | solution.py:159
  21.7 1.8 %shard_map.68 = (f32[256,1152]{1,0:T(8,128)S(1)}, f32[24,128]{1,0:T(8,128)S(1)}) custom-call(f32[3]{0:T(128)S(1)} %pad_maximum_fusion.scalars.refs_0_, bf16[256,1152]{1,0:T(8,128)(2,1)S(1)} %get-tuple-element.32.refs_1_, bf16[256,1152]{1,0:T(8,128)(2,1)S(1)} %collective-permute-done.refs_2_, f32[256,1152]{1,0:T(8,128)S(1)} %get-tuple-element.38.refs_3_, ...), custom_call_target="tpu_custom_call" | custom-call | flops 301989888 | bytes 3538944 | tf_op jit(solution)/shard_map/pallas_call | solution.py:114
  23.5 1.8 %shard_map.69 = (f32[256,1152]{1,0:T(8,128)S(1)}, f32[24,128]{1,0:T(8,128)S(1)}) custom-call(f32[3]{0:T(128)S(1)} %pad_maximum_fusion.scalars.refs_0_, bf16[256,1152]{1,0:T(8,128)(2,1)S(1)} %get-tuple-element.32.refs_1_, bf16[256,1152]{1,0:T(8,128)(2,1)S(1)} %collective-permute-done.1.refs_2_, f32[256,1152]{1,0:T(8,128)S(1)} %get-tuple-element.40.refs_3_, ...), custom_call_target="tpu_custom_call" | custom-call | flops 301989888 | bytes 3538944 | tf_op jit(solution)/shard_map/pallas_call | solution.py:114
  25.2 4.6 %collective-permute-done.3.refs_2_ = bf16[256,1152]{1,0:T(8,128)(2,1)S(1)} collective-permute-done((bf16[256,1152]{1,0:T(8,128)(2,1)}, bf16[256,1152]{1,0:T(8,128)(2,1)S(1)}, u32[]{:S(2)}, u32[]{:S(2)}) %collective-permute-start.3) | collective-permute-done | bytes 589856 | tf_op jit(solution)/shard_map/ppermute | solution.py:159
  29.8 1.6 %collective-permute-done.4.refs_2_ = bf16[256,1152]{1,0:T(8,128)(2,1)} collective-permute-done((bf16[256,1152]{1,0:T(8,128)(2,1)}, bf16[256,1152]{1,0:T(8,128)(2,1)}, u32[]{:S(2)}, u32[]{:S(2)}) %collective-permute-start.4) | collective-permute-done | bytes 589856 | tf_op jit(solution)/shard_map/ppermute | solution.py:159
  31.4 1.6 %collective-permute-start.8 = (bf16[256,1152]{1,0:T(8,128)(2,1)S(1)}, bf16[256,1152]{1,0:T(8,128)(2,1)}, u32[]{:S(2)}, u32[]{:S(2)}) collective-permute-start(bf16[256,1152]{1,0:T(8,128)(2,1)S(1)} %collective-permute-done.3.refs_2_), channel_id=1, source_target_pairs={{0,8},{2,10},{4,28},{6,30},{8,16},{10,18},{12,4},{14,6},{16,24},{1... | collective-permute-start | bytes 1769480 | tf_op jit(solution)/shard_map/ppermute | solution.py:159
  33.0 3.4 %collective-permute-start.6 = (bf16[256,1152]{1,0:T(8,128)(2,1)S(1)}, bf16[256,1152]{1,0:T(8,128)(2,1)S(1)}, u32[]{:S(2)}, u32[]{:S(2)}) collective-permute-start(bf16[256,1152]{1,0:T(8,128)(2,1)S(1)} %collective-permute-done.refs_2_), channel_id=1, source_target_pairs={{0,2},{6,4},{8,10},{14,12},{16,18},{22,20},{24,26},{30,28},{1,3},{... | collective-permute-start | bytes 1769480 | tf_op jit(solution)/shard_map/ppermute | solution.py:159
  36.4 2.3 %collective-permute-start.7 = (bf16[256,1152]{1,0:T(8,128)(2,1)}, bf16[256,1152]{1,0:T(8,128)(2,1)S(1)}, u32[]{:S(2)}, u32[]{:S(2)}) collective-permute-start(bf16[256,1152]{1,0:T(8,128)(2,1)} %collective-permute-done.4.refs_2_), channel_id=1, source_target_pairs={{0,4},{6,2},{8,12},{14,10},{16,20},{22,18},{24,28},{30,26},{1,5},{... | collective-permute-start | bytes 1769480 | tf_op jit(solution)/shard_map/ppermute | solution.py:159
  38.8 1.6 %shard_map.70.refs_3_ = f32[256,1152]{1,0:T(8,128)S(1)} custom-call(f32[3]{0:T(128)S(1)} %pad_maximum_fusion.scalars.refs_0_, bf16[256,1152]{1,0:T(8,128)(2,1)S(1)} %get-tuple-element.36.refs_1_, bf16[256,1152]{1,0:T(8,128)(2,1)S(1)} %collective-permute-done.3.refs_2_, f32[256,1152]{1,0:T(8,128)S(1)} %get-tuple-element.44.refs_3_), custom_call_target="tpu_custom_call" | custom-call | flops 301989888 | bytes 3538944 | tf_op jit(solution)/shard_map/pallas_call | solution.py:114
  40.4 0.0 collective-permute-done.2.refs_2_
  40.4 1.3 %collective-permute-start.5 = (bf16[256,1152]{1,0:T(8,128)(2,1)S(1)}, bf16[256,1152]{1,0:T(8,128)(2,1)S(1)}, u32[]{:S(2)}, u32[]{:S(2)}) collective-permute-start(bf16[256,1152]{1,0:T(8,128)(2,1)S(1)} %collective-permute-done.2.refs_2_), channel_id=1, source_target_pairs={{2,0},{4,6},{10,8},{12,14},{18,16},{20,22},{26,24},{28,30},{3,1},{... | collective-permute-start | bytes 1769480 | tf_op jit(solution)/shard_map/ppermute | solution.py:159
  41.7 2.2 %shard_map.72.refs_3_ = f32[256,1152]{1,0:T(8,128)S(1)} custom-call(f32[3]{0:T(128)S(1)} %pad_maximum_fusion.scalars.refs_0_, bf16[256,1152]{1,0:T(8,128)(2,1)S(1)} %get-tuple-element.36.refs_1_, bf16[256,1152]{1,0:T(8,128)(2,1)} %collective-permute-done.4.refs_2_, f32[256,1152]{1,0:T(8,128)S(1)} %shard_map.70.refs_3_), custom_call_target="tpu_custom_call" | custom-call | flops 301989888 | bytes 3538944 | tf_op jit(solution)/shard_map/pallas_call | solution.py:114
  43.9 1.8 %shard_map.71 = (f32[256,1152]{1,0:T(8,128)S(1)}, f32[24,128]{1,0:T(8,128)S(1)}) custom-call(f32[3]{0:T(128)S(1)} %pad_maximum_fusion.scalars.refs_0_, bf16[256,1152]{1,0:T(8,128)(2,1)S(1)} %get-tuple-element.32.refs_1_, bf16[256,1152]{1,0:T(8,128)(2,1)S(1)} %collective-permute-done.2.refs_2_, f32[256,1152]{1,0:T(8,128)S(1)} %get-tuple-element.47.refs_3_, ...), custom_call_target="tpu_custom_call" | custom-call | flops 301989888 | bytes 3538944 | tf_op jit(solution)/shard_map/pallas_call | solution.py:114
  45.7 1.6 %collective-permute-done.8.refs_2_ = bf16[256,1152]{1,0:T(8,128)(2,1)} collective-permute-done((bf16[256,1152]{1,0:T(8,128)(2,1)S(1)}, bf16[256,1152]{1,0:T(8,128)(2,1)}, u32[]{:S(2)}, u32[]{:S(2)}) %collective-permute-start.8) | collective-permute-done | bytes 589856 | tf_op jit(solution)/shard_map/ppermute | solution.py:159
  47.2 1.3 %collective-permute-start.9 = (bf16[256,1152]{1,0:T(8,128)(2,1)}, bf16[256,1152]{1,0:T(8,128)(2,1)S(1)}, u32[]{:S(2)}, u32[]{:S(2)}) collective-permute-start(bf16[256,1152]{1,0:T(8,128)(2,1)} %collective-permute-done.8.refs_2_), channel_id=1, source_target_pairs={{2,0},{4,6},{10,8},{12,14},{18,16},{20,22},{26,24},{28,30},{3,1},{... | collective-permute-start | bytes 1769480 | tf_op jit(solution)/shard_map/ppermute | solution.py:159
  48.5 1.7 %collective-permute-done.7.refs_3_ = bf16[256,1152]{1,0:T(8,128)(2,1)S(1)} collective-permute-done((bf16[256,1152]{1,0:T(8,128)(2,1)}, bf16[256,1152]{1,0:T(8,128)(2,1)S(1)}, u32[]{:S(2)}, u32[]{:S(2)}) %collective-permute-start.7) | collective-permute-done | bytes 589856 | tf_op jit(solution)/shard_map/ppermute | solution.py:159
  50.2 0.0 collective-permute-done.6.refs_3_
  50.2 8.3 %collective-permute-done.5.refs_2_ = bf16[256,1152]{1,0:T(8,128)(2,1)S(1)} collective-permute-done((bf16[256,1152]{1,0:T(8,128)(2,1)S(1)}, bf16[256,1152]{1,0:T(8,128)(2,1)S(1)}, u32[]{:S(2)}, u32[]{:S(2)}) %collective-permute-start.5) | collective-permute-done | bytes 589856 | tf_op jit(solution)/shard_map/ppermute | solution.py:159
  58.6 3.1 %shard_map.73 = (f32[256,1152]{1,0:T(8,128)}, f32[32,8,128]{2,1,0:T(8,128)}) custom-call(f32[3]{0:T(128)S(1)} %pad_maximum_fusion.scalars.refs_0_, bf16[256,1152]{1,0:T(8,128)(2,1)S(1)} %get-tuple-element.32.refs_1_, bf16[256,1152]{1,0:T(8,128)(2,1)S(1)} %collective-permute-done.5.refs_2_, bf16[256,1152]{1,0:T(8,128)(2,1)S(1)} %collective-permute-done.6.refs_3_, ...), custom_call_target="tpu_custom_call" | custom-call | flops 301989888 | bytes 3538944 | tf_op jit(solution)/shard_map/pallas_call | solution.py:114
  61.6 2.8 %all-to-all-start = ((f32[32,8,128]{2,1,0:T(8,128)}), f32[32,8,128]{2,1,0:T(8,128)S(1)}, u32[]{:S(2)}, u32[]{:S(2)}) async-start(f32[32,8,128]{2,1,0:T(8,128)} %get-tuple-element.60), calls=%async_computation | async-start | bytes 262144 | tf_op jit(solution)/shard_map/all_to_all | solution.py:205
  64.5 0.0 copy-start.1
  64.5 0.0 copy-start.4
  64.5 2.2 %shard_map.74.refs_4_ = f32[256,1152]{1,0:T(8,128)S(1)} custom-call(f32[3]{0:T(128)S(1)} %pad_maximum_fusion.scalars.refs_0_, bf16[256,1152]{1,0:T(8,128)(2,1)S(1)} %get-tuple-element.36.refs_1_, bf16[256,1152]{1,0:T(8,128)(2,1)} %collective-permute-done.8.refs_2_, f32[256,1152]{1,0:T(8,128)S(1)} %shard_map.72.refs_3_), custom_call_target="tpu_custom_call" | custom-call | flops 301989888 | bytes 3538944 | tf_op jit(solution)/shard_map/pallas_call | solution.py:114
  66.7 2.0 %collective-permute-done.9.refs_2_ = bf16[256,1152]{1,0:T(8,128)(2,1)S(1)} collective-permute-done((bf16[256,1152]{1,0:T(8,128)(2,1)}, bf16[256,1152]{1,0:T(8,128)(2,1)S(1)}, u32[]{:S(2)}, u32[]{:S(2)}) %collective-permute-start.9) | collective-permute-done | bytes 589856 | tf_op jit(solution)/shard_map/ppermute | solution.py:159
  68.7 0.0 copy-done.1
  68.7 0.0 copy-done.4
  68.7 3.0 %shard_map.75 = f32[256,1152]{1,0:T(8,128)} custom-call(f32[3]{0:T(128)S(1)} %pad_maximum_fusion.scalars.refs_0_, bf16[256,1152]{1,0:T(8,128)(2,1)S(1)} %get-tuple-element.36.refs_1_, bf16[256,1152]{1,0:T(8,128)(2,1)S(1)} %collective-permute-done.9.refs_2_, bf16[256,1152]{1,0:T(8,128)(2,1)S(1)} %collective-permute-done.7.refs_3_, ...), custom_call_target="tpu_custom_call" | custom-call | flops 301989888 | bytes 3538944 | tf_op jit(solution)/shard_map/pallas_call | solution.py:114
  71.7 1.0 %all-to-all-done = f32[32,8,128]{2,1,0:T(8,128)S(1)} async-done(((f32[32,8,128]{2,1,0:T(8,128)}), f32[32,8,128]{2,1,0:T(8,128)S(1)}, u32[]{:S(2)}, u32[]{:S(2)}) %all-to-all-start) | async-done | bytes 131104 | tf_op jit(solution)/shard_map/all_to_all | solution.py:205
  72.7 0.1 slice_reduce_fusion
  72.7 0.5 broadcast_multiply_fusion
Async XLA Ops:
  0.6 17.4 %collective-permute-start = (bf16[256,1152]{1,0:T(8,128)(2,1)}, bf16[256,1152]{1,0:T(8,128)(2,1)S(1)}, u32[]{:S(2)}, u32[]{:S(2)}) collective-permute-start(bf16[256,1152]{1,0:T(8,128)(2,1)} %refs_5_.1), channel_id=1, source_target_pairs={{0,4},{2,6},{4,0},{6,2},{8,12},{10,14},{12,8},{14,10},{16,20},{18,... | collective-permute-start | bytes 1769480 | tf_op jit(solution)/shard_map/ppermute | solution.py:159
  3.7 16.5 %collective-permute-start.1 = (bf16[256,1152]{1,0:T(8,128)(2,1)}, bf16[256,1152]{1,0:T(8,128)(2,1)S(1)}, u32[]{:S(2)}, u32[]{:S(2)}) collective-permute-start(bf16[256,1152]{1,0:T(8,128)(2,1)} %refs_5_.1), channel_id=1, source_target_pairs={{0,2},{2,0},{4,6},{6,4},{8,10},{10,8},{12,14},{14,12},{16,18},{18,... | collective-permute-start | bytes 1769480 | tf_op jit(solution)/shard_map/ppermute | solution.py:159
  5.2 24.7 %collective-permute-start.3 = (bf16[256,1152]{1,0:T(8,128)(2,1)}, bf16[256,1152]{1,0:T(8,128)(2,1)S(1)}, u32[]{:S(2)}, u32[]{:S(2)}) collective-permute-start(bf16[256,1152]{1,0:T(8,128)(2,1)} %refs_6_.1), channel_id=1, source_target_pairs={{0,4},{2,6},{4,0},{6,2},{8,12},{10,14},{12,8},{14,10},{16,20},{18,... | collective-permute-start | bytes 1769480 | tf_op jit(solution)/shard_map/ppermute | solution.py:159
  5.7 25.7 %collective-permute-start.4 = (bf16[256,1152]{1,0:T(8,128)(2,1)}, bf16[256,1152]{1,0:T(8,128)(2,1)}, u32[]{:S(2)}, u32[]{:S(2)}) collective-permute-start(bf16[256,1152]{1,0:T(8,128)(2,1)} %refs_6_.1), channel_id=1, source_target_pairs={{0,2},{2,0},{4,6},{6,4},{8,10},{10,8},{12,14},{14,12},{16,18},{18,... | collective-permute-start | bytes 1769480 | tf_op jit(solution)/shard_map/ppermute | solution.py:159
  7.2 1.1 %copy-start = (bf16[256,1152]{1,0:T(8,128)(2,1)S(1)}, bf16[256,1152]{1,0:T(8,128)(2,1)}, u32[]{:S(2)}) copy-start(bf16[256,1152]{1,0:T(8,128)(2,1)} %refs_5_.1) | copy-start | bytes 1769476
  8.3 1.1 %copy-start.2 = (bf16[256,1152]{1,0:T(8,128)(2,1)S(1)}, bf16[256,1152]{1,0:T(8,128)(2,1)}, u32[]{:S(2)}) copy-start(bf16[256,1152]{1,0:T(8,128)(2,1)} %refs_6_.1) | copy-start | bytes 1769476
  12.1 0.7 copy-start.3
  20.1 20.3 %collective-permute-start.2 = (bf16[256,1152]{1,0:T(8,128)(2,1)S(1)}, bf16[256,1152]{1,0:T(8,128)(2,1)S(1)}, u32[]{:S(2)}, u32[]{:S(2)}) collective-permute-start(bf16[256,1152]{1,0:T(8,128)(2,1)S(1)} %collective-permute-done.refs_2_), channel_id=1, source_target_pairs={{0,8},{2,10},{4,28},{6,30},{8,16},{10,18},{12,4},{14,6},{16,24},{1... | collective-permute-start | bytes 1769480 | tf_op jit(solution)/shard_map/ppermute | solution.py:159
  31.4 15.8 %collective-permute-start.8 = (bf16[256,1152]{1,0:T(8,128)(2,1)S(1)}, bf16[256,1152]{1,0:T(8,128)(2,1)}, u32[]{:S(2)}, u32[]{:S(2)}) collective-permute-start(bf16[256,1152]{1,0:T(8,128)(2,1)S(1)} %collective-permute-done.3.refs_2_), channel_id=1, source_target_pairs={{0,8},{2,10},{4,28},{6,30},{8,16},{10,18},{12,4},{14,6},{16,24},{1... | collective-permute-start | bytes 1769480 | tf_op jit(solution)/shard_map/ppermute | solution.py:159
  33.0 17.2 %collective-permute-start.6 = (bf16[256,1152]{1,0:T(8,128)(2,1)S(1)}, bf16[256,1152]{1,0:T(8,128)(2,1)S(1)}, u32[]{:S(2)}, u32[]{:S(2)}) collective-permute-start(bf16[256,1152]{1,0:T(8,128)(2,1)S(1)} %collective-permute-done.refs_2_), channel_id=1, source_target_pairs={{0,2},{6,4},{8,10},{14,12},{16,18},{22,20},{24,26},{30,28},{1,3},{... | collective-permute-start | bytes 1769480 | tf_op jit(solution)/shard_map/ppermute | solution.py:159
  36.4 13.8 %collective-permute-start.7 = (bf16[256,1152]{1,0:T(8,128)(2,1)}, bf16[256,1152]{1,0:T(8,128)(2,1)S(1)}, u32[]{:S(2)}, u32[]{:S(2)}) collective-permute-start(bf16[256,1152]{1,0:T(8,128)(2,1)} %collective-permute-done.4.refs_2_), channel_id=1, source_target_pairs={{0,4},{6,2},{8,12},{14,10},{16,20},{22,18},{24,28},{30,26},{1,5},{... | collective-permute-start | bytes 1769480 | tf_op jit(solution)/shard_map/ppermute | solution.py:159
  40.4 18.2 %collective-permute-start.5 = (bf16[256,1152]{1,0:T(8,128)(2,1)S(1)}, bf16[256,1152]{1,0:T(8,128)(2,1)S(1)}, u32[]{:S(2)}, u32[]{:S(2)}) collective-permute-start(bf16[256,1152]{1,0:T(8,128)(2,1)S(1)} %collective-permute-done.2.refs_2_), channel_id=1, source_target_pairs={{2,0},{4,6},{10,8},{12,14},{18,16},{20,22},{26,24},{28,30},{3,1},{... | collective-permute-start | bytes 1769480 | tf_op jit(solution)/shard_map/ppermute | solution.py:159
  47.2 21.5 %collective-permute-start.9 = (bf16[256,1152]{1,0:T(8,128)(2,1)}, bf16[256,1152]{1,0:T(8,128)(2,1)S(1)}, u32[]{:S(2)}, u32[]{:S(2)}) collective-permute-start(bf16[256,1152]{1,0:T(8,128)(2,1)} %collective-permute-done.8.refs_2_), channel_id=1, source_target_pairs={{2,0},{4,6},{10,8},{12,14},{18,16},{20,22},{26,24},{28,30},{3,1},{... | collective-permute-start | bytes 1769480 | tf_op jit(solution)/shard_map/ppermute | solution.py:159
  61.6 11.0 %all-to-all-start = ((f32[32,8,128]{2,1,0:T(8,128)}), f32[32,8,128]{2,1,0:T(8,128)S(1)}, u32[]{:S(2)}, u32[]{:S(2)}) async-start(f32[32,8,128]{2,1,0:T(8,128)} %get-tuple-element.60), calls=%async_computation | async-start | bytes 262144 | tf_op jit(solution)/shard_map/all_to_all | solution.py:205
  64.5 4.3 %copy-start.1 = (bf16[256,1152]{1,0:T(8,128)(2,1)S(1)}, bf16[256,1152]{1,0:T(8,128)(2,1)}, u32[]{:S(2)}) copy-start(bf16[256,1152]{1,0:T(8,128)(2,1)} %refs_5_.1) | copy-start | bytes 1769476
  64.5 4.2 %copy-start.4 = (f32[256,128]{1,0:T(8,128)S(1)}, f32[256,128]{1,0:T(8,128)}, u32[]{:S(2)}) copy-start(f32[256,128]{1,0:T(8,128)} %copy-done.3) | copy-start | bytes 393220

commit v3 on v1

v3 whole, which is shorter than its diff:
```python
import functools

import jax
import jax.numpy as jnp
from jax import lax
from jax.experimental import pallas as pl
from jax.experimental.pallas import tpu as pltpu
from jax.sharding import PartitionSpec as P

REACH = 2
QUAD = 4
VMEM_LIMIT = 16 * 1024 * 1024
IN_VMEM = pl.BlockSpec(memory_space=pltpu.VMEM)
IN_SMEM = pl.BlockSpec(memory_space=pltpu.SMEM)


def unit_rows(raw):
    wide = raw.astype(jnp.float32)
    inverse = 1.0 / jnp.sqrt(jnp.sum(wide * wide, axis=1, keepdims=True) + 1e-06)
    return wide * inverse, inverse


def slopes(similar, temper, offset_bias, diagonal):
    logits = temper * similar + offset_bias
    tail = jnp.exp(-jnp.abs(logits))
    upper = jnp.where(logits >= 0, 1.0, tail) / (1.0 + tail)
    if not diagonal:
        return logits, tail, upper, logits
    lower = jnp.where(logits >= 0, tail, 1.0) / (1.0 + tail)
    same = lax.broadcasted_iota(jnp.int32, similar.shape, 0) == lax.broadcasted_iota(
        jnp.int32, similar.shape, 1
    )
    return logits, tail, jnp.where(same, -lower, upper), jnp.where(same, -logits, logits)


def fold(tile):
    rows, columns = tile.shape
    part = jnp.sum(tile.reshape(rows // 8, 8, columns), axis=0)
    return sum(part[:, c : c + 128] for c in range(0, columns, 128))


def tallies(margin, tail, slope, logits_part):
    pair_loss = jnp.maximum(margin, 0.0) + jnp.log1p(tail)
    return jnp.concatenate([fold(pair_loss), fold(slope * logits_part), fold(slope)], axis=0)


def across(left, right):
    return lax.dot_general(
        left, right, (((1,), (1,)), ((), ())), preferred_element_type=jnp.float32
    )


def own_kernel(scalars, image, text, img_unit, txt_unit, img_inv, txt_inv, gx, gy, stats):
    temper, offset_bias = scalars[0], scalars[1]
    x_wide, x_inv = unit_rows(image[...])
    y_wide, y_inv = unit_rows(text[...])
    x, y = x_wide.astype(jnp.bfloat16), y_wide.astype(jnp.bfloat16)
    img_unit[...] = x
    txt_unit[...] = y
    img_inv[...] = jnp.broadcast_to(x_inv, img_inv.shape)
    txt_inv[...] = jnp.broadcast_to(y_inv, txt_inv.shape)
    similar = across(x, y)
    _, tail, slope, margin = slopes(similar, temper, offset_bias, True)
    stats[...] = tallies(margin, tail, slope, temper * similar)
    scaled = (temper * slope).astype(jnp.bfloat16)
    gx[...] = jnp.dot(scaled, y, preferred_element_type=jnp.float32)
    _, _, slope, _ = slopes(across(y, x), temper, offset_bias, True)
    scaled = (temper * slope).astype(jnp.bfloat16)
    gy[...] = jnp.dot(scaled, x, preferred_element_type=jnp.float32)


def widened(ref):
    return ref[...].astype(jnp.float32)


def rounded_unit(raw):
    return unit_rows(raw)[0].astype(jnp.bfloat16)


def meet(scalars, own, unit, counted=False):
    temper, offset_bias = scalars[0], scalars[1]
    similar = across(own, unit)
    logits, tail, slope, _ = slopes(similar, temper, offset_bias, False)
    scaled = (temper * slope).astype(jnp.bfloat16)
    grad = jnp.dot(scaled, unit, preferred_element_type=jnp.float32)
    tally = tallies(logits, tail, slope, temper * similar) if counted else None
    return grad, tally


def finished(grad, raw, inverse):
    inv = inverse[:, :1]
    wide = widened(raw) * inv
    return inv * (grad - wide * jnp.sum(wide * grad, axis=1, keepdims=True))


def text_pair_kernel(scalars, own, first, second, gx, stats, gx_out, stats_out, unit_out):
    unit = rounded_unit(widened(first))
    unit_out[...] = unit
    grad_a, tally_a = meet(scalars, own[...], unit, True)
    grad_b, tally_b = meet(scalars, own[...], rounded_unit(widened(second)), True)
    gx_out[...] = gx[...] + grad_a + grad_b
    stats_out[...] = stats[...] + tally_a + tally_b


def image_pair_kernel(scalars, own, first, second, gy, gy_out, part, unit_out):
    part[...] = second[: part.shape[0]]
    unit = rounded_unit(widened(second))
    unit_out[...] = unit
    grad_a, _ = meet(scalars, own[...], rounded_unit(widened(first)))
    grad_b, _ = meet(scalars, own[...], unit)
    gy_out[...] = gy[...] + grad_a + grad_b


def text_far_kernel(scalars, own, far, near_image, near_text, gx, stats, gx_out, sums_out):
    temper, offset_bias = scalars[0], scalars[1]
    wide = unit_rows(widened(far))[0]
    grad, tally = meet(scalars, own[...], wide.astype(jnp.bfloat16), True)
    gx_out[...] = gx[...] + grad
    partner = jnp.where(scalars[2] > 0.5, widened(near_text), wide).astype(jnp.bfloat16)
    similar = across(near_image[...], partner)
    logits, tail, slope, _ = slopes(similar, temper, offset_bias, False)
    tally = stats[...] + tally + tallies(logits, tail, slope, temper * similar)
    lane = lax.broadcasted_iota(jnp.int32, (8, 128), 1)
    sums = [jnp.sum(tally[8 * i : 8 * i + 8]) for i in range(3)]
    row = jnp.where(lane == 0, sums[0], jnp.where(lane == 1, sums[1], sums[2]))
    sums_out[...] = jnp.broadcast_to(row[None], sums_out.shape)


def image_far_kernel(scalars, own, far, upper, middle, gy, gy_out):
    grad_a, _ = meet(scalars, own[...], rounded_unit(widened(far)))
    block = jnp.where(scalars[2] > 0.5, widened(upper), widened(middle.at[: upper.shape[0]]))
    grad_b, _ = meet(scalars, own[...], rounded_unit(block))
    gy_out[...] = gy[...] + grad_a + grad_b


def pick_kernel(scalars, outer, inner, out):
    out[...] = jnp.where(scalars[2] > 0.5, widened(outer), widened(inner)).astype(out.dtype)


def last_text_kernel(scalars, own, block, acc, raw, inverse, out):
    grad, _ = meet(scalars, own[...], rounded_unit(widened(block)))
    out[...] = finished(acc[...] + grad, raw, inverse)


def last_image_kernel(scalars, own, lower, middle, acc, raw, inverse, out):
    rest = widened(middle.at[middle.shape[0] - lower.shape[0] :])
    block = jnp.where(scalars[2] > 0.5, widened(lower), rest)
    grad, _ = meet(scalars, own[...], rounded_unit(block))
    out[...] = finished(acc[...] + grad, raw, inverse)


def tied(*values):
    return lax.optimization_barrier(values)


def cost(rows, width, tiles):
    return pl.CostEstimate(
        flops=4 * tiles * rows * rows * width,
        bytes_accessed=12 * tiles * rows * width,
        transcendentals=tiles * rows * rows,
    )


def call(kernel, operands, shapes, rows, width, tiles):
    return pl.pallas_call(
        kernel,
        out_shape=shapes,
        in_specs=[IN_SMEM] + [IN_VMEM] * (len(operands) - 1),
        out_specs=tuple(IN_VMEM for _ in shapes),
        compiler_params=pltpu.CompilerParams(vmem_limit_bytes=VMEM_LIMIT),
        cost_estimate=cost(rows, width, tiles),
    )(*operands)


def on_device(image, text, log_temp, bias):
    rows, width = image.shape
    half = rows // 2
    blocks = lax.axis_size("blk")
    devices = blocks * lax.axis_size("grp")
    place = lax.axis_index("blk") % QUAD
    everyone = range(blocks)
    f32 = jnp.float32
    scalars = jnp.stack(
        [jnp.exp(log_temp[0]), bias[0], jnp.where((place == 0) | (place == 3), 1.0, 0.0).astype(f32)]
    )

    def send(block, route):
        return lax.ppermute(block, "blk", route)

    beside = [(b, b ^ 1) for b in everyone]
    above = [(b, b ^ 2) for b in everyone]
    beyond = [(b, (b + QUAD if b % QUAD < 2 else b - QUAD) % blocks) for b in everyone]
    corner = [(b, b ^ 1) for b in everyone if b % QUAD in (1, 2)]
    turn = [(b, (b + 2 if b % QUAD == 2 else b - 2) % blocks) for b in everyone if b % QUAD in (1, 2)]
    middle = [(b, b ^ 1) for b in everyone if b % QUAD in (0, 3)]
    mixed = [(b, b ^ (1 if b % QUAD in (1, 2) else 2)) for b in everyone]

    tile = jax.ShapeDtypeStruct((rows, width), f32)
    unit = jax.ShapeDtypeStruct((rows, width), jnp.bfloat16)
    part = jax.ShapeDtypeStruct((half, width), jnp.bfloat16)
    column = jax.ShapeDtypeStruct((rows, 128), f32)
    tally = jax.ShapeDtypeStruct((24, 128), f32)
    spread = jax.ShapeDtypeStruct((devices, 8, 128), f32)

    def run(kernel, tiles, operands, *shapes):
        return call(kernel, [scalars, *operands], shapes, rows, width, tiles)

    txt_y = send(text, above)
    txt_x = send(text, beside)
    img_y = send(image, above)
    img_x = send(image, beside)
    img_unit, txt_unit, img_inv, txt_inv, gx, gy, stats = run(
        own_kernel, 2, [image, text], unit, unit, column, column, tile, tile, tally
    )

    txt_y, gx, gy = tied(txt_y, gx, gy)
    txt_z = send(txt_y, beyond)
    gx, stats, unit_y = run(
        text_pair_kernel, 2, [img_unit, txt_y, txt_x, gx, stats], tile, tally, unit
    )
    img_y, img_x, gx = tied(img_y, img_x, gx)
    img_z = send(img_y, beyond)
    (txt_v,) = run(pick_kernel, 1, [txt_x, txt_z], unit)
    txt_w = send(txt_v, mixed)
    txt_v, gy, img_y = tied(txt_v, gy, img_y)
    img_m = send(img_y, middle)
    gy, img_h, unit_x = run(
        image_pair_kernel, 2, [txt_unit, img_y, img_x, gy], tile, part, unit
    )
    img_t = send(img_h, turn)
    gx, sums = run(
        text_far_kernel, 2, [img_unit, txt_z, unit_x, unit_y, gx, stats], tile, spread
    )
    img_z, gx, gy = tied(img_z, gx, gy)
    img_c = send(img_z[half:], corner)
    (gy,) = run(image_far_kernel, 2, [txt_unit, img_z, img_t, img_m, gy], tile)
    img_m, gx, gy = tied(img_m, gx, gy)
    sums, txt_w = tied(sums, txt_w)
    seen = lax.all_to_all(sums, ("blk", "grp"), 0, 0)
    pairs = jnp.float32(rows * rows * (2 * REACH + 1) * devices)
    statistics = jnp.sum(seen[:, 0, :3], axis=0) / pairs
    (grad_image,) = run(last_text_kernel, 1, [img_unit, txt_w, gx, image, img_inv], tile)
    (grad_text,) = run(
        last_image_kernel, 1, [txt_unit, img_c, img_m, gy, text, txt_inv], tile
    )
    return grad_image, grad_text, statistics


def solution(mesh):
    placed = P(("blk", "grp"), None)
    return jax.shard_map(
        on_device,
        mesh=mesh,
        in_specs=(placed, placed, P(), P()),
        out_specs=(placed, placed, P()),
        check_vma=False,
    )
```

time: 83.1 us -> 69 us (0.83)
  starting transfers between devices: 30.5 us -> 22.4 us
  waiting for transfers between devices: 22.8 us -> 16.2 us
  local copies, waits for them, and re-layouts: 3.62 us -> 5.56 us
  Pallas kernels: 21.9 us -> 20.6 us
    ppermute x10, starting transfers between devices: 24.7 us -> 15.4 us  [send(): return lax.ppermute(block, 'blk', route)]
    ppermute x10, waiting for transfers between devices: 22.8 us -> 16.2 us  [send(): return lax.ppermute(block, 'blk', route)]
    pallas_call x9 -> x8, Pallas kernels: 21.9 us -> 20.6 us  [call(): pl.pallas_call(kernel, out_shape=shapes, in_specs=[IN_SMEM] + [IN_VMEM] *...]
    all_to_all x1, starting transfers between devices: 5.8 us -> 7.03 us  [on_device(): seen = lax.all_to_all(sums, ('blk', 'grp'), 0, 0)]
    unnamed x16 -> x30, local copies, waits for them, and re-layouts: 3.62 us -> 4.81 us
  transfers between devices with their start and end apart: 11 -> 11, of which waited for: 3 -> 4; matrix products, arithmetic and copies ran while one was open for 0% -> 1% of each run, Pallas kernels for 27% -> 30%
where the time goes in v3:
time: 69 us; the launch traced here: 68.5 us
  starting transfers between devices  22.4 us (32%)
  Pallas kernels  20.6 us (30%)
  waiting for transfers between devices  16.2 us (23%)
  local copies, waits for them, and re-layouts  5.56 us (8%)
  between operations  2.22 us (3%)
  other arithmetic  1.55 us (2%)
    pallas_call x8, Pallas kernels, call(): pl.pallas_call(kernel, out_shape=shapes, in_specs=[IN_SMEM] + [IN_VMEM] *...  20.6 us
    ppermute x10, waiting for transfers between devices, send(): return lax.ppermute(block, 'blk', route)  16.2 us
    ppermute x10, starting transfers between devices, send(): return lax.ppermute(block, 'blk', route)  15.4 us
    all_to_all x1, starting transfers between devices, on_device(): seen = lax.all_to_all(sums, ('blk', 'grp'), 0, 0)  7.03 us
    unnamed x30, local copies, waits for them, and re-layouts  4.81 us
  transfers between devices with their start and end apart: 11, of which 4 were waited for; matrix products, arithmetic and copies ran while one was open for 1% of the time, Pallas kernels for 30%

profile of v3, /device:TPU:0, one launch (start us, length us, event | category | flops | bytes accessed | tf_op | source)
XLA Modules:
  0.0 68.5 jit_solution(6001848738748783092)
XLA Ops:
  0.6 3.0 %collective-permute-start = (bf16[256,1152]{1,0:T(8,128)(2,1)}, bf16[256,1152]{1,0:T(8,128)(2,1)S(1)}, u32[]{:S(2)}, u32[]{:S(2)}) collective-permute-start(bf16[256,1152]{1,0:T(8,128)(2,1)} %raw.3), channel_id=1, source_target_pairs={{0,4},{2,6},{4,0},{6,2},{8,12},{10,14},{12,8},{14,10},{16,20},{18,... | collective-permute-start | bytes 1769480 | tf_op jit(solution)/shard_map/ppermute | solution.py:188
  3.7 1.5 %collective-permute-start.2 = (bf16[256,1152]{1,0:T(8,128)(2,1)}, bf16[256,1152]{1,0:T(8,128)(2,1)S(1)}, u32[]{:S(2)}, u32[]{:S(2)}) collective-permute-start(bf16[256,1152]{1,0:T(8,128)(2,1)} %raw.3), channel_id=1, source_target_pairs={{0,2},{2,0},{4,6},{6,4},{8,10},{10,8},{12,14},{14,12},{16,18},{18,... | collective-permute-start | bytes 1769480 | tf_op jit(solution)/shard_map/ppermute | solution.py:188
  5.2 0.5 collective-permute-start.3
  5.7 0.1 collective-permute-start.4
  7.1 0.1 pad_maximum_fusion.scalars
  7.2 1.1 %copy-done.2 = bf16[256,1152]{1,0:T(8,128)(2,1)S(1)} copy-done((bf16[256,1152]{1,0:T(8,128)(2,1)S(1)}, bf16[256,1152]{1,0:T(8,128)(2,1)}, u32[]{:S(2)}) %copy-start.2) | copy-done | bytes 589848
  8.3 1.1 %copy-done.4 = bf16[256,1152]{1,0:T(8,128)(2,1)S(1)} copy-done((bf16[256,1152]{1,0:T(8,128)(2,1)S(1)}, bf16[256,1152]{1,0:T(8,128)(2,1)}, u32[]{:S(2)}) %copy-start.4) | copy-done | bytes 589848
  9.3 2.7 %shard_map.67 = (bf16[256,1152]{1,0:T(8,128)(2,1)S(1)}, bf16[256,1152]{1,0:T(8,128)(2,1)S(1)}, f32[256,128]{1,0:T(8,128)S(1)}, f32[256,128]{1,0:T(8,128)S(1)}, f...) custom-call(f32[3]{0:T(128)S(1)} %pad_maximum_fusion.scalars, ...), custom_call_target="tpu_custom_call" | custom-call | flops 603979776 | bytes 7077888 | tf_op jit(solution)/shard_map/pallas_call | solution.py:165
  12.1 0.0 copy-start.10
  12.1 0.0 copy-start.12
  12.1 5.9 %collective-permute-done.first = bf16[256,1152]{1,0:T(8,128)(2,1)S(1)} collective-permute-done((bf16[256,1152]{1,0:T(8,128)(2,1)}, bf16[256,1152]{1,0:T(8,128)(2,1)S(1)}, u32[]{:S(2)}, u32[]{:S(2)}) %collective-permute-start) | collective-permute-done | bytes 589856 | tf_op jit(solution)/shard_map/ppermute | solution.py:188
  18.0 2.1 %collective-permute-start.1 = (bf16[256,1152]{1,0:T(8,128)(2,1)S(1)}, bf16[256,1152]{1,0:T(8,128)(2,1)S(1)}, u32[]{:S(2)}, u32[]{:S(2)}) collective-permute-start(bf16[256,1152]{1,0:T(8,128)(2,1)S(1)} %collective-permute-done.first), channel_id=1, source_target_pairs={{0,8},{2,10},{4,28},{6,30},{8,16},{10,18},{12,4},{14,6},{16,24},{1... | collective-permute-start | bytes 1769480 | tf_op jit(solution)/shard_map/ppermute | solution.py:188
  20.1 0.0 collective-permute-done.2.outer.second
  20.1 2.5 %shard_map.69 = (f32[256,1152]{1,0:T(8,128)S(1)}, f32[24,128]{1,0:T(8,128)S(1)}, bf16[256,1152]{1,0:T(8,128)(2,1)S(1)}) custom-call(f32[3]{0:T(128)S(1)} %pad_maximum_fusion.scalars, bf16[256,1152]{1,0:T(8,128)(2,1)S(1)} %get-tuple-element.34.own, bf16[256,1152]{1,0:T(8,128)(2,1)S(1)} %collective-permute-done.first, ...), custom_call_target="tpu_custom_call" | custom-call | flops 603979776 | bytes 7077888 | tf_op jit(solution)/shard_map/pallas_call | solution.py:165
  22.7 7.3 %collective-permute-done.3.first = bf16[256,1152]{1,0:T(8,128)(2,1)} collective-permute-done((bf16[256,1152]{1,0:T(8,128)(2,1)}, bf16[256,1152]{1,0:T(8,128)(2,1)}, u32[]{:S(2)}, u32[]{:S(2)}) %collective-permute-start.3) | collective-permute-done | bytes 589856 | tf_op jit(solution)/shard_map/ppermute | solution.py:188
  29.9 1.4 %collective-permute-done.4.second = bf16[256,1152]{1,0:T(8,128)(2,1)S(1)} collective-permute-done((bf16[256,1152]{1,0:T(8,128)(2,1)}, bf16[256,1152]{1,0:T(8,128)(2,1)S(1)}, u32[]{:S(2)}, u32[]{:S(2)}) %collective-permute-start.4) | collective-permute-done | bytes 589856 | tf_op jit(solution)/shard_map/ppermute | solution.py:188
  31.3 0.8 %copy-done.8 = bf16[256,1152]{1,0:T(8,128)(2,1)} copy-done((bf16[256,1152]{1,0:T(8,128)(2,1)}, bf16[256,1152]{1,0:T(8,128)(2,1)S(1)}, u32[]{:S(2)}) %copy-start.8) | copy-done | bytes 589848
  32.1 1.6 %collective-permute-start.7 = (bf16[256,1152]{1,0:T(8,128)(2,1)}, bf16[256,1152]{1,0:T(8,128)(2,1)S(1)}, u32[]{:S(2)}, u32[]{:S(2)}) collective-permute-start(bf16[256,1152]{1,0:T(8,128)(2,1)} %collective-permute-done.3.first), channel_id=1, source_target_pairs={{0,8},{2,10},{4,28},{6,30},{8,16},{10,18},{12,4},{14,6},{16,24},{1... | collective-permute-start | bytes 1769480 | tf_op jit(solution)/shard_map/ppermute | solution.py:188
  33.7 0.0 collective-permute-done.1.inner.far
  33.7 0.7 %shard_map.68 = bf16[256,1152]{1,0:T(8,128)(2,1)S(1)} custom-call(f32[3]{0:T(128)S(1)} %pad_maximum_fusion.scalars, bf16[256,1152]{1,0:T(8,128)(2,1)S(1)} %collective-permute-done.2.outer.second, bf16[256,1152]{1,0:T(8,128)(2,1)S(1)} %collective-permute-done.1.inner.far), custom_call_target="tpu_custom_call" | custom-call | flops 301989888 | bytes 3538944 | tf_op jit(solution)/shard_map/pallas_call | solution.py:165
  34.4 2.6 %collective-permute-start.5 = (bf16[256,1152]{1,0:T(8,128)(2,1)S(1)}, bf16[256,1152]{1,0:T(8,128)(2,1)S(1)}, u32[]{:S(2)}, u32[]{:S(2)}) collective-permute-start(bf16[256,1152]{1,0:T(8,128)(2,1)S(1)} %shard_map.68), channel_id=1, source_target_pairs={{0,4},{2,0},{4,6},{6,2},{8,12},{10,8},{12,14},{14,10},{16,20},{18,... | collective-permute-start | bytes 1769480 | tf_op jit(solution)/shard_map/ppermute | solution.py:188
  37.0 1.4 %collective-permute-start.6 = (bf16[256,1152]{1,0:T(8,128)(2,1)}, bf16[256,1152]{1,0:T(8,128)(2,1)S(1)}, u32[]{:S(2)}, u32[]{:S(2)}) collective-permute-start(bf16[256,1152]{1,0:T(8,128)(2,1)} %collective-permute-done.3.first), channel_id=1, source_target_pairs={{0,2},{6,4},{8,10},{14,12},{16,18},{22,20},{24,26},{30,28},{1,3},{... | collective-permute-start | bytes 1769480 | tf_op jit(solution)/shard_map/ppermute | solution.py:188
  38.4 3.5 %shard_map.70 = (f32[256,1152]{1,0:T(8,128)S(1)}, bf16[128,1152]{1,0:T(8,128)(2,1)}, bf16[256,1152]{1,0:T(8,128)(2,1)S(1)}) custom-call(f32[3]{0:T(128)S(1)} %pad_maximum_fusion.scalars, bf16[256,1152]{1,0:T(8,128)(2,1)S(1)} %get-tuple-element.38.own, bf16[256,1152]{1,0:T(8,128)(2,1)} %collective-permute-done.3.first, bf16[256,1152]{1,0:T(8,128)(2,1)S(1)} %copy-done.9, ...), custom_call_target="tpu_custom_call" | custom-call | flops 603979776 | bytes 7077888 | tf_op jit(solution)/shard_map/pallas_call | solution.py:165
  41.9 1.3 %collective-permute-start.8 = (bf16[128,1152]{1,0:T(8,128)(2,1)}, bf16[128,1152]{1,0:T(8,128)(2,1)}, u32[]{:S(2)}, u32[]{:S(2)}) collective-permute-start(bf16[128,1152]{1,0:T(8,128)(2,1)} %get-tuple-element.57), channel_id=1, source_target_pairs={{2,30},{4,8},{10,6},{12,16},{18,14},{20,24},{26,22},{28,0},{3,31},... | collective-permute-start | bytes 884744 | tf_op jit(solution)/shard_map/ppermute | solution.py:188
  43.2 2.3 %shard_map.71 = (f32[256,1152]{1,0:T(8,128)S(1)}, f32[32,8,128]{2,1,0:T(8,128)S(1)}) custom-call(f32[3]{0:T(128)S(1)} %pad_maximum_fusion.scalars, bf16[256,1152]{1,0:T(8,128)(2,1)S(1)} %get-tuple-element.34.own, bf16[256,1152]{1,0:T(8,128)(2,1)S(1)} %collective-permute-done.1.inner.far, bf16[256,1152]{1,0:T(8,128)(2,1)S(1)} %get-tuple-element.47.near_image, ...), custom_call_target="tpu_custom_call" | custom-call | flops 603979776 | bytes 7077888 | tf_op jit(solution)/shard_map/pallas_call | solution.py:165
  45.5 0.0 copy-start
  45.6 1.0 %copy-done = f32[256,1152]{1,0:T(8,128)} copy-done((f32[256,1152]{1,0:T(8,128)}, f32[256,1152]{1,0:T(8,128)S(1)}, u32[]{:S(2)}) %copy-start) | copy-done | bytes 1179672
  46.6 1.6 %collective-permute-done.7.far = bf16[256,1152]{1,0:T(8,128)(2,1)S(1)} collective-permute-done((bf16[256,1152]{1,0:T(8,128)(2,1)}, bf16[256,1152]{1,0:T(8,128)(2,1)S(1)}, u32[]{:S(2)}, u32[]{:S(2)}) %collective-permute-start.7) | collective-permute-done | bytes 589856 | tf_op jit(solution)/shard_map/ppermute | solution.py:188
  48.2 0.7 %slice.6 = bf16[128,1152]{1,0:T(8,128)(2,1)} slice(bf16[256,1152]{1,0:T(8,128)(2,1)S(1)} %collective-permute-done.7.far), slice={[128:256], [0:1152]} | slice | bytes 589824 | tf_op jit(solution)/shard_map/slice | solution.py:235
  48.9 1.3 %collective-permute-start.9 = (bf16[128,1152]{1,0:T(8,128)(2,1)}, bf16[128,1152]{1,0:T(8,128)(2,1)}, u32[]{:S(2)}, u32[]{:S(2)}) collective-permute-start(bf16[128,1152]{1,0:T(8,128)(2,1)} %slice.6), channel_id=1, source_target_pairs={{2,0},{4,6},{10,8},{12,14},{18,16},{20,22},{26,24},{28,30},{3,1},{... | collective-permute-start | bytes 884744 | tf_op jit(solution)/shard_map/ppermute | solution.py:188
  50.2 0.0 collective-permute-done.5.block
  50.2 0.0 copy-start.6
  50.2 0.8 %copy-done.6 = bf16[256,1152]{1,0:T(8,128)(2,1)} copy-done((bf16[256,1152]{1,0:T(8,128)(2,1)}, bf16[256,1152]{1,0:T(8,128)(2,1)S(1)}, u32[]{:S(2)}) %copy-start.6) | copy-done | bytes 589848
  51.0 7.0 %all-to-all-start = ((f32[32,8,128]{2,1,0:T(8,128)}), f32[32,8,128]{2,1,0:T(8,128)}, u32[]{:S(2)}, u32[]{:S(2)}) async-start(f32[32,8,128]{2,1,0:T(8,128)} %copy-done.14), calls=%async_computation | async-start | bytes 262144 | tf_op jit(solution)/shard_map/all_to_all | solution.py:239
  58.1 0.0 copy-start.1
  58.1 0.0 copy-start.3
  58.1 0.0 copy-start.7
  58.1 0.0 copy-start.13
  58.1 0.0 collective-permute-done.8.upper
  58.1 0.0 collective-permute-done.6.middle
  58.2 2.7 %shard_map.72.acc = f32[256,1152]{1,0:T(8,128)S(1)} custom-call(f32[3]{0:T(128)S(1)} %pad_maximum_fusion.scalars, bf16[256,1152]{1,0:T(8,128)(2,1)S(1)} %get-tuple-element.38.own, bf16[256,1152]{1,0:T(8,128)(2,1)S(1)} %collective-permute-done.7.far, bf16[128,1152]{1,0:T(8,128)(2,1)} %collective-permute-done.8.upper, ...), custom_call_target="tpu_custom_call" | custom-call | flops 603979776 | bytes 7077888 | tf_op jit(solution)/shard_map/pallas_call | solution.py:165
  60.9 0.0 copy-start.5
  60.9 2.9 %shard_map.73 = f32[256,1152]{1,0:T(8,128)} custom-call(f32[3]{0:T(128)S(1)} %pad_maximum_fusion.scalars, bf16[256,1152]{1,0:T(8,128)(2,1)S(1)} %get-tuple-element.34.own, bf16[256,1152]{1,0:T(8,128)(2,1)S(1)} %copy-done.7, f32[256,1152]{1,0:T(8,128)S(1)} %copy-done.1, bf16[256,1152]{1,0:T(8,128)(2,1)S(1)} %copy-done.3, f32[256,128]{1,0:T(8,128)S(1)} %copy-done.13), custom_call_target="tpu_custom_call" | custom-call | flops 301989888 | bytes 3538944 | tf_op jit(solution)/shard_map/pallas_call | solution.py:165
  63.8 0.0 collective-permute-done.9.lower
  63.8 3.2 %shard_map.74 = f32[256,1152]{1,0:T(8,128)} custom-call(f32[3]{0:T(128)S(1)} %pad_maximum_fusion.scalars, bf16[256,1152]{1,0:T(8,128)(2,1)S(1)} %get-tuple-element.38.own, bf16[128,1152]{1,0:T(8,128)(2,1)} %collective-permute-done.9.lower, bf16[256,1152]{1,0:T(8,128)(2,1)S(1)} %collective-permute-done.6.middle, f32[256,1152]{1,0:T(8,128)S(1)} %shard_map.72.acc, ...), custom_call_target="tpu_custom_call" | custom-call | flops 301989888 | bytes 3538944 | tf_op jit(solution)/shard_map/pallas_call | solution.py:165
  67.0 0.0 all-to-all-done
  67.0 1.0 %slice_reduce_fusion = f32[3]{0:T(128)S(1)} fusion(f32[32,8,128]{2,1,0:T(8,128)} %all-to-all-done), kind=kLoop, calls=%fused_computation | loop fusion | flops 93 | bytes 396 | tf_op jit(solution)/shard_map/reduce_sum | solution.py:241
  68.0 0.5 broadcast_multiply_fusion
  (16 shorter events, 0.0 us)
Async XLA Ops:
  0.6 17.4 %collective-permute-start = (bf16[256,1152]{1,0:T(8,128)(2,1)}, bf16[256,1152]{1,0:T(8,128)(2,1)S(1)}, u32[]{:S(2)}, u32[]{:S(2)}) collective-permute-start(bf16[256,1152]{1,0:T(8,128)(2,1)} %raw.3), channel_id=1, source_target_pairs={{0,4},{2,6},{4,0},{6,2},{8,12},{10,14},{12,8},{14,10},{16,20},{18,... | collective-permute-start | bytes 1769480 | tf_op jit(solution)/shard_map/ppermute | solution.py:188
  3.7 16.5 %collective-permute-start.2 = (bf16[256,1152]{1,0:T(8,128)(2,1)}, bf16[256,1152]{1,0:T(8,128)(2,1)S(1)}, u32[]{:S(2)}, u32[]{:S(2)}) collective-permute-start(bf16[256,1152]{1,0:T(8,128)(2,1)} %raw.3), channel_id=1, source_target_pairs={{0,2},{2,0},{4,6},{6,4},{8,10},{10,8},{12,14},{14,12},{16,18},{18,... | collective-permute-start | bytes 1769480 | tf_op jit(solution)/shard_map/ppermute | solution.py:188
  5.2 24.8 %collective-permute-start.3 = (bf16[256,1152]{1,0:T(8,128)(2,1)}, bf16[256,1152]{1,0:T(8,128)(2,1)}, u32[]{:S(2)}, u32[]{:S(2)}) collective-permute-start(bf16[256,1152]{1,0:T(8,128)(2,1)} %raw.2), channel_id=1, source_target_pairs={{0,4},{2,6},{4,0},{6,2},{8,12},{10,14},{12,8},{14,10},{16,20},{18,... | collective-permute-start | bytes 1769480 | tf_op jit(solution)/shard_map/ppermute | solution.py:188
  5.7 25.6 %collective-permute-start.4 = (bf16[256,1152]{1,0:T(8,128)(2,1)}, bf16[256,1152]{1,0:T(8,128)(2,1)S(1)}, u32[]{:S(2)}, u32[]{:S(2)}) collective-permute-start(bf16[256,1152]{1,0:T(8,128)(2,1)} %raw.2), channel_id=1, source_target_pairs={{0,2},{2,0},{4,6},{6,4},{8,10},{10,8},{12,14},{14,12},{16,18},{18,... | collective-permute-start | bytes 1769480 | tf_op jit(solution)/shard_map/ppermute | solution.py:188
  7.2 1.1 %copy-start.2 = (bf16[256,1152]{1,0:T(8,128)(2,1)S(1)}, bf16[256,1152]{1,0:T(8,128)(2,1)}, u32[]{:S(2)}) copy-start(bf16[256,1152]{1,0:T(8,128)(2,1)} %raw.2) | copy-start | bytes 1769476
  8.3 1.1 %copy-start.4 = (bf16[256,1152]{1,0:T(8,128)(2,1)S(1)}, bf16[256,1152]{1,0:T(8,128)(2,1)}, u32[]{:S(2)}) copy-start(bf16[256,1152]{1,0:T(8,128)(2,1)} %raw.3) | copy-start | bytes 1769476
  12.1 10.6 %copy-start.10 = (f32[256,128]{1,0:T(8,128)}, f32[256,128]{1,0:T(8,128)S(1)}, u32[]{:S(2)}) copy-start(f32[256,128]{1,0:T(8,128)S(1)} %get-tuple-element.63.inverse) | copy-start | bytes 393220
  12.1 10.6 %copy-start.12 = (f32[256,128]{1,0:T(8,128)}, f32[256,128]{1,0:T(8,128)S(1)}, u32[]{:S(2)}) copy-start(f32[256,128]{1,0:T(8,128)S(1)} %get-tuple-element.60.inverse) | copy-start | bytes 393220
  18.0 15.7 %collective-permute-start.1 = (bf16[256,1152]{1,0:T(8,128)(2,1)S(1)}, bf16[256,1152]{1,0:T(8,128)(2,1)S(1)}, u32[]{:S(2)}, u32[]{:S(2)}) collective-permute-start(bf16[256,1152]{1,0:T(8,128)(2,1)S(1)} %collective-permute-done.first), channel_id=1, source_target_pairs={{0,8},{2,10},{4,28},{6,30},{8,16},{10,18},{12,4},{14,6},{16,24},{1... | collective-permute-start | bytes 1769480 | tf_op jit(solution)/shard_map/ppermute | solution.py:188
  31.3 0.8 %copy-start.8 = (bf16[256,1152]{1,0:T(8,128)(2,1)}, bf16[256,1152]{1,0:T(8,128)(2,1)S(1)}, u32[]{:S(2)}) copy-start(bf16[256,1152]{1,0:T(8,128)(2,1)S(1)} %collective-permute-done.4.second) | copy-start | bytes 1769476
  32.1 6.3 %copy-start.9 = (bf16[256,1152]{1,0:T(8,128)(2,1)S(1)}, bf16[256,1152]{1,0:T(8,128)(2,1)}, u32[]{:S(2)}) copy-start(bf16[256,1152]{1,0:T(8,128)(2,1)} %copy-done.8) | copy-start | bytes 1769476
  32.1 16.1 %collective-permute-start.7 = (bf16[256,1152]{1,0:T(8,128)(2,1)}, bf16[256,1152]{1,0:T(8,128)(2,1)S(1)}, u32[]{:S(2)}, u32[]{:S(2)}) collective-permute-start(bf16[256,1152]{1,0:T(8,128)(2,1)} %collective-permute-done.3.first), channel_id=1, source_target_pairs={{0,8},{2,10},{4,28},{6,30},{8,16},{10,18},{12,4},{14,6},{16,24},{1... | collective-permute-start | bytes 1769480 | tf_op jit(solution)/shard_map/ppermute | solution.py:188
  34.4 15.8 %collective-permute-start.5 = (bf16[256,1152]{1,0:T(8,128)(2,1)S(1)}, bf16[256,1152]{1,0:T(8,128)(2,1)S(1)}, u32[]{:S(2)}, u32[]{:S(2)}) collective-permute-start(bf16[256,1152]{1,0:T(8,128)(2,1)S(1)} %shard_map.68), channel_id=1, source_target_pairs={{0,4},{2,0},{4,6},{6,2},{8,12},{10,8},{12,14},{14,10},{16,20},{18,... | collective-permute-start | bytes 1769480 | tf_op jit(solution)/shard_map/ppermute | solution.py:188
  37.0 21.2 %collective-permute-start.6 = (bf16[256,1152]{1,0:T(8,128)(2,1)}, bf16[256,1152]{1,0:T(8,128)(2,1)S(1)}, u32[]{:S(2)}, u32[]{:S(2)}) collective-permute-start(bf16[256,1152]{1,0:T(8,128)(2,1)} %collective-permute-done.3.first), channel_id=1, source_target_pairs={{0,2},{6,4},{8,10},{14,12},{16,18},{22,20},{24,26},{30,28},{1,3},{... | collective-permute-start | bytes 1769480 | tf_op jit(solution)/shard_map/ppermute | solution.py:188
  41.9 16.2 %collective-permute-start.8 = (bf16[128,1152]{1,0:T(8,128)(2,1)}, bf16[128,1152]{1,0:T(8,128)(2,1)}, u32[]{:S(2)}, u32[]{:S(2)}) collective-permute-start(bf16[128,1152]{1,0:T(8,128)(2,1)} %get-tuple-element.57), channel_id=1, source_target_pairs={{2,30},{4,8},{10,6},{12,16},{18,14},{20,24},{26,22},{28,0},{3,31},... | collective-permute-start | bytes 884744 | tf_op jit(solution)/shard_map/ppermute | solution.py:188
  45.5 1.0 %copy-start = (f32[256,1152]{1,0:T(8,128)}, f32[256,1152]{1,0:T(8,128)S(1)}, u32[]{:S(2)}) copy-start(f32[256,1152]{1,0:T(8,128)S(1)} %get-tuple-element.59.acc) | copy-start | bytes 3538948
  46.6 3.7 %copy-start.14 = (f32[32,8,128]{2,1,0:T(8,128)}, f32[32,8,128]{2,1,0:T(8,128)S(1)}, u32[]{:S(2)}) copy-start(f32[32,8,128]{2,1,0:T(8,128)S(1)} %get-tuple-element.64) | copy-start | bytes 393220
  48.9 14.9 %collective-permute-start.9 = (bf16[128,1152]{1,0:T(8,128)(2,1)}, bf16[128,1152]{1,0:T(8,128)(2,1)}, u32[]{:S(2)}, u32[]{:S(2)}) collective-permute-start(bf16[128,1152]{1,0:T(8,128)(2,1)} %slice.6), channel_id=1, source_target_pairs={{2,0},{4,6},{10,8},{12,14},{18,16},{20,22},{26,24},{28,30},{3,1},{... | collective-permute-start | bytes 884744 | tf_op jit(solution)/shard_map/ppermute | solution.py:188
  50.2 0.8 %copy-start.6 = (bf16[256,1152]{1,0:T(8,128)(2,1)}, bf16[256,1152]{1,0:T(8,128)(2,1)S(1)}, u32[]{:S(2)}) copy-start(bf16[256,1152]{1,0:T(8,128)(2,1)S(1)} %collective-permute-done.5.block) | copy-start | bytes 1769476
  51.0 16.0 %all-to-all-start = ((f32[32,8,128]{2,1,0:T(8,128)}), f32[32,8,128]{2,1,0:T(8,128)}, u32[]{:S(2)}, u32[]{:S(2)}) async-start(f32[32,8,128]{2,1,0:T(8,128)} %copy-done.14), calls=%async_computation | async-start | bytes 262144 | tf_op jit(solution)/shard_map/all_to_all | solution.py:239
  58.1 2.8 %copy-start.1 = (f32[256,1152]{1,0:T(8,128)S(1)}, f32[256,1152]{1,0:T(8,128)}, u32[]{:S(2)}) copy-start(f32[256,1152]{1,0:T(8,128)} %copy-done) | copy-start | bytes 3538948
  58.1 2.8 %copy-start.3 = (bf16[256,1152]{1,0:T(8,128)(2,1)S(1)}, bf16[256,1152]{1,0:T(8,128)(2,1)}, u32[]{:S(2)}) copy-start(bf16[256,1152]{1,0:T(8,128)(2,1)} %raw.2) | copy-start | bytes 1769476
  58.1 2.8 %copy-start.7 = (bf16[256,1152]{1,0:T(8,128)(2,1)S(1)}, bf16[256,1152]{1,0:T(8,128)(2,1)}, u32[]{:S(2)}) copy-start(bf16[256,1152]{1,0:T(8,128)(2,1)} %copy-done.6) | copy-start | bytes 1769476
  58.1 2.8 %copy-start.13 = (f32[256,128]{1,0:T(8,128)S(1)}, f32[256,128]{1,0:T(8,128)}, u32[]{:S(2)}) copy-start(f32[256,128]{1,0:T(8,128)} %copy-done.12) | copy-start | bytes 393220
  60.9 2.9 %copy-start.5 = (bf16[256,1152]{1,0:T(8,128)(2,1)S(1)}, bf16[256,1152]{1,0:T(8,128)(2,1)}, u32[]{:S(2)}) copy-start(bf16[256,1152]{1,0:T(8,128)(2,1)} %raw.3) | copy-start | bytes 1769476
  60.9 2.9 %copy-start.11 = (f32[256,128]{1,0:T(8,128)S(1)}, f32[256,128]{1,0:T(8,128)}, u32[]{:S(2)}) copy-start(f32[256,128]{1,0:T(8,128)} %copy-done.10) | copy-start | bytes 393220

commit v4 on v3

--- a/solution.py
+++ b/solution.py
@@ -87,10 +87,13 @@
     return grad, tally
 
 
-def finished(grad, raw, inverse):
-    inv = inverse[:, :1]
-    wide = widened(raw) * inv
-    return inv * (grad - wide * jnp.sum(wide * grad, axis=1, keepdims=True))
+def finish(out, grad, raw, inverse):
+    inv = inverse[...]
+    spans = [slice(c, c + 128) for c in range(0, raw.shape[1], 128)]
+    dot = sum(widened(raw.at[:, s]) * grad[:, s] for s in spans)
+    pull = jnp.sum(dot, axis=1, keepdims=True) * (inv * inv * inv)
+    for s in spans:
+        out[:, s] = inv * grad[:, s] - widened(raw.at[:, s]) * pull
 
 
 def text_pair_kernel(scalars, own, first, second, gx, stats, gx_out, stats_out, unit_out):
@@ -102,8 +105,7 @@
     stats_out[...] = stats[...] + tally_a + tally_b
 
 
-def image_pair_kernel(scalars, own, first, second, gy, gy_out, part, unit_out):
-    part[...] = second[: part.shape[0]]
+def image_pair_kernel(scalars, own, first, second, gy, gy_out, unit_out):
     unit = rounded_unit(widened(second))
     unit_out[...] = unit
     grad_a, _ = meet(scalars, own[...], rounded_unit(widened(first)))
@@ -123,30 +125,29 @@
     lane = lax.broadcasted_iota(jnp.int32, (8, 128), 1)
     sums = [jnp.sum(tally[8 * i : 8 * i + 8]) for i in range(3)]
     row = jnp.where(lane == 0, sums[0], jnp.where(lane == 1, sums[1], sums[2]))
-    sums_out[...] = jnp.broadcast_to(row[None], sums_out.shape)
-
-
-def image_far_kernel(scalars, own, far, upper, middle, gy, gy_out):
-    grad_a, _ = meet(scalars, own[...], rounded_unit(widened(far)))
-    block = jnp.where(scalars[2] > 0.5, widened(upper), widened(middle.at[: upper.shape[0]]))
-    grad_b, _ = meet(scalars, own[...], rounded_unit(block))
-    gy_out[...] = gy[...] + grad_a + grad_b
-
-
-def pick_kernel(scalars, outer, inner, out):
-    out[...] = jnp.where(scalars[2] > 0.5, widened(outer), widened(inner)).astype(out.dtype)
-
-
-def last_text_kernel(scalars, own, block, acc, raw, inverse, out):
-    grad, _ = meet(scalars, own[...], rounded_unit(widened(block)))
-    out[...] = finished(acc[...] + grad, raw, inverse)
-
-
-def last_image_kernel(scalars, own, lower, middle, acc, raw, inverse, out):
-    rest = widened(middle.at[middle.shape[0] - lower.shape[0] :])
-    block = jnp.where(scalars[2] > 0.5, widened(lower), rest)
-    grad, _ = meet(scalars, own[...], rounded_unit(block))
-    out[...] = finished(acc[...] + grad, raw, inverse)
+    sums_out[...] = jnp.broadcast_to((row * scalars[3])[None], sums_out.shape)
+
+
+def chosen(scalars, outer, inner):
+    return jnp.where(scalars[2] > 0.5, widened(outer), widened(inner)).astype(outer.dtype)
+
+
+def pick_kernel(scalars, outer, inner, whole, out, part):
+    out[...] = chosen(scalars, outer, inner)
+    part[...] = whole[: part.shape[0]]
+
+
+def pick_half_kernel(scalars, outer, inner, out):
+    half = out.shape[0]
+    out[...] = chosen(scalars, outer.at[half:], inner.at[half:])
+
+
+def last_kernel(scalars, own, *refs):
+    *pieces, acc, raw, inverse, out = refs
+    grad = acc[...]
+    for piece in pieces:
+        grad += meet(scalars, own[...], rounded_unit(widened(piece)))[0]
+    finish(out, grad, raw, inverse)
 
 
 def tied(*values):
@@ -180,9 +181,9 @@
     place = lax.axis_index("blk") % QUAD
     everyone = range(blocks)
     f32 = jnp.float32
-    scalars = jnp.stack(
-        [jnp.exp(log_temp[0]), bias[0], jnp.where((place == 0) | (place == 3), 1.0, 0.0).astype(f32)]
-    )
+    share = 1.0 / (rows * rows * (2 * REACH + 1) * devices)
+    outer = jnp.where((place == 0) | (place == 3), 1.0, 0.0).astype(f32)
+    scalars = jnp.stack([jnp.exp(log_temp[0]), bias[0], outer, jnp.full((), share, f32)])
 
     def send(block, route):
         return lax.ppermute(block, "blk", route)
@@ -190,10 +191,11 @@
     beside = [(b, b ^ 1) for b in everyone]
     above = [(b, b ^ 2) for b in everyone]
     beyond = [(b, (b + QUAD if b % QUAD < 2 else b - QUAD) % blocks) for b in everyone]
-    corner = [(b, b ^ 1) for b in everyone if b % QUAD in (1, 2)]
-    turn = [(b, (b + 2 if b % QUAD == 2 else b - 2) % blocks) for b in everyone if b % QUAD in (1, 2)]
-    middle = [(b, b ^ 1) for b in everyone if b % QUAD in (0, 3)]
-    mixed = [(b, b ^ (1 if b % QUAD in (1, 2) else 2)) for b in everyone]
+    def turned(b):
+        step = {0: 2, 1: -2, 2: 2, 3: -2}[b % QUAD]
+        return (b + step) % blocks
+
+    turn = [(b, turned(b)) for b in everyone]
 
     tile = jax.ShapeDtypeStruct((rows, width), f32)
     unit = jax.ShapeDtypeStruct((rows, width), jnp.bfloat16)
@@ -220,29 +222,24 @@
     )
     img_y, img_x, gx = tied(img_y, img_x, gx)
     img_z = send(img_y, beyond)
-    (txt_v,) = run(pick_kernel, 1, [txt_x, txt_z], unit)
-    txt_w = send(txt_v, mixed)
-    txt_v, gy, img_y = tied(txt_v, gy, img_y)
-    img_m = send(img_y, middle)
-    gy, img_h, unit_x = run(
-        image_pair_kernel, 2, [txt_unit, img_y, img_x, gy], tile, part, unit
-    )
-    img_t = send(img_h, turn)
+    txt_z, img_x, img_y = tied(txt_z, img_x, img_y)
+    txt_v, img_h = run(pick_kernel, 1, [txt_y, txt_z, img_x], unit, part)
+    txt_w = send(txt_v, beside)
+    img_k = send(img_h, turn)
+    txt_v, gy = tied(txt_v, gy)
+    gy, unit_x = run(image_pair_kernel, 2, [txt_unit, img_y, img_x, gy], tile, unit)
     gx, sums = run(
         text_far_kernel, 2, [img_unit, txt_z, unit_x, unit_y, gx, stats], tile, spread
     )
     img_z, gx, gy = tied(img_z, gx, gy)
-    img_c = send(img_z[half:], corner)
-    (gy,) = run(image_far_kernel, 2, [txt_unit, img_z, img_t, img_m, gy], tile)
-    img_m, gx, gy = tied(img_m, gx, gy)
+    (img_v,) = run(pick_half_kernel, 1, [img_y, img_z], part)
+    img_w = send(img_v, beside)
     sums, txt_w = tied(sums, txt_w)
     seen = lax.all_to_all(sums, ("blk", "grp"), 0, 0)
-    pairs = jnp.float32(rows * rows * (2 * REACH + 1) * devices)
-    statistics = jnp.sum(seen[:, 0, :3], axis=0) / pairs
-    (grad_image,) = run(last_text_kernel, 1, [img_unit, txt_w, gx, image, img_inv], tile)
-    (grad_text,) = run(
-        last_image_kernel, 1, [txt_unit, img_c, img_m, gy, text, txt_inv], tile
-    )
+    statistics = jnp.sum(seen[:, 0, :3], axis=0)
+    (grad_image,) = run(last_kernel, 1, [img_unit, txt_w, gx, image, img_inv], tile)
+    gy, grad_image = tied(gy, grad_image)
+    (grad_text,) = run(last_kernel, 1, [txt_unit, img_z, img_k, img_w, gy, text, txt_inv], tile)
     return grad_image, grad_text, statistics
 
 

time: 69 us -> 65.3 us (0.946)
  starting transfers between devices: 22.4 us -> 16.9 us
  local copies, waits for them, and re-layouts: 5.56 us -> 7.63 us
  waiting for transfers between devices: 16.2 us -> 17.8 us
  other arithmetic: 1.55 us -> 0.64 us
  Pallas kernels: 20.6 us -> 19.7 us
    ppermute x10 -> x9, starting transfers between devices: 15.4 us -> 11.8 us  [send(): return lax.ppermute(block, 'blk', route)]
    unnamed x30 -> x28, local copies, waits for them, and re-layouts: 4.81 us -> 7.63 us
    all_to_all x1, starting transfers between devices: 7.03 us -> 5.08 us  [on_device(): seen = lax.all_to_all(sums, ('blk', 'grp'), 0, 0)]
    ppermute x10 -> x9, waiting for transfers between devices: 16.2 us -> 17.8 us  [send(): return lax.ppermute(block, 'blk', route)]
    pallas_call x8, Pallas kernels: 20.6 us -> 19.7 us  [call(): pl.pallas_call(kernel, out_shape=shapes, in_specs=[IN_SMEM] + [IN_VMEM] *...]
    slice x1 -> x0, local copies, waits for them, and re-layouts: 0.75 us -> none  [on_device(): img_c = send(img_z[half:], corner)]
  transfers between devices with their start and end apart: 11 -> 10, of which waited for: 4 -> 6; matrix products, arithmetic and copies ran while one was open for 1% -> 0% of each run, Pallas kernels for 30% -> 30%
where the time goes in v4:
time: 65.3 us; the launch traced here: 64.8 us
  Pallas kernels  19.7 us (30%)
  waiting for transfers between devices  17.8 us (27%)
  starting transfers between devices  16.9 us (26%)
  local copies, waits for them, and re-layouts  7.63 us (12%)
  between operations  2.1 us (3%)
    pallas_call x8, Pallas kernels, call(): pl.pallas_call(kernel, out_shape=shapes, in_specs=[IN_SMEM] + [IN_VMEM] *...  19.7 us
    ppermute x9, waiting for transfers between devices, send(): return lax.ppermute(block, 'blk', route)  17.8 us
    ppermute x9, starting transfers between devices, send(): return lax.ppermute(block, 'blk', route)  11.8 us
    unnamed x28, local copies, waits for them, and re-layouts  7.63 us
    all_to_all x1, starting transfers between devices, on_device(): seen = lax.all_to_all(sums, ('blk', 'grp'), 0, 0)  5.08 us
  transfers between devices with their start and end apart: 10, of which 6 were waited for; matrix products, arithmetic and copies ran while one was open for 0% of the time, Pallas kernels for 30%

profile of v4, /device:TPU:0, one launch (start us, length us, event | category | flops | bytes accessed | tf_op | source)
XLA Modules:
  0.0 64.8 jit_solution(15727686712606606114)
XLA Ops:
  0.6 3.0 %collective-permute-start.2 = (bf16[256,1152]{1,0:T(8,128)(2,1)}, bf16[256,1152]{1,0:T(8,128)(2,1)S(1)}, u32[]{:S(2)}, u32[]{:S(2)}) collective-permute-start(bf16[256,1152]{1,0:T(8,128)(2,1)} %refs_4_.1), channel_id=1, source_target_pairs={{0,4},{2,6},{4,0},{6,2},{8,12},{10,14},{12,8},{14,10},{16,20},{18,... | collective-permute-start | bytes 1769480 | tf_op jit(solution)/shard_map/ppermute | solution.py:189
  3.7 1.5 %collective-permute-start.3 = (bf16[256,1152]{1,0:T(8,128)(2,1)}, bf16[256,1152]{1,0:T(8,128)(2,1)}, u32[]{:S(2)}, u32[]{:S(2)}) collective-permute-start(bf16[256,1152]{1,0:T(8,128)(2,1)} %refs_4_.1), channel_id=1, source_target_pairs={{0,2},{2,0},{4,6},{6,4},{8,10},{10,8},{12,14},{14,12},{16,18},{18,... | collective-permute-start | bytes 1769480 | tf_op jit(solution)/shard_map/ppermute | solution.py:189
  5.2 0.5 collective-permute-start
  5.7 0.1 collective-permute-start.1
  7.1 0.1 pad_maximum_fusion.scalars
  7.2 0.0 copy-start.4
  7.2 1.1 %copy-done.4 = bf16[256,1152]{1,0:T(8,128)(2,1)S(1)} copy-done((bf16[256,1152]{1,0:T(8,128)(2,1)S(1)}, bf16[256,1152]{1,0:T(8,128)(2,1)}, u32[]{:S(2)}) %copy-start.4) | copy-done | bytes 589848
  8.3 1.1 %copy-done.6 = bf16[256,1152]{1,0:T(8,128)(2,1)S(1)} copy-done((bf16[256,1152]{1,0:T(8,128)(2,1)S(1)}, bf16[256,1152]{1,0:T(8,128)(2,1)}, u32[]{:S(2)}) %copy-start.6) | copy-done | bytes 589848
  9.3 2.8 %shard_map.67 = (bf16[256,1152]{1,0:T(8,128)(2,1)S(1)}, bf16[256,1152]{1,0:T(8,128)(2,1)S(1)}, f32[256,128]{1,0:T(8,128)S(1)}, f32[256,128]{1,0:T(8,128)S(1)}, f...) custom-call(f32[4]{0:T(128)S(1)} %pad_maximum_fusion.scalars, ...), custom_call_target="tpu_custom_call" | custom-call | flops 603979776 | bytes 7077888 | tf_op jit(solution)/shard_map/pallas_call | solution.py:166
  12.1 0.0 copy-start.10
  12.1 0.6 copy-done.10
  12.7 0.6 %copy-done.12 = f32[256,128]{1,0:T(8,128)} copy-done((f32[256,128]{1,0:T(8,128)}, f32[256,128]{1,0:T(8,128)S(1)}, u32[]{:S(2)}) %copy-start.12) | copy-done | bytes 131096
  13.4 4.6 %collective-permute-done.2.first.outer = bf16[256,1152]{1,0:T(8,128)(2,1)S(1)} collective-permute-done((bf16[256,1152]{1,0:T(8,128)(2,1)}, bf16[256,1152]{1,0:T(8,128)(2,1)S(1)}, u32[]{:S(2)}, u32[]{:S(2)}) %collective-permute-start.2) | collective-permute-done | bytes 589856 | tf_op jit(solution)/shard_map/ppermute | solution.py:189
  18.0 2.1 %collective-permute-start.5 = (bf16[256,1152]{1,0:T(8,128)(2,1)S(1)}, bf16[256,1152]{1,0:T(8,128)(2,1)S(1)}, u32[]{:S(2)}, u32[]{:S(2)}) collective-permute-start(bf16[256,1152]{1,0:T(8,128)(2,1)S(1)} %collective-permute-done.2.first.outer), channel_id=1, source_target_pairs={{0,8},{2,10},{4,28},{6,30},{8,16},{10,18},{12,4},{14,6},{16,24},{1... | collective-permute-start | bytes 1769480 | tf_op jit(solution)/shard_map/ppermute | solution.py:189
  20.1 0.1 collective-permute-done.3.second
  20.2 3.0 %shard_map.68 = (f32[256,1152]{1,0:T(8,128)S(1)}, f32[24,128]{1,0:T(8,128)S(1)}, bf16[256,1152]{1,0:T(8,128)(2,1)S(1)}) custom-call(f32[4]{0:T(128)S(1)} %pad_maximum_fusion.scalars, bf16[256,1152]{1,0:T(8,128)(2,1)S(1)} %get-tuple-element.36.own, bf16[256,1152]{1,0:T(8,128)(2,1)S(1)} %collective-permute-done.2.first.outer, ...), custom_call_target="tpu_custom_call" | custom-call | flops 603979776 | bytes 7077888 | tf_op jit(solution)/shard_map/pallas_call | solution.py:166
  23.3 6.6 %collective-permute-done.first.outer = bf16[256,1152]{1,0:T(8,128)(2,1)S(1)} collective-permute-done((bf16[256,1152]{1,0:T(8,128)(2,1)}, bf16[256,1152]{1,0:T(8,128)(2,1)S(1)}, u32[]{:S(2)}, u32[]{:S(2)}) %collective-permute-start) | collective-permute-done | bytes 589856 | tf_op jit(solution)/shard_map/ppermute | solution.py:189
  29.8 1.5 %collective-permute-done.1.whole.second = bf16[256,1152]{1,0:T(8,128)(2,1)S(1)} collective-permute-done((bf16[256,1152]{1,0:T(8,128)(2,1)}, bf16[256,1152]{1,0:T(8,128)(2,1)S(1)}, u32[]{:S(2)}, u32[]{:S(2)}) %collective-permute-start.1) | collective-permute-done | bytes 589856 | tf_op jit(solution)/shard_map/ppermute | solution.py:189
  31.3 1.6 %collective-permute-start.4 = (bf16[256,1152]{1,0:T(8,128)(2,1)S(1)}, bf16[256,1152]{1,0:T(8,128)(2,1)S(1)}, u32[]{:S(2)}, u32[]{:S(2)}) collective-permute-start(bf16[256,1152]{1,0:T(8,128)(2,1)S(1)} %collective-permute-done.first.outer), channel_id=1, source_target_pairs={{0,8},{2,10},{4,28},{6,30},{8,16},{10,18},{12,4},{14,6},{16,24},{1... | collective-permute-start | bytes 1769480 | tf_op jit(solution)/shard_map/ppermute | solution.py:189
  32.9 0.7 %collective-permute-done.5.inner.far = bf16[256,1152]{1,0:T(8,128)(2,1)S(1)} collective-permute-done((bf16[256,1152]{1,0:T(8,128)(2,1)S(1)}, bf16[256,1152]{1,0:T(8,128)(2,1)S(1)}, u32[]{:S(2)}, u32[]{:S(2)}) %collective-permute-start.5) | collective-permute-done | bytes 589856 | tf_op jit(solution)/shard_map/ppermute | solution.py:189
  33.6 1.3 %shard_map.69 = (bf16[256,1152]{1,0:T(8,128)(2,1)S(1)}, bf16[128,1152]{1,0:T(8,128)(2,1)}) custom-call(f32[4]{0:T(128)S(1)} %pad_maximum_fusion.scalars, bf16[256,1152]{1,0:T(8,128)(2,1)S(1)} %collective-permute-done.2.first.outer, bf16[256,1152]{1,0:T(8,128)(2,1)S(1)} %collective-permute-done.5.inner.far, ...), custom_call_target="tpu_custom_call" | custom-call | flops 301989888 | bytes 3538944 | tf_op jit(solution)/shard_map/pallas_call | solution.py:166
  35.0 1.5 %collective-permute-start.6 = (bf16[256,1152]{1,0:T(8,128)(2,1)S(1)}, bf16[256,1152]{1,0:T(8,128)(2,1)S(1)}, u32[]{:S(2)}, u32[]{:S(2)}) collective-permute-start(bf16[256,1152]{1,0:T(8,128)(2,1)S(1)} %get-tuple-element.49), channel_id=1, source_target_pairs={{0,2},{2,0},{4,6},{6,4},{8,10},{10,8},{12,14},{14,12},{16,18},{18,... | collective-permute-start | bytes 1769480 | tf_op jit(solution)/shard_map/ppermute | solution.py:189
  36.4 2.3 %shard_map.70 = (f32[256,1152]{1,0:T(8,128)S(1)}, bf16[256,1152]{1,0:T(8,128)(2,1)S(1)}) custom-call(f32[4]{0:T(128)S(1)} %pad_maximum_fusion.scalars, bf16[256,1152]{1,0:T(8,128)(2,1)S(1)} %get-tuple-element.46.own, bf16[256,1152]{1,0:T(8,128)(2,1)S(1)} %collective-permute-done.first.outer, bf16[256,1152]{1,0:T(8,128)(2,1)S(1)} %collective-permute-done.1.whole.second, ...), custom_call_target="tpu_custom_call" | custom-call | flops 603979776 | bytes 7077888 | tf_op jit(solution)/shard_map/pallas_call | solution.py:166
  38.7 0.0 copy-start
  38.7 1.0 %copy-done = f32[256,1152]{1,0:T(8,128)} copy-done((f32[256,1152]{1,0:T(8,128)}, f32[256,1152]{1,0:T(8,128)S(1)}, u32[]{:S(2)}) %copy-start) | copy-done | bytes 1179672
  39.8 2.9 %shard_map.71 = (f32[256,1152]{1,0:T(8,128)S(1)}, f32[32,8,128]{2,1,0:T(8,128)}) custom-call(f32[4]{0:T(128)S(1)} %pad_maximum_fusion.scalars, bf16[256,1152]{1,0:T(8,128)(2,1)S(1)} %get-tuple-element.36.own, bf16[256,1152]{1,0:T(8,128)(2,1)S(1)} %collective-permute-done.5.inner.far, bf16[256,1152]{1,0:T(8,128)(2,1)S(1)} %get-tuple-element.52.near_image, ...), custom_call_target="tpu_custom_call" | custom-call | flops 603979776 | bytes 7077888 | tf_op jit(solution)/shard_map/pallas_call | solution.py:166
  42.7 4.3 %collective-permute-done.4.inner.refs_0_ = bf16[256,1152]{1,0:T(8,128)(2,1)S(1)} collective-permute-done((bf16[256,1152]{1,0:T(8,128)(2,1)S(1)}, bf16[256,1152]{1,0:T(8,128)(2,1)S(1)}, u32[]{:S(2)}, u32[]{:S(2)}) %collective-permute-start.4) | collective-permute-done | bytes 589856 | tf_op jit(solution)/shard_map/ppermute | solution.py:189
  47.0 0.6 shard_map.73
  47.7 0.0 copy-done.2
  47.7 1.6 %collective-permute-start.8 = (bf16[128,1152]{1,0:T(8,128)(2,1)S(1)}, bf16[128,1152]{1,0:T(8,128)(2,1)S(1)}, u32[]{:S(2)}, u32[]{:S(2)}) collective-permute-start(bf16[128,1152]{1,0:T(8,128)(2,1)S(1)} %shard_map.73), channel_id=1, source_target_pairs={{0,2},{2,0},{4,6},{6,4},{8,10},{10,8},{12,14},{14,12},{16,18},{18,... | collective-permute-start | bytes 884744 | tf_op jit(solution)/shard_map/ppermute | solution.py:189
  49.2 0.0 collective-permute-start.7
  49.2 0.0 collective-permute-done.6.refs_0_
  49.2 0.8 %copy-done.8 = bf16[256,1152]{1,0:T(8,128)(2,1)} copy-done((bf16[256,1152]{1,0:T(8,128)(2,1)}, bf16[256,1152]{1,0:T(8,128)(2,1)S(1)}, u32[]{:S(2)}) %copy-start.8) | copy-done | bytes 589848
  50.0 5.1 %all-to-all-start = ((f32[32,8,128]{2,1,0:T(8,128)}), f32[32,8,128]{2,1,0:T(8,128)S(1)}, u32[]{:S(2)}, u32[]{:S(2)}) async-start(f32[32,8,128]{2,1,0:T(8,128)} %get-tuple-element.68), calls=%async_computation | async-start | bytes 262144 | tf_op jit(solution)/shard_map/all_to_all | solution.py:238
  55.1 0.0 copy-done.5
  55.1 0.0 copy-done.13
  55.2 0.0 copy-start.3
  55.2 1.3 %copy-done.3 = f32[256,1152]{1,0:T(8,128)S(1)} copy-done((f32[256,1152]{1,0:T(8,128)S(1)}, f32[256,1152]{1,0:T(8,128)}, u32[]{:S(2)}) %copy-start.3) | copy-done | bytes 1179672
  56.4 1.1 %copy-done.9 = bf16[256,1152]{1,0:T(8,128)(2,1)S(1)} copy-done((bf16[256,1152]{1,0:T(8,128)(2,1)S(1)}, bf16[256,1152]{1,0:T(8,128)(2,1)}, u32[]{:S(2)}) %copy-start.9) | copy-done | bytes 589848
  57.5 2.8 %shard_map.72 = f32[256,1152]{1,0:T(8,128)} custom-call(f32[4]{0:T(128)S(1)} %pad_maximum_fusion.scalars, bf16[256,1152]{1,0:T(8,128)(2,1)S(1)} %get-tuple-element.36.own, bf16[256,1152]{1,0:T(8,128)(2,1)S(1)} %copy-done.9, f32[256,1152]{1,0:T(8,128)S(1)} %copy-done.3, bf16[256,1152]{1,0:T(8,128)(2,1)S(1)} %copy-done.5, f32[256,128]{1,0:T(8,128)S(1)} %copy-done.13), custom_call_target="tpu_custom_call" | custom-call | flops 301989888 | bytes 3538944 | tf_op jit(solution)/shard_map/pallas_call | solution.py:166
  60.3 0.0 collective-permute-done.8.refs_2_
  60.3 0.0 collective-permute-done.7.refs_1_
  60.3 0.0 copy-done.1
  60.4 0.0 copy-done.7
  60.4 0.0 copy-done.11
  60.4 3.9 %shard_map.74 = f32[256,1152]{1,0:T(8,128)} custom-call(f32[4]{0:T(128)S(1)} %pad_maximum_fusion.scalars, bf16[256,1152]{1,0:T(8,128)(2,1)S(1)} %get-tuple-element.46.own, bf16[256,1152]{1,0:T(8,128)(2,1)S(1)} %collective-permute-done.4.inner.refs_0_, bf16[128,1152]{1,0:T(8,128)(2,1)S(1)} %collective-permute-done.7.refs_1_, ...), custom_call_target="tpu_custom_call" | custom-call | flops 301989888 | bytes 3538944 | tf_op jit(solution)/shard_map/pallas_call | solution.py:166
  64.3 0.0 all-to-all-done
  64.3 0.6 slice_reduce_fusion
  (10 shorter events, 0.0 us)
Async XLA Ops:
  0.6 17.4 %collective-permute-start.2 = (bf16[256,1152]{1,0:T(8,128)(2,1)}, bf16[256,1152]{1,0:T(8,128)(2,1)S(1)}, u32[]{:S(2)}, u32[]{:S(2)}) collective-permute-start(bf16[256,1152]{1,0:T(8,128)(2,1)} %refs_4_.1), channel_id=1, source_target_pairs={{0,4},{2,6},{4,0},{6,2},{8,12},{10,14},{12,8},{14,10},{16,20},{18,... | collective-permute-start | bytes 1769480 | tf_op jit(solution)/shard_map/ppermute | solution.py:189
  3.7 16.6 %collective-permute-start.3 = (bf16[256,1152]{1,0:T(8,128)(2,1)}, bf16[256,1152]{1,0:T(8,128)(2,1)}, u32[]{:S(2)}, u32[]{:S(2)}) collective-permute-start(bf16[256,1152]{1,0:T(8,128)(2,1)} %refs_4_.1), channel_id=1, source_target_pairs={{0,2},{2,0},{4,6},{6,4},{8,10},{10,8},{12,14},{14,12},{16,18},{18,... | collective-permute-start | bytes 1769480 | tf_op jit(solution)/shard_map/ppermute | solution.py:189
  5.2 24.7 %collective-permute-start = (bf16[256,1152]{1,0:T(8,128)(2,1)}, bf16[256,1152]{1,0:T(8,128)(2,1)S(1)}, u32[]{:S(2)}, u32[]{:S(2)}) collective-permute-start(bf16[256,1152]{1,0:T(8,128)(2,1)} %refs_2_.1), channel_id=1, source_target_pairs={{0,4},{2,6},{4,0},{6,2},{8,12},{10,14},{12,8},{14,10},{16,20},{18,... | collective-permute-start | bytes 1769480 | tf_op jit(solution)/shard_map/ppermute | solution.py:189
  5.7 25.6 %collective-permute-start.1 = (bf16[256,1152]{1,0:T(8,128)(2,1)}, bf16[256,1152]{1,0:T(8,128)(2,1)S(1)}, u32[]{:S(2)}, u32[]{:S(2)}) collective-permute-start(bf16[256,1152]{1,0:T(8,128)(2,1)} %refs_2_.1), channel_id=1, source_target_pairs={{0,2},{2,0},{4,6},{6,4},{8,10},{10,8},{12,14},{14,12},{16,18},{18,... | collective-permute-start | bytes 1769480 | tf_op jit(solution)/shard_map/ppermute | solution.py:189
  7.2 1.1 %copy-start.4 = (bf16[256,1152]{1,0:T(8,128)(2,1)S(1)}, bf16[256,1152]{1,0:T(8,128)(2,1)}, u32[]{:S(2)}) copy-start(bf16[256,1152]{1,0:T(8,128)(2,1)} %refs_2_.1) | copy-start | bytes 1769476
  8.3 1.1 %copy-start.6 = (bf16[256,1152]{1,0:T(8,128)(2,1)S(1)}, bf16[256,1152]{1,0:T(8,128)(2,1)}, u32[]{:S(2)}) copy-start(bf16[256,1152]{1,0:T(8,128)(2,1)} %refs_4_.1) | copy-start | bytes 1769476
  12.1 0.7 %copy-start.10 = (f32[256,128]{1,0:T(8,128)}, f32[256,128]{1,0:T(8,128)S(1)}, u32[]{:S(2)}) copy-start(f32[256,128]{1,0:T(8,128)S(1)} %get-tuple-element.67.refs_5_) | copy-start | bytes 393220
  12.7 0.7 %copy-start.12 = (f32[256,128]{1,0:T(8,128)}, f32[256,128]{1,0:T(8,128)S(1)}, u32[]{:S(2)}) copy-start(f32[256,128]{1,0:T(8,128)S(1)} %get-tuple-element.62.refs_3_) | copy-start | bytes 393220
  18.0 15.6 %collective-permute-start.5 = (bf16[256,1152]{1,0:T(8,128)(2,1)S(1)}, bf16[256,1152]{1,0:T(8,128)(2,1)S(1)}, u32[]{:S(2)}, u32[]{:S(2)}) collective-permute-start(bf16[256,1152]{1,0:T(8,128)(2,1)S(1)} %collective-permute-done.2.first.outer), channel_id=1, source_target_pairs={{0,8},{2,10},{4,28},{6,30},{8,16},{10,18},{12,4},{14,6},{16,24},{1... | collective-permute-start | bytes 1769480 | tf_op jit(solution)/shard_map/ppermute | solution.py:189
  31.3 15.7 %collective-permute-start.4 = (bf16[256,1152]{1,0:T(8,128)(2,1)S(1)}, bf16[256,1152]{1,0:T(8,128)(2,1)S(1)}, u32[]{:S(2)}, u32[]{:S(2)}) collective-permute-start(bf16[256,1152]{1,0:T(8,128)(2,1)S(1)} %collective-permute-done.first.outer), channel_id=1, source_target_pairs={{0,8},{2,10},{4,28},{6,30},{8,16},{10,18},{12,4},{14,6},{16,24},{1... | collective-permute-start | bytes 1769480 | tf_op jit(solution)/shard_map/ppermute | solution.py:189
  35.0 14.3 %collective-permute-start.6 = (bf16[256,1152]{1,0:T(8,128)(2,1)S(1)}, bf16[256,1152]{1,0:T(8,128)(2,1)S(1)}, u32[]{:S(2)}, u32[]{:S(2)}) collective-permute-start(bf16[256,1152]{1,0:T(8,128)(2,1)S(1)} %get-tuple-element.49), channel_id=1, source_target_pairs={{0,2},{2,0},{4,6},{6,4},{8,10},{10,8},{12,14},{14,12},{16,18},{18,... | collective-permute-start | bytes 1769480 | tf_op jit(solution)/shard_map/ppermute | solution.py:189
  38.7 1.0 %copy-start = (f32[256,1152]{1,0:T(8,128)}, f32[256,1152]{1,0:T(8,128)S(1)}, u32[]{:S(2)}) copy-start(f32[256,1152]{1,0:T(8,128)S(1)} %get-tuple-element.66.refs_3_) | copy-start | bytes 3538948
  42.7 5.0 %copy-start.2 = (f32[256,1152]{1,0:T(8,128)}, f32[256,1152]{1,0:T(8,128)S(1)}, u32[]{:S(2)}) copy-start(f32[256,1152]{1,0:T(8,128)S(1)} %get-tuple-element.61.refs_1_) | copy-start | bytes 3538948
  42.7 12.4 %copy-start.5 = (bf16[256,1152]{1,0:T(8,128)(2,1)S(1)}, bf16[256,1152]{1,0:T(8,128)(2,1)}, u32[]{:S(2)}) copy-start(bf16[256,1152]{1,0:T(8,128)(2,1)} %refs_2_.1) | copy-start | bytes 1769476
  42.7 12.4 %copy-start.13 = (f32[256,128]{1,0:T(8,128)S(1)}, f32[256,128]{1,0:T(8,128)}, u32[]{:S(2)}) copy-start(f32[256,128]{1,0:T(8,128)} %copy-done.12) | copy-start | bytes 393220
  47.7 12.7 %collective-permute-start.8 = (bf16[128,1152]{1,0:T(8,128)(2,1)S(1)}, bf16[128,1152]{1,0:T(8,128)(2,1)S(1)}, u32[]{:S(2)}, u32[]{:S(2)}) collective-permute-start(bf16[128,1152]{1,0:T(8,128)(2,1)S(1)} %shard_map.73), channel_id=1, source_target_pairs={{0,2},{2,0},{4,6},{6,4},{8,10},{10,8},{12,14},{14,12},{16,18},{18,... | collective-permute-start | bytes 884744 | tf_op jit(solution)/shard_map/ppermute | solution.py:189
  49.2 11.1 %collective-permute-start.7 = (bf16[128,1152]{1,0:T(8,128)(2,1)}, bf16[128,1152]{1,0:T(8,128)(2,1)S(1)}, u32[]{:S(2)}, u32[]{:S(2)}) collective-permute-start(bf16[128,1152]{1,0:T(8,128)(2,1)} %get-tuple-element.65), channel_id=1, source_target_pairs={{0,4},{2,30},{4,8},{6,2},{8,12},{10,6},{12,16},{14,10},{16,20},{18... | collective-permute-start | bytes 884744 | tf_op jit(solution)/shard_map/ppermute | solution.py:189
  49.2 0.8 %copy-start.8 = (bf16[256,1152]{1,0:T(8,128)(2,1)}, bf16[256,1152]{1,0:T(8,128)(2,1)S(1)}, u32[]{:S(2)}) copy-start(bf16[256,1152]{1,0:T(8,128)(2,1)S(1)} %collective-permute-done.6.refs_0_) | copy-start | bytes 1769476
  50.0 14.2 %all-to-all-start = ((f32[32,8,128]{2,1,0:T(8,128)}), f32[32,8,128]{2,1,0:T(8,128)S(1)}, u32[]{:S(2)}, u32[]{:S(2)}) async-start(f32[32,8,128]{2,1,0:T(8,128)} %get-tuple-element.68), calls=%async_computation | async-start | bytes 262144 | tf_op jit(solution)/shard_map/all_to_all | solution.py:238
  55.2 1.3 %copy-start.3 = (f32[256,1152]{1,0:T(8,128)S(1)}, f32[256,1152]{1,0:T(8,128)}, u32[]{:S(2)}) copy-start(f32[256,1152]{1,0:T(8,128)} %copy-done.2) | copy-start | bytes 3538948
  56.4 1.1 %copy-start.9 = (bf16[256,1152]{1,0:T(8,128)(2,1)S(1)}, bf16[256,1152]{1,0:T(8,128)(2,1)}, u32[]{:S(2)}) copy-start(bf16[256,1152]{1,0:T(8,128)(2,1)} %copy-done.8) | copy-start | bytes 1769476
  57.5 2.9 %copy-start.1 = (f32[256,1152]{1,0:T(8,128)S(1)}, f32[256,1152]{1,0:T(8,128)}, u32[]{:S(2)}) copy-start(f32[256,1152]{1,0:T(8,128)} %copy-done) | copy-start | bytes 3538948
  57.5 2.9 %copy-start.7 = (bf16[256,1152]{1,0:T(8,128)(2,1)S(1)}, bf16[256,1152]{1,0:T(8,128)(2,1)}, u32[]{:S(2)}) copy-start(bf16[256,1152]{1,0:T(8,128)(2,1)} %refs_4_.1) | copy-start | bytes 1769476
  57.5 2.9 %copy-start.11 = (f32[256,128]{1,0:T(8,128)S(1)}, f32[256,128]{1,0:T(8,128)}, u32[]{:S(2)}) copy-start(f32[256,128]{1,0:T(8,128)} %copy-done.10) | copy-start | bytes 393220

commit v5 on v4

--- a/solution.py
+++ b/solution.py
@@ -128,6 +128,10 @@
     sums_out[...] = jnp.broadcast_to((row * scalars[3])[None], sums_out.shape)
 
 
+def image_far_kernel(scalars, own, far, out):
+    out[...] = meet(scalars, own[...], rounded_unit(widened(far)))[0]
+
+
 def chosen(scalars, outer, inner):
     return jnp.where(scalars[2] > 0.5, widened(outer), widened(inner)).astype(outer.dtype)
 
@@ -142,9 +146,9 @@
     out[...] = chosen(scalars, outer.at[half:], inner.at[half:])
 
 
-def last_kernel(scalars, own, *refs):
-    *pieces, acc, raw, inverse, out = refs
-    grad = acc[...]
+def last_kernel(count, scalars, own, *refs):
+    pieces, (*sums, raw, inverse, out) = refs[:count], refs[count:]
+    grad = sum(held[...] for held in sums)
     for piece in pieces:
         grad += meet(scalars, own[...], rounded_unit(widened(piece)))[0]
     finish(out, grad, raw, inverse)
@@ -237,9 +241,18 @@
     sums, txt_w = tied(sums, txt_w)
     seen = lax.all_to_all(sums, ("blk", "grp"), 0, 0)
     statistics = jnp.sum(seen[:, 0, :3], axis=0)
-    (grad_image,) = run(last_kernel, 1, [img_unit, txt_w, gx, image, img_inv], tile)
+    (far,) = run(image_far_kernel, 1, [txt_unit, img_z], tile)
+    far, gx = tied(far, gx)
+    (grad_image,) = run(
+        functools.partial(last_kernel, 1), 1, [img_unit, txt_w, gx, image, img_inv], tile
+    )
     gy, grad_image = tied(gy, grad_image)
-    (grad_text,) = run(last_kernel, 1, [txt_unit, img_z, img_k, img_w, gy, text, txt_inv], tile)
+    (grad_text,) = run(
+        functools.partial(last_kernel, 2),
+        1,
+        [txt_unit, img_k, img_w, gy, far, text, txt_inv],
+        tile,
+    )
     return grad_image, grad_text, statistics
 
 

time: 65.3 us -> 63.4 us (0.971)
  local copies, waits for them, and re-layouts: 7.63 us -> 3.21 us
  waiting for transfers between devices: 17.8 us -> 20.1 us
    unnamed x28 -> x24, local copies, waits for them, and re-layouts: 7.63 us -> 3.21 us
    ppermute x9, waiting for transfers between devices: 17.8 us -> 19.9 us  [send(): return lax.ppermute(block, 'blk', route)]
    pallas_call x8 -> x9, Pallas kernels: 19.7 us -> 20.1 us  [call(): pl.pallas_call(kernel, out_shape=shapes, in_specs=[IN_SMEM] + [IN_VMEM] *...]
  transfers between devices with their start and end apart: 10 -> 10, of which waited for: 6 -> 7; matrix products, arithmetic and copies ran while one was open for 0% -> 0% of each run, Pallas kernels for 30% -> 32%
where the time goes in v5:
time: 63.4 us; the launch traced here: 63.1 us
  Pallas kernels  20.1 us (32%)
  waiting for transfers between devices  20.1 us (32%)
  starting transfers between devices  16.9 us (27%)
  local copies, waits for them, and re-layouts  3.21 us (5%)
  between operations  2.15 us (3%)
  other arithmetic  0.64 us (1%)
    pallas_call x9, Pallas kernels, call(): pl.pallas_call(kernel, out_shape=shapes, in_specs=[IN_SMEM] + [IN_VMEM] *...  20.1 us
    ppermute x9, waiting for transfers between devices, send(): return lax.ppermute(block, 'blk', route)  19.9 us
    ppermute x9, starting transfers between devices, send(): return lax.ppermute(block, 'blk', route)  11.8 us
    all_to_all x1, starting transfers between devices, on_device(): seen = lax.all_to_all(sums, ('blk', 'grp'), 0, 0)  5.09 us
    unnamed x24, local copies, waits for them, and re-layouts  3.21 us
  transfers between devices with their start and end apart: 10, of which 7 were waited for; matrix products, arithmetic and copies ran while one was open for 0% of the time, Pallas kernels for 32%

profile of v5, /device:TPU:0, one launch (start us, length us, event | category | flops | bytes accessed | tf_op | source)
XLA Modules:
  0.0 63.1 jit_solution(16063509352056539985)
XLA Ops:
  0.6 3.0 %collective-permute-start.2 = (bf16[256,1152]{1,0:T(8,128)(2,1)}, bf16[256,1152]{1,0:T(8,128)(2,1)S(1)}, u32[]{:S(2)}, u32[]{:S(2)}) collective-permute-start(bf16[256,1152]{1,0:T(8,128)(2,1)} %refs_4_.1), channel_id=1, source_target_pairs={{0,4},{2,6},{4,0},{6,2},{8,12},{10,14},{12,8},{14,10},{16,20},{18,... | collective-permute-start | bytes 1769480 | tf_op jit(solution)/shard_map/ppermute | solution.py:193
  3.7 1.5 %collective-permute-start.3 = (bf16[256,1152]{1,0:T(8,128)(2,1)}, bf16[256,1152]{1,0:T(8,128)(2,1)S(1)}, u32[]{:S(2)}, u32[]{:S(2)}) collective-permute-start(bf16[256,1152]{1,0:T(8,128)(2,1)} %refs_4_.1), channel_id=1, source_target_pairs={{0,2},{2,0},{4,6},{6,4},{8,10},{10,8},{12,14},{14,12},{16,18},{18,... | collective-permute-start | bytes 1769480 | tf_op jit(solution)/shard_map/ppermute | solution.py:193
  5.2 0.5 collective-permute-start
  5.7 0.1 collective-permute-start.1
  7.1 0.1 pad_maximum_fusion.scalars
  7.2 1.1 %copy-done.4 = bf16[256,1152]{1,0:T(8,128)(2,1)S(1)} copy-done((bf16[256,1152]{1,0:T(8,128)(2,1)S(1)}, bf16[256,1152]{1,0:T(8,128)(2,1)}, u32[]{:S(2)}) %copy-start.4) | copy-done | bytes 589848
  8.3 1.1 %copy-done.6 = bf16[256,1152]{1,0:T(8,128)(2,1)S(1)} copy-done((bf16[256,1152]{1,0:T(8,128)(2,1)S(1)}, bf16[256,1152]{1,0:T(8,128)(2,1)}, u32[]{:S(2)}) %copy-start.6) | copy-done | bytes 589848
  9.3 2.7 %shard_map.67 = (bf16[256,1152]{1,0:T(8,128)(2,1)S(1)}, bf16[256,1152]{1,0:T(8,128)(2,1)S(1)}, f32[256,128]{1,0:T(8,128)S(1)}, f32[256,128]{1,0:T(8,128)S(1)}, f...) custom-call(f32[4]{0:T(128)S(1)} %pad_maximum_fusion.scalars, ...), custom_call_target="tpu_custom_call" | custom-call | flops 603979776 | bytes 7077888 | tf_op jit(solution)/shard_map/pallas_call | solution.py:170
  12.1 0.0 copy-start.8
  12.1 0.0 copy-start.10
  12.1 5.9 %collective-permute-done.2.first.outer = bf16[256,1152]{1,0:T(8,128)(2,1)S(1)} collective-permute-done((bf16[256,1152]{1,0:T(8,128)(2,1)}, bf16[256,1152]{1,0:T(8,128)(2,1)S(1)}, u32[]{:S(2)}, u32[]{:S(2)}) %collective-permute-start.2) | collective-permute-done | bytes 589856 | tf_op jit(solution)/shard_map/ppermute | solution.py:193
  18.0 2.1 %collective-permute-start.5 = (bf16[256,1152]{1,0:T(8,128)(2,1)S(1)}, bf16[256,1152]{1,0:T(8,128)(2,1)S(1)}, u32[]{:S(2)}, u32[]{:S(2)}) collective-permute-start(bf16[256,1152]{1,0:T(8,128)(2,1)S(1)} %collective-permute-done.2.first.outer), channel_id=1, source_target_pairs={{0,8},{2,10},{4,28},{6,30},{8,16},{10,18},{12,4},{14,6},{16,24},{1... | collective-permute-start | bytes 1769480 | tf_op jit(solution)/shard_map/ppermute | solution.py:193
  20.1 0.0 collective-permute-done.3.second
  20.1 2.5 %shard_map.68 = (f32[256,1152]{1,0:T(8,128)S(1)}, f32[24,128]{1,0:T(8,128)S(1)}, bf16[256,1152]{1,0:T(8,128)(2,1)S(1)}) custom-call(f32[4]{0:T(128)S(1)} %pad_maximum_fusion.scalars, bf16[256,1152]{1,0:T(8,128)(2,1)S(1)} %get-tuple-element.38.own, bf16[256,1152]{1,0:T(8,128)(2,1)S(1)} %collective-permute-done.2.first.outer, ...), custom_call_target="tpu_custom_call" | custom-call | flops 603979776 | bytes 7077888 | tf_op jit(solution)/shard_map/pallas_call | solution.py:170
  22.7 0.0 copy-done.8
  22.7 0.0 copy-done.10
  22.7 7.1 %collective-permute-done.first.outer = bf16[256,1152]{1,0:T(8,128)(2,1)S(1)} collective-permute-done((bf16[256,1152]{1,0:T(8,128)(2,1)}, bf16[256,1152]{1,0:T(8,128)(2,1)S(1)}, u32[]{:S(2)}, u32[]{:S(2)}) %collective-permute-start) | collective-permute-done | bytes 589856 | tf_op jit(solution)/shard_map/ppermute | solution.py:193
  29.8 1.5 %collective-permute-done.1.whole.second = bf16[256,1152]{1,0:T(8,128)(2,1)S(1)} collective-permute-done((bf16[256,1152]{1,0:T(8,128)(2,1)}, bf16[256,1152]{1,0:T(8,128)(2,1)S(1)}, u32[]{:S(2)}, u32[]{:S(2)}) %collective-permute-start.1) | collective-permute-done | bytes 589856 | tf_op jit(solution)/shard_map/ppermute | solution.py:193
  31.3 1.6 %collective-permute-start.4 = (bf16[256,1152]{1,0:T(8,128)(2,1)S(1)}, bf16[256,1152]{1,0:T(8,128)(2,1)S(1)}, u32[]{:S(2)}, u32[]{:S(2)}) collective-permute-start(bf16[256,1152]{1,0:T(8,128)(2,1)S(1)} %collective-permute-done.first.outer), channel_id=1, source_target_pairs={{0,8},{2,10},{4,28},{6,30},{8,16},{10,18},{12,4},{14,6},{16,24},{1... | collective-permute-start | bytes 1769480 | tf_op jit(solution)/shard_map/ppermute | solution.py:193
  32.9 0.6 %collective-permute-done.5.inner.far = bf16[256,1152]{1,0:T(8,128)(2,1)S(1)} collective-permute-done((bf16[256,1152]{1,0:T(8,128)(2,1)S(1)}, bf16[256,1152]{1,0:T(8,128)(2,1)S(1)}, u32[]{:S(2)}, u32[]{:S(2)}) %collective-permute-start.5) | collective-permute-done | bytes 589856 | tf_op jit(solution)/shard_map/ppermute | solution.py:193
  33.5 1.4 %shard_map.69 = (bf16[256,1152]{1,0:T(8,128)(2,1)S(1)}, bf16[128,1152]{1,0:T(8,128)(2,1)}) custom-call(f32[4]{0:T(128)S(1)} %pad_maximum_fusion.scalars, bf16[256,1152]{1,0:T(8,128)(2,1)S(1)} %collective-permute-done.2.first.outer, bf16[256,1152]{1,0:T(8,128)(2,1)S(1)} %collective-permute-done.5.inner.far, ...), custom_call_target="tpu_custom_call" | custom-call | flops 301989888 | bytes 3538944 | tf_op jit(solution)/shard_map/pallas_call | solution.py:170
  34.9 1.5 %collective-permute-start.6 = (bf16[256,1152]{1,0:T(8,128)(2,1)S(1)}, bf16[256,1152]{1,0:T(8,128)(2,1)S(1)}, u32[]{:S(2)}, u32[]{:S(2)}) collective-permute-start(bf16[256,1152]{1,0:T(8,128)(2,1)S(1)} %get-tuple-element.51), channel_id=1, source_target_pairs={{0,2},{2,0},{4,6},{6,4},{8,10},{10,8},{12,14},{14,12},{16,18},{18,... | collective-permute-start | bytes 1769480 | tf_op jit(solution)/shard_map/ppermute | solution.py:193
  36.3 2.3 %shard_map.70 = (f32[256,1152]{1,0:T(8,128)S(1)}, bf16[256,1152]{1,0:T(8,128)(2,1)S(1)}) custom-call(f32[4]{0:T(128)S(1)} %pad_maximum_fusion.scalars, bf16[256,1152]{1,0:T(8,128)(2,1)S(1)} %get-tuple-element.48.own, bf16[256,1152]{1,0:T(8,128)(2,1)S(1)} %collective-permute-done.first.outer, bf16[256,1152]{1,0:T(8,128)(2,1)S(1)} %collective-permute-done.1.whole.second, ...), custom_call_target="tpu_custom_call" | custom-call | flops 603979776 | bytes 7077888 | tf_op jit(solution)/shard_map/pallas_call | solution.py:170
  38.6 0.0 copy-start
  38.6 1.0 %copy-done = f32[256,1152]{1,0:T(8,128)} copy-done((f32[256,1152]{1,0:T(8,128)}, f32[256,1152]{1,0:T(8,128)S(1)}, u32[]{:S(2)}) %copy-start) | copy-done | bytes 1179672
  39.7 2.9 %shard_map.71 = (f32[256,1152]{1,0:T(8,128)S(1)}, f32[32,8,128]{2,1,0:T(8,128)}) custom-call(f32[4]{0:T(128)S(1)} %pad_maximum_fusion.scalars, bf16[256,1152]{1,0:T(8,128)(2,1)S(1)} %get-tuple-element.38.own, bf16[256,1152]{1,0:T(8,128)(2,1)S(1)} %collective-permute-done.5.inner.far, bf16[256,1152]{1,0:T(8,128)(2,1)S(1)} %get-tuple-element.54.near_image, ...), custom_call_target="tpu_custom_call" | custom-call | flops 603979776 | bytes 7077888 | tf_op jit(solution)/shard_map/pallas_call | solution.py:170
  42.6 4.5 %collective-permute-done.4.far.inner = bf16[256,1152]{1,0:T(8,128)(2,1)S(1)} collective-permute-done((bf16[256,1152]{1,0:T(8,128)(2,1)S(1)}, bf16[256,1152]{1,0:T(8,128)(2,1)S(1)}, u32[]{:S(2)}, u32[]{:S(2)}) %collective-permute-start.4) | collective-permute-done | bytes 589856 | tf_op jit(solution)/shard_map/ppermute | solution.py:193
  47.0 0.6 shard_map.74
  47.7 0.0 copy-done.2
  47.7 1.6 %collective-permute-start.8 = (bf16[128,1152]{1,0:T(8,128)(2,1)S(1)}, bf16[128,1152]{1,0:T(8,128)(2,1)S(1)}, u32[]{:S(2)}, u32[]{:S(2)}) collective-permute-start(bf16[128,1152]{1,0:T(8,128)(2,1)S(1)} %shard_map.74), channel_id=1, source_target_pairs={{0,2},{2,0},{4,6},{6,4},{8,10},{10,8},{12,14},{14,12},{16,18},{18,... | collective-permute-start | bytes 884744 | tf_op jit(solution)/shard_map/ppermute | solution.py:193
  49.2 0.0 collective-permute-start.7
  49.2 0.0 collective-permute-done.6.refs_0_
  49.2 5.1 %all-to-all-start = ((f32[32,8,128]{2,1,0:T(8,128)}), f32[32,8,128]{2,1,0:T(8,128)S(1)}, u32[]{:S(2)}, u32[]{:S(2)}) async-start(f32[32,8,128]{2,1,0:T(8,128)} %get-tuple-element.72), calls=%async_computation | async-start | bytes 262144 | tf_op jit(solution)/shard_map/all_to_all | solution.py:242
  54.3 0.0 copy-start.3
  54.3 0.0 copy-start.5
  54.3 0.0 copy-start.11
  54.4 1.6 %shard_map.72.refs_3_ = f32[256,1152]{1,0:T(8,128)S(1)} custom-call(f32[4]{0:T(128)S(1)} %pad_maximum_fusion.scalars, bf16[256,1152]{1,0:T(8,128)(2,1)S(1)} %get-tuple-element.48.own, bf16[256,1152]{1,0:T(8,128)(2,1)S(1)} %collective-permute-done.4.far.inner), custom_call_target="tpu_custom_call" | custom-call | flops 301989888 | bytes 3538944 | tf_op jit(solution)/shard_map/pallas_call | solution.py:170
  56.0 0.0 copy-done.3
  56.0 0.0 copy-done.5
  56.0 0.0 copy-done.11
  56.0 0.0 copy-start.7
  56.1 2.8 %shard_map.73 = f32[256,1152]{1,0:T(8,128)} custom-call(f32[4]{0:T(128)S(1)} %pad_maximum_fusion.scalars, bf16[256,1152]{1,0:T(8,128)(2,1)S(1)} %get-tuple-element.38.own, bf16[256,1152]{1,0:T(8,128)(2,1)S(1)} %collective-permute-done.6.refs_0_, f32[256,1152]{1,0:T(8,128)S(1)} %copy-done.3, bf16[256,1152]{1,0:T(8,128)(2,1)S(1)} %copy-done.5, ...), custom_call_target="tpu_custom_call" | custom-call | flops 301989888 | bytes 3538944 | tf_op jit(solution)/shard_map/pallas_call | solution.py:170
  58.9 0.0 collective-permute-done.8.refs_1_
  58.9 0.2 collective-permute-done.7.refs_0_
  59.2 0.0 copy-done.9
  59.2 3.2 %shard_map.75 = f32[256,1152]{1,0:T(8,128)} custom-call(f32[4]{0:T(128)S(1)} %pad_maximum_fusion.scalars, bf16[256,1152]{1,0:T(8,128)(2,1)S(1)} %get-tuple-element.48.own, bf16[128,1152]{1,0:T(8,128)(2,1)S(1)} %collective-permute-done.7.refs_0_, bf16[128,1152]{1,0:T(8,128)(2,1)S(1)} %collective-permute-done.8.refs_1_, f32[256,1152]{1,0:T(8,128)S(1)} %copy-done.1, ...), custom_call_target="tpu_custom_call" | custom-call | flops 301989888 | bytes 3538944 | tf_op jit(solution)/shard_map/pallas_call | solution.py:170
  62.3 0.2 all-to-all-done
  62.6 0.6 slice_reduce_fusion
  (7 shorter events, 0.0 us)
Async XLA Ops:
  0.6 17.4 %collective-permute-start.2 = (bf16[256,1152]{1,0:T(8,128)(2,1)}, bf16[256,1152]{1,0:T(8,128)(2,1)S(1)}, u32[]{:S(2)}, u32[]{:S(2)}) collective-permute-start(bf16[256,1152]{1,0:T(8,128)(2,1)} %refs_4_.1), channel_id=1, source_target_pairs={{0,4},{2,6},{4,0},{6,2},{8,12},{10,14},{12,8},{14,10},{16,20},{18,... | collective-permute-start | bytes 1769480 | tf_op jit(solution)/shard_map/ppermute | solution.py:193
  3.7 16.5 %collective-permute-start.3 = (bf16[256,1152]{1,0:T(8,128)(2,1)}, bf16[256,1152]{1,0:T(8,128)(2,1)S(1)}, u32[]{:S(2)}, u32[]{:S(2)}) collective-permute-start(bf16[256,1152]{1,0:T(8,128)(2,1)} %refs_4_.1), channel_id=1, source_target_pairs={{0,2},{2,0},{4,6},{6,4},{8,10},{10,8},{12,14},{14,12},{16,18},{18,... | collective-permute-start | bytes 1769480 | tf_op jit(solution)/shard_map/ppermute | solution.py:193
  5.2 24.7 %collective-permute-start = (bf16[256,1152]{1,0:T(8,128)(2,1)}, bf16[256,1152]{1,0:T(8,128)(2,1)S(1)}, u32[]{:S(2)}, u32[]{:S(2)}) collective-permute-start(bf16[256,1152]{1,0:T(8,128)(2,1)} %refs_2_.1), channel_id=1, source_target_pairs={{0,4},{2,6},{4,0},{6,2},{8,12},{10,14},{12,8},{14,10},{16,20},{18,... | collective-permute-start | bytes 1769480 | tf_op jit(solution)/shard_map/ppermute | solution.py:193
  5.7 25.6 %collective-permute-start.1 = (bf16[256,1152]{1,0:T(8,128)(2,1)}, bf16[256,1152]{1,0:T(8,128)(2,1)S(1)}, u32[]{:S(2)}, u32[]{:S(2)}) collective-permute-start(bf16[256,1152]{1,0:T(8,128)(2,1)} %refs_2_.1), channel_id=1, source_target_pairs={{0,2},{2,0},{4,6},{6,4},{8,10},{10,8},{12,14},{14,12},{16,18},{18,... | collective-permute-start | bytes 1769480 | tf_op jit(solution)/shard_map/ppermute | solution.py:193
  7.2 1.1 %copy-start.4 = (bf16[256,1152]{1,0:T(8,128)(2,1)S(1)}, bf16[256,1152]{1,0:T(8,128)(2,1)}, u32[]{:S(2)}) copy-start(bf16[256,1152]{1,0:T(8,128)(2,1)} %refs_2_.1) | copy-start | bytes 1769476
  8.3 1.1 %copy-start.6 = (bf16[256,1152]{1,0:T(8,128)(2,1)S(1)}, bf16[256,1152]{1,0:T(8,128)(2,1)}, u32[]{:S(2)}) copy-start(bf16[256,1152]{1,0:T(8,128)(2,1)} %refs_4_.1) | copy-start | bytes 1769476
  12.1 10.6 %copy-start.8 = (f32[256,128]{1,0:T(8,128)}, f32[256,128]{1,0:T(8,128)S(1)}, u32[]{:S(2)}) copy-start(f32[256,128]{1,0:T(8,128)S(1)} %get-tuple-element.71.refs_5_) | copy-start | bytes 393220
  12.1 10.6 %copy-start.10 = (f32[256,128]{1,0:T(8,128)}, f32[256,128]{1,0:T(8,128)S(1)}, u32[]{:S(2)}) copy-start(f32[256,128]{1,0:T(8,128)S(1)} %get-tuple-element.66.refs_3_) | copy-start | bytes 393220
  18.0 15.5 %collective-permute-start.5 = (bf16[256,1152]{1,0:T(8,128)(2,1)S(1)}, bf16[256,1152]{1,0:T(8,128)(2,1)S(1)}, u32[]{:S(2)}, u32[]{:S(2)}) collective-permute-start(bf16[256,1152]{1,0:T(8,128)(2,1)S(1)} %collective-permute-done.2.first.outer), channel_id=1, source_target_pairs={{0,8},{2,10},{4,28},{6,30},{8,16},{10,18},{12,4},{14,6},{16,24},{1... | collective-permute-start | bytes 1769480 | tf_op jit(solution)/shard_map/ppermute | solution.py:193
  31.3 15.7 %collective-permute-start.4 = (bf16[256,1152]{1,0:T(8,128)(2,1)S(1)}, bf16[256,1152]{1,0:T(8,128)(2,1)S(1)}, u32[]{:S(2)}, u32[]{:S(2)}) collective-permute-start(bf16[256,1152]{1,0:T(8,128)(2,1)S(1)} %collective-permute-done.first.outer), channel_id=1, source_target_pairs={{0,8},{2,10},{4,28},{6,30},{8,16},{10,18},{12,4},{14,6},{16,24},{1... | collective-permute-start | bytes 1769480 | tf_op jit(solution)/shard_map/ppermute | solution.py:193
  34.9 14.4 %collective-permute-start.6 = (bf16[256,1152]{1,0:T(8,128)(2,1)S(1)}, bf16[256,1152]{1,0:T(8,128)(2,1)S(1)}, u32[]{:S(2)}, u32[]{:S(2)}) collective-permute-start(bf16[256,1152]{1,0:T(8,128)(2,1)S(1)} %get-tuple-element.51), channel_id=1, source_target_pairs={{0,2},{2,0},{4,6},{6,4},{8,10},{10,8},{12,14},{14,12},{16,18},{18,... | collective-permute-start | bytes 1769480 | tf_op jit(solution)/shard_map/ppermute | solution.py:193
  38.6 1.0 %copy-start = (f32[256,1152]{1,0:T(8,128)}, f32[256,1152]{1,0:T(8,128)S(1)}, u32[]{:S(2)}) copy-start(f32[256,1152]{1,0:T(8,128)S(1)} %get-tuple-element.69.refs_2_) | copy-start | bytes 3538948
  42.6 5.1 %copy-start.2 = (f32[256,1152]{1,0:T(8,128)}, f32[256,1152]{1,0:T(8,128)S(1)}, u32[]{:S(2)}) copy-start(f32[256,1152]{1,0:T(8,128)S(1)} %get-tuple-element.65.refs_1_) | copy-start | bytes 3538948
  47.7 11.3 %collective-permute-start.8 = (bf16[128,1152]{1,0:T(8,128)(2,1)S(1)}, bf16[128,1152]{1,0:T(8,128)(2,1)S(1)}, u32[]{:S(2)}, u32[]{:S(2)}) collective-permute-start(bf16[128,1152]{1,0:T(8,128)(2,1)S(1)} %shard_map.74), channel_id=1, source_target_pairs={{0,2},{2,0},{4,6},{6,4},{8,10},{10,8},{12,14},{14,12},{16,18},{18,... | collective-permute-start | bytes 884744 | tf_op jit(solution)/shard_map/ppermute | solution.py:193
  49.2 9.9 %collective-permute-start.7 = (bf16[128,1152]{1,0:T(8,128)(2,1)}, bf16[128,1152]{1,0:T(8,128)(2,1)S(1)}, u32[]{:S(2)}, u32[]{:S(2)}) collective-permute-start(bf16[128,1152]{1,0:T(8,128)(2,1)} %get-tuple-element.68), channel_id=1, source_target_pairs={{0,4},{2,30},{4,8},{6,2},{8,12},{10,6},{12,16},{14,10},{16,20},{18... | collective-permute-start | bytes 884744 | tf_op jit(solution)/shard_map/ppermute | solution.py:193
  49.2 13.3 %all-to-all-start = ((f32[32,8,128]{2,1,0:T(8,128)}), f32[32,8,128]{2,1,0:T(8,128)S(1)}, u32[]{:S(2)}, u32[]{:S(2)}) async-start(f32[32,8,128]{2,1,0:T(8,128)} %get-tuple-element.72), calls=%async_computation | async-start | bytes 262144 | tf_op jit(solution)/shard_map/all_to_all | solution.py:242
  54.3 1.7 %copy-start.3 = (f32[256,1152]{1,0:T(8,128)S(1)}, f32[256,1152]{1,0:T(8,128)}, u32[]{:S(2)}) copy-start(f32[256,1152]{1,0:T(8,128)} %copy-done.2) | copy-start | bytes 3538948
  54.3 1.7 %copy-start.5 = (bf16[256,1152]{1,0:T(8,128)(2,1)S(1)}, bf16[256,1152]{1,0:T(8,128)(2,1)}, u32[]{:S(2)}) copy-start(bf16[256,1152]{1,0:T(8,128)(2,1)} %refs_2_.1) | copy-start | bytes 1769476
  54.3 1.7 %copy-start.11 = (f32[256,128]{1,0:T(8,128)S(1)}, f32[256,128]{1,0:T(8,128)}, u32[]{:S(2)}) copy-start(f32[256,128]{1,0:T(8,128)} %copy-done.10) | copy-start | bytes 393220
  56.0 3.1 %copy-start.1 = (f32[256,1152]{1,0:T(8,128)S(1)}, f32[256,1152]{1,0:T(8,128)}, u32[]{:S(2)}) copy-start(f32[256,1152]{1,0:T(8,128)} %copy-done) | copy-start | bytes 3538948
  56.0 3.1 %copy-start.7 = (bf16[256,1152]{1,0:T(8,128)(2,1)S(1)}, bf16[256,1152]{1,0:T(8,128)(2,1)}, u32[]{:S(2)}) copy-start(bf16[256,1152]{1,0:T(8,128)(2,1)} %refs_4_.1) | copy-start | bytes 1769476
  56.1 3.1 %copy-start.9 = (f32[256,128]{1,0:T(8,128)S(1)}, f32[256,128]{1,0:T(8,128)}, u32[]{:S(2)}) copy-start(f32[256,128]{1,0:T(8,128)} %copy-done.8) | copy-start | bytes 393220

commit v6 on v5

--- a/solution.py
+++ b/solution.py
@@ -125,7 +125,7 @@
     lane = lax.broadcasted_iota(jnp.int32, (8, 128), 1)
     sums = [jnp.sum(tally[8 * i : 8 * i + 8]) for i in range(3)]
     row = jnp.where(lane == 0, sums[0], jnp.where(lane == 1, sums[1], sums[2]))
-    sums_out[...] = jnp.broadcast_to((row * scalars[3])[None], sums_out.shape)
+    sums_out[...] = jnp.broadcast_to((row * scalars[3])[:4][None], sums_out.shape)
 
 
 def image_far_kernel(scalars, own, far, out):
@@ -206,7 +206,7 @@
     part = jax.ShapeDtypeStruct((half, width), jnp.bfloat16)
     column = jax.ShapeDtypeStruct((rows, 128), f32)
     tally = jax.ShapeDtypeStruct((24, 128), f32)
-    spread = jax.ShapeDtypeStruct((devices, 8, 128), f32)
+    spread = jax.ShapeDtypeStruct((devices, 4, 128), f32)
 
     def run(kernel, tiles, operands, *shapes):
         return call(kernel, [scalars, *operands], shapes, rows, width, tiles)
@@ -224,17 +224,18 @@
     gx, stats, unit_y = run(
         text_pair_kernel, 2, [img_unit, txt_y, txt_x, gx, stats], tile, tally, unit
     )
-    img_y, img_x, gx = tied(img_y, img_x, gx)
+    img_y, gx = tied(img_y, gx)
     img_z = send(img_y, beyond)
     txt_z, img_x, img_y = tied(txt_z, img_x, img_y)
     txt_v, img_h = run(pick_kernel, 1, [txt_y, txt_z, img_x], unit, part)
     txt_w = send(txt_v, beside)
-    img_k = send(img_h, turn)
     txt_v, gy = tied(txt_v, gy)
     gy, unit_x = run(image_pair_kernel, 2, [txt_unit, img_y, img_x, gy], tile, unit)
     gx, sums = run(
         text_far_kernel, 2, [img_unit, txt_z, unit_x, unit_y, gx, stats], tile, spread
     )
+    img_h, gx = tied(img_h, gx)
+    img_k = send(img_h, turn)
     img_z, gx, gy = tied(img_z, gx, gy)
     (img_v,) = run(pick_half_kernel, 1, [img_y, img_z], part)
     img_w = send(img_v, beside)

time: 63.4 us -> 62.6 us (0.987)
  waiting for transfers between devices: 20.1 us -> 18.6 us
  starting transfers between devices: 16.9 us -> 17.6 us
    ppermute x9, waiting for transfers between devices: 19.9 us -> 18.6 us  [send(): return lax.ppermute(block, 'blk', route)]
    ppermute x9, starting transfers between devices: 11.8 us -> 12.8 us  [send(): return lax.ppermute(block, 'blk', route)]
  transfers between devices with their start and end apart: 10 -> 10, of which waited for: 7 -> 4; matrix products, arithmetic and copies ran while one was open for 0% -> 0% of each run, Pallas kernels for 32% -> 32%
where the time goes in v6:
time: 62.6 us; the launch traced here: 62.3 us
  Pallas kernels  20.1 us (32%)
  waiting for transfers between devices  18.6 us (30%)
  starting transfers between devices  17.6 us (28%)
  local copies, waits for them, and re-layouts  3.21 us (5%)
  between operations  2.17 us (3%)
  other arithmetic  0.64 us (1%)
    pallas_call x9, Pallas kernels, call(): pl.pallas_call(kernel, out_shape=shapes, in_specs=[IN_SMEM] + [IN_VMEM] *...  20.1 us
    ppermute x9, waiting for transfers between devices, send(): return lax.ppermute(block, 'blk', route)  18.6 us
    ppermute x9, starting transfers between devices, send(): return lax.ppermute(block, 'blk', route)  12.8 us
    all_to_all x1, starting transfers between devices, on_device(): seen = lax.all_to_all(sums, ('blk', 'grp'), 0, 0)  4.84 us
    unnamed x24, local copies, waits for them, and re-layouts  3.21 us
  transfers between devices with their start and end apart: 10, of which 4 were waited for; matrix products, arithmetic and copies ran while one was open for 0% of the time, Pallas kernels for 32%

profile of v6, /device:TPU:0, one launch (start us, length us, event | category | flops | bytes accessed | tf_op | source)
XLA Modules:
  0.0 62.3 jit_solution(17747667603844288575)
XLA Ops:
  0.6 3.0 %collective-permute-start.1 = (bf16[256,1152]{1,0:T(8,128)(2,1)}, bf16[256,1152]{1,0:T(8,128)(2,1)S(1)}, u32[]{:S(2)}, u32[]{:S(2)}) collective-permute-start(bf16[256,1152]{1,0:T(8,128)(2,1)} %refs_4_.1), channel_id=1, source_target_pairs={{0,4},{2,6},{4,0},{6,2},{8,12},{10,14},{12,8},{14,10},{16,20},{18,... | collective-permute-start | bytes 1769480 | tf_op jit(solution)/shard_map/ppermute | solution.py:193
  3.7 1.5 %collective-permute-start.2 = (bf16[256,1152]{1,0:T(8,128)(2,1)}, bf16[256,1152]{1,0:T(8,128)(2,1)S(1)}, u32[]{:S(2)}, u32[]{:S(2)}) collective-permute-start(bf16[256,1152]{1,0:T(8,128)(2,1)} %refs_4_.1), channel_id=1, source_target_pairs={{0,2},{2,0},{4,6},{6,4},{8,10},{10,8},{12,14},{14,12},{16,18},{18,... | collective-permute-start | bytes 1769480 | tf_op jit(solution)/shard_map/ppermute | solution.py:193
  5.2 0.5 collective-permute-start
  5.7 0.1 collective-permute-start.5
  7.1 0.1 pad_maximum_fusion.scalars
  7.2 1.1 %copy-done.4 = bf16[256,1152]{1,0:T(8,128)(2,1)S(1)} copy-done((bf16[256,1152]{1,0:T(8,128)(2,1)S(1)}, bf16[256,1152]{1,0:T(8,128)(2,1)}, u32[]{:S(2)}) %copy-start.4) | copy-done | bytes 589848
  8.3 1.1 %copy-done.6 = bf16[256,1152]{1,0:T(8,128)(2,1)S(1)} copy-done((bf16[256,1152]{1,0:T(8,128)(2,1)S(1)}, bf16[256,1152]{1,0:T(8,128)(2,1)}, u32[]{:S(2)}) %copy-start.6) | copy-done | bytes 589848
  9.3 2.7 %shard_map.67 = (bf16[256,1152]{1,0:T(8,128)(2,1)S(1)}, bf16[256,1152]{1,0:T(8,128)(2,1)S(1)}, f32[256,128]{1,0:T(8,128)S(1)}, f32[256,128]{1,0:T(8,128)S(1)}, f...) custom-call(f32[4]{0:T(128)S(1)} %pad_maximum_fusion.scalars, ...), custom_call_target="tpu_custom_call" | custom-call | flops 603979776 | bytes 7077888 | tf_op jit(solution)/shard_map/pallas_call | solution.py:170
  12.1 0.0 copy-start.8
  12.1 0.0 copy-start.10
  12.1 5.9 %collective-permute-done.1.first.outer = bf16[256,1152]{1,0:T(8,128)(2,1)S(1)} collective-permute-done((bf16[256,1152]{1,0:T(8,128)(2,1)}, bf16[256,1152]{1,0:T(8,128)(2,1)S(1)}, u32[]{:S(2)}, u32[]{:S(2)}) %collective-permute-start.1) | collective-permute-done | bytes 589856 | tf_op jit(solution)/shard_map/ppermute | solution.py:193
  18.0 2.1 %collective-permute-start.4 = (bf16[256,1152]{1,0:T(8,128)(2,1)S(1)}, bf16[256,1152]{1,0:T(8,128)(2,1)S(1)}, u32[]{:S(2)}, u32[]{:S(2)}) collective-permute-start(bf16[256,1152]{1,0:T(8,128)(2,1)S(1)} %collective-permute-done.1.first.outer), channel_id=1, source_target_pairs={{0,8},{2,10},{4,28},{6,30},{8,16},{10,18},{12,4},{14,6},{16,24},{1... | collective-permute-start | bytes 1769480 | tf_op jit(solution)/shard_map/ppermute | solution.py:193
  20.1 0.0 collective-permute-done.2.second
  20.1 2.5 %shard_map.68 = (f32[256,1152]{1,0:T(8,128)S(1)}, f32[24,128]{1,0:T(8,128)S(1)}, bf16[256,1152]{1,0:T(8,128)(2,1)S(1)}) custom-call(f32[4]{0:T(128)S(1)} %pad_maximum_fusion.scalars, bf16[256,1152]{1,0:T(8,128)(2,1)S(1)} %get-tuple-element.39.own, bf16[256,1152]{1,0:T(8,128)(2,1)S(1)} %collective-permute-done.1.first.outer, ...), custom_call_target="tpu_custom_call" | custom-call | flops 603979776 | bytes 7077888 | tf_op jit(solution)/shard_map/pallas_call | solution.py:170
  22.7 0.0 copy-done.8
  22.7 0.0 copy-done.10
  22.7 7.1 %collective-permute-done.first.outer = bf16[256,1152]{1,0:T(8,128)(2,1)S(1)} collective-permute-done((bf16[256,1152]{1,0:T(8,128)(2,1)}, bf16[256,1152]{1,0:T(8,128)(2,1)S(1)}, u32[]{:S(2)}, u32[]{:S(2)}) %collective-permute-start) | collective-permute-done | bytes 589856 | tf_op jit(solution)/shard_map/ppermute | solution.py:193
  29.8 1.8 %collective-permute-start.3 = (bf16[256,1152]{1,0:T(8,128)(2,1)S(1)}, bf16[256,1152]{1,0:T(8,128)(2,1)S(1)}, u32[]{:S(2)}, u32[]{:S(2)}) collective-permute-start(bf16[256,1152]{1,0:T(8,128)(2,1)S(1)} %collective-permute-done.first.outer), channel_id=1, source_target_pairs={{0,8},{2,10},{4,28},{6,30},{8,16},{10,18},{12,4},{14,6},{16,24},{1... | collective-permute-start | bytes 1769480 | tf_op jit(solution)/shard_map/ppermute | solution.py:193
  31.6 0.0 collective-permute-done.5.whole.second
  31.6 1.9 %collective-permute-done.4.inner.far = bf16[256,1152]{1,0:T(8,128)(2,1)S(1)} collective-permute-done((bf16[256,1152]{1,0:T(8,128)(2,1)S(1)}, bf16[256,1152]{1,0:T(8,128)(2,1)S(1)}, u32[]{:S(2)}, u32[]{:S(2)}) %collective-permute-start.4) | collective-permute-done | bytes 589856 | tf_op jit(solution)/shard_map/ppermute | solution.py:193
  33.5 1.4 %shard_map.69 = (bf16[256,1152]{1,0:T(8,128)(2,1)S(1)}, bf16[128,1152]{1,0:T(8,128)(2,1)}) custom-call(f32[4]{0:T(128)S(1)} %pad_maximum_fusion.scalars, bf16[256,1152]{1,0:T(8,128)(2,1)S(1)} %collective-permute-done.1.first.outer, bf16[256,1152]{1,0:T(8,128)(2,1)S(1)} %collective-permute-done.4.inner.far, ...), custom_call_target="tpu_custom_call" | custom-call | flops 301989888 | bytes 3538944 | tf_op jit(solution)/shard_map/pallas_call | solution.py:170
  34.9 1.5 %collective-permute-start.6 = (bf16[256,1152]{1,0:T(8,128)(2,1)S(1)}, bf16[256,1152]{1,0:T(8,128)(2,1)S(1)}, u32[]{:S(2)}, u32[]{:S(2)}) collective-permute-start(bf16[256,1152]{1,0:T(8,128)(2,1)S(1)} %get-tuple-element.52), channel_id=1, source_target_pairs={{0,2},{2,0},{4,6},{6,4},{8,10},{10,8},{12,14},{14,12},{16,18},{18,... | collective-permute-start | bytes 1769480 | tf_op jit(solution)/shard_map/ppermute | solution.py:193
  36.3 2.3 %shard_map.70 = (f32[256,1152]{1,0:T(8,128)S(1)}, bf16[256,1152]{1,0:T(8,128)(2,1)S(1)}) custom-call(f32[4]{0:T(128)S(1)} %pad_maximum_fusion.scalars, bf16[256,1152]{1,0:T(8,128)(2,1)S(1)} %get-tuple-element.50.own, bf16[256,1152]{1,0:T(8,128)(2,1)S(1)} %collective-permute-done.first.outer, bf16[256,1152]{1,0:T(8,128)(2,1)S(1)} %collective-permute-done.5.whole.second, ...), custom_call_target="tpu_custom_call" | custom-call | flops 603979776 | bytes 7077888 | tf_op jit(solution)/shard_map/pallas_call | solution.py:170
  38.6 0.0 copy-start
  38.6 1.0 %copy-done = f32[256,1152]{1,0:T(8,128)} copy-done((f32[256,1152]{1,0:T(8,128)}, f32[256,1152]{1,0:T(8,128)S(1)}, u32[]{:S(2)}) %copy-start) | copy-done | bytes 1179672
  39.7 2.9 %shard_map.71 = (f32[256,1152]{1,0:T(8,128)S(1)}, f32[32,4,128]{2,1,0:T(4,128)}) custom-call(f32[4]{0:T(128)S(1)} %pad_maximum_fusion.scalars, bf16[256,1152]{1,0:T(8,128)(2,1)S(1)} %get-tuple-element.39.own, bf16[256,1152]{1,0:T(8,128)(2,1)S(1)} %collective-permute-done.4.inner.far, bf16[256,1152]{1,0:T(8,128)(2,1)S(1)} %get-tuple-element.55.near_image, ...), custom_call_target="tpu_custom_call" | custom-call | flops 603979776 | bytes 7077888 | tf_op jit(solution)/shard_map/pallas_call | solution.py:170
  42.6 3.6 %collective-permute-done.3.far.inner = bf16[256,1152]{1,0:T(8,128)(2,1)S(1)} collective-permute-done((bf16[256,1152]{1,0:T(8,128)(2,1)S(1)}, bf16[256,1152]{1,0:T(8,128)(2,1)S(1)}, u32[]{:S(2)}, u32[]{:S(2)}) %collective-permute-start.3) | collective-permute-done | bytes 589856 | tf_op jit(solution)/shard_map/ppermute | solution.py:193
  46.2 0.6 shard_map.74
  46.8 1.5 %collective-permute-start.8 = (bf16[128,1152]{1,0:T(8,128)(2,1)S(1)}, bf16[128,1152]{1,0:T(8,128)(2,1)S(1)}, u32[]{:S(2)}, u32[]{:S(2)}) collective-permute-start(bf16[128,1152]{1,0:T(8,128)(2,1)S(1)} %shard_map.74), channel_id=1, source_target_pairs={{0,2},{2,0},{4,6},{6,4},{8,10},{10,8},{12,14},{14,12},{16,18},{18,... | collective-permute-start | bytes 884744 | tf_op jit(solution)/shard_map/ppermute | solution.py:193
  48.3 0.8 %collective-permute-start.7 = (bf16[128,1152]{1,0:T(8,128)(2,1)}, bf16[128,1152]{1,0:T(8,128)(2,1)S(1)}, u32[]{:S(2)}, u32[]{:S(2)}) collective-permute-start(bf16[128,1152]{1,0:T(8,128)(2,1)} %get-tuple-element.70), channel_id=1, source_target_pairs={{0,4},{2,30},{4,8},{6,2},{8,12},{10,6},{12,16},{14,10},{16,20},{18... | collective-permute-start | bytes 884744 | tf_op jit(solution)/shard_map/ppermute | solution.py:193
  49.1 0.0 collective-permute-done.6.refs_0_
  49.1 4.8 %all-to-all-start = ((f32[32,4,128]{2,1,0:T(4,128)}), f32[32,4,128]{2,1,0:T(4,128)S(1)}, u32[]{:S(2)}, u32[]{:S(2)}) async-start(f32[32,4,128]{2,1,0:T(4,128)} %get-tuple-element.74), calls=%async_computation | async-start | bytes 131072 | tf_op jit(solution)/shard_map/all_to_all | solution.py:243
  53.9 0.0 copy-start.3
  53.9 0.0 copy-start.5
  54.0 0.0 copy-start.11
  54.0 1.6 %shard_map.72.refs_3_ = f32[256,1152]{1,0:T(8,128)S(1)} custom-call(f32[4]{0:T(128)S(1)} %pad_maximum_fusion.scalars, bf16[256,1152]{1,0:T(8,128)(2,1)S(1)} %get-tuple-element.50.own, bf16[256,1152]{1,0:T(8,128)(2,1)S(1)} %collective-permute-done.3.far.inner), custom_call_target="tpu_custom_call" | custom-call | flops 301989888 | bytes 3538944 | tf_op jit(solution)/shard_map/pallas_call | solution.py:170
  55.6 0.0 copy-done.3
  55.6 0.0 copy-done.5
  55.6 0.0 copy-done.11
  55.6 0.0 copy-start.1
  55.7 0.0 copy-start.7
  55.7 2.8 %shard_map.73 = f32[256,1152]{1,0:T(8,128)} custom-call(f32[4]{0:T(128)S(1)} %pad_maximum_fusion.scalars, bf16[256,1152]{1,0:T(8,128)(2,1)S(1)} %get-tuple-element.39.own, bf16[256,1152]{1,0:T(8,128)(2,1)S(1)} %collective-permute-done.6.refs_0_, f32[256,1152]{1,0:T(8,128)S(1)} %copy-done.3, bf16[256,1152]{1,0:T(8,128)(2,1)S(1)} %copy-done.5, ...), custom_call_target="tpu_custom_call" | custom-call | flops 301989888 | bytes 3538944 | tf_op jit(solution)/shard_map/pallas_call | solution.py:170
  58.5 0.0 collective-permute-done.8.refs_1_
  58.5 0.0 collective-permute-done.7.refs_0_
  58.5 0.0 copy-done.1
  58.6 3.2 %shard_map.75 = f32[256,1152]{1,0:T(8,128)} custom-call(f32[4]{0:T(128)S(1)} %pad_maximum_fusion.scalars, bf16[256,1152]{1,0:T(8,128)(2,1)S(1)} %get-tuple-element.50.own, bf16[128,1152]{1,0:T(8,128)(2,1)S(1)} %collective-permute-done.7.refs_0_, bf16[128,1152]{1,0:T(8,128)(2,1)S(1)} %collective-permute-done.8.refs_1_, f32[256,1152]{1,0:T(8,128)S(1)} %copy-done.1, ...), custom_call_target="tpu_custom_call" | custom-call | flops 301989888 | bytes 3538944 | tf_op jit(solution)/shard_map/pallas_call | solution.py:170
  61.7 0.0 all-to-all-done
  61.7 0.6 slice_reduce_fusion
  (7 shorter events, 0.0 us)
Async XLA Ops:
  0.6 17.4 %collective-permute-start.1 = (bf16[256,1152]{1,0:T(8,128)(2,1)}, bf16[256,1152]{1,0:T(8,128)(2,1)S(1)}, u32[]{:S(2)}, u32[]{:S(2)}) collective-permute-start(bf16[256,1152]{1,0:T(8,128)(2,1)} %refs_4_.1), channel_id=1, source_target_pairs={{0,4},{2,6},{4,0},{6,2},{8,12},{10,14},{12,8},{14,10},{16,20},{18,... | collective-permute-start | bytes 1769480 | tf_op jit(solution)/shard_map/ppermute | solution.py:193
  3.7 16.5 %collective-permute-start.2 = (bf16[256,1152]{1,0:T(8,128)(2,1)}, bf16[256,1152]{1,0:T(8,128)(2,1)S(1)}, u32[]{:S(2)}, u32[]{:S(2)}) collective-permute-start(bf16[256,1152]{1,0:T(8,128)(2,1)} %refs_4_.1), channel_id=1, source_target_pairs={{0,2},{2,0},{4,6},{6,4},{8,10},{10,8},{12,14},{14,12},{16,18},{18,... | collective-permute-start | bytes 1769480 | tf_op jit(solution)/shard_map/ppermute | solution.py:193
  5.2 24.7 %collective-permute-start = (bf16[256,1152]{1,0:T(8,128)(2,1)}, bf16[256,1152]{1,0:T(8,128)(2,1)S(1)}, u32[]{:S(2)}, u32[]{:S(2)}) collective-permute-start(bf16[256,1152]{1,0:T(8,128)(2,1)} %refs_2_.1), channel_id=1, source_target_pairs={{0,4},{2,6},{4,0},{6,2},{8,12},{10,14},{12,8},{14,10},{16,20},{18,... | collective-permute-start | bytes 1769480 | tf_op jit(solution)/shard_map/ppermute | solution.py:193
  5.7 26.0 %collective-permute-start.5 = (bf16[256,1152]{1,0:T(8,128)(2,1)}, bf16[256,1152]{1,0:T(8,128)(2,1)S(1)}, u32[]{:S(2)}, u32[]{:S(2)}) collective-permute-start(bf16[256,1152]{1,0:T(8,128)(2,1)} %refs_2_.1), channel_id=1, source_target_pairs={{0,2},{2,0},{4,6},{6,4},{8,10},{10,8},{12,14},{14,12},{16,18},{18,... | collective-permute-start | bytes 1769480 | tf_op jit(solution)/shard_map/ppermute | solution.py:193
  7.2 1.1 %copy-start.4 = (bf16[256,1152]{1,0:T(8,128)(2,1)S(1)}, bf16[256,1152]{1,0:T(8,128)(2,1)}, u32[]{:S(2)}) copy-start(bf16[256,1152]{1,0:T(8,128)(2,1)} %refs_2_.1) | copy-start | bytes 1769476
  8.3 1.1 %copy-start.6 = (bf16[256,1152]{1,0:T(8,128)(2,1)S(1)}, bf16[256,1152]{1,0:T(8,128)(2,1)}, u32[]{:S(2)}) copy-start(bf16[256,1152]{1,0:T(8,128)(2,1)} %refs_4_.1) | copy-start | bytes 1769476
  12.1 10.6 %copy-start.8 = (f32[256,128]{1,0:T(8,128)}, f32[256,128]{1,0:T(8,128)S(1)}, u32[]{:S(2)}) copy-start(f32[256,128]{1,0:T(8,128)S(1)} %get-tuple-element.73.refs_5_) | copy-start | bytes 393220
  12.1 10.6 %copy-start.10 = (f32[256,128]{1,0:T(8,128)}, f32[256,128]{1,0:T(8,128)S(1)}, u32[]{:S(2)}) copy-start(f32[256,128]{1,0:T(8,128)S(1)} %get-tuple-element.68.refs_3_) | copy-start | bytes 393220
  18.0 15.5 %collective-permute-start.4 = (bf16[256,1152]{1,0:T(8,128)(2,1)S(1)}, bf16[256,1152]{1,0:T(8,128)(2,1)S(1)}, u32[]{:S(2)}, u32[]{:S(2)}) collective-permute-start(bf16[256,1152]{1,0:T(8,128)(2,1)S(1)} %collective-permute-done.1.first.outer), channel_id=1, source_target_pairs={{0,8},{2,10},{4,28},{6,30},{8,16},{10,18},{12,4},{14,6},{16,24},{1... | collective-permute-start | bytes 1769480 | tf_op jit(solution)/shard_map/ppermute | solution.py:193
  29.8 16.3 %collective-permute-start.3 = (bf16[256,1152]{1,0:T(8,128)(2,1)S(1)}, bf16[256,1152]{1,0:T(8,128)(2,1)S(1)}, u32[]{:S(2)}, u32[]{:S(2)}) collective-permute-start(bf16[256,1152]{1,0:T(8,128)(2,1)S(1)} %collective-permute-done.first.outer), channel_id=1, source_target_pairs={{0,8},{2,10},{4,28},{6,30},{8,16},{10,18},{12,4},{14,6},{16,24},{1... | collective-permute-start | bytes 1769480 | tf_op jit(solution)/shard_map/ppermute | solution.py:193
  34.9 14.2 %collective-permute-start.6 = (bf16[256,1152]{1,0:T(8,128)(2,1)S(1)}, bf16[256,1152]{1,0:T(8,128)(2,1)S(1)}, u32[]{:S(2)}, u32[]{:S(2)}) collective-permute-start(bf16[256,1152]{1,0:T(8,128)(2,1)S(1)} %get-tuple-element.52), channel_id=1, source_target_pairs={{0,2},{2,0},{4,6},{6,4},{8,10},{10,8},{12,14},{14,12},{16,18},{18,... | collective-permute-start | bytes 1769480 | tf_op jit(solution)/shard_map/ppermute | solution.py:193
  38.6 1.0 %copy-start = (f32[256,1152]{1,0:T(8,128)}, f32[256,1152]{1,0:T(8,128)S(1)}, u32[]{:S(2)}) copy-start(f32[256,1152]{1,0:T(8,128)S(1)} %get-tuple-element.71.refs_2_) | copy-start | bytes 3538948
  42.5 4.2 %copy-start.2 = (f32[256,1152]{1,0:T(8,128)}, f32[256,1152]{1,0:T(8,128)S(1)}, u32[]{:S(2)}) copy-start(f32[256,1152]{1,0:T(8,128)S(1)} %get-tuple-element.67.refs_1_) | copy-start | bytes 3538948
  46.8 11.7 %collective-permute-start.8 = (bf16[128,1152]{1,0:T(8,128)(2,1)S(1)}, bf16[128,1152]{1,0:T(8,128)(2,1)S(1)}, u32[]{:S(2)}, u32[]{:S(2)}) collective-permute-start(bf16[128,1152]{1,0:T(8,128)(2,1)S(1)} %shard_map.74), channel_id=1, source_target_pairs={{0,2},{2,0},{4,6},{6,4},{8,10},{10,8},{12,14},{14,12},{16,18},{18,... | collective-permute-start | bytes 884744 | tf_op jit(solution)/shard_map/ppermute | solution.py:193
  48.3 10.2 %collective-permute-start.7 = (bf16[128,1152]{1,0:T(8,128)(2,1)}, bf16[128,1152]{1,0:T(8,128)(2,1)S(1)}, u32[]{:S(2)}, u32[]{:S(2)}) collective-permute-start(bf16[128,1152]{1,0:T(8,128)(2,1)} %get-tuple-element.70), channel_id=1, source_target_pairs={{0,4},{2,30},{4,8},{6,2},{8,12},{10,6},{12,16},{14,10},{16,20},{18... | collective-permute-start | bytes 884744 | tf_op jit(solution)/shard_map/ppermute | solution.py:193
  49.1 12.6 %all-to-all-start = ((f32[32,4,128]{2,1,0:T(4,128)}), f32[32,4,128]{2,1,0:T(4,128)S(1)}, u32[]{:S(2)}, u32[]{:S(2)}) async-start(f32[32,4,128]{2,1,0:T(4,128)} %get-tuple-element.74), calls=%async_computation | async-start | bytes 131072 | tf_op jit(solution)/shard_map/all_to_all | solution.py:243
  53.9 1.7 %copy-start.3 = (f32[256,1152]{1,0:T(8,128)S(1)}, f32[256,1152]{1,0:T(8,128)}, u32[]{:S(2)}) copy-start(f32[256,1152]{1,0:T(8,128)} %copy-done.2) | copy-start | bytes 3538948
  53.9 1.7 %copy-start.5 = (bf16[256,1152]{1,0:T(8,128)(2,1)S(1)}, bf16[256,1152]{1,0:T(8,128)(2,1)}, u32[]{:S(2)}) copy-start(bf16[256,1152]{1,0:T(8,128)(2,1)} %refs_2_.1) | copy-start | bytes 1769476
  54.0 1.7 %copy-start.11 = (f32[256,128]{1,0:T(8,128)S(1)}, f32[256,128]{1,0:T(8,128)}, u32[]{:S(2)}) copy-start(f32[256,128]{1,0:T(8,128)} %copy-done.10) | copy-start | bytes 393220
  55.6 2.9 %copy-start.1 = (f32[256,1152]{1,0:T(8,128)S(1)}, f32[256,1152]{1,0:T(8,128)}, u32[]{:S(2)}) copy-start(f32[256,1152]{1,0:T(8,128)} %copy-done) | copy-start | bytes 3538948
  55.7 2.9 %copy-start.7 = (bf16[256,1152]{1,0:T(8,128)(2,1)S(1)}, bf16[256,1152]{1,0:T(8,128)(2,1)}, u32[]{:S(2)}) copy-start(bf16[256,1152]{1,0:T(8,128)(2,1)} %refs_4_.1) | copy-start | bytes 1769476
  55.7 2.9 %copy-start.9 = (f32[256,128]{1,0:T(8,128)S(1)}, f32[256,128]{1,0:T(8,128)}, u32[]{:S(2)}) copy-start(f32[256,128]{1,0:T(8,128)} %copy-done.8) | copy-start | bytes 393220

commit v7 on v6

--- a/solution.py
+++ b/solution.py
@@ -105,7 +105,8 @@
     stats_out[...] = stats[...] + tally_a + tally_b
 
 
-def image_pair_kernel(scalars, own, first, second, gy, gy_out, unit_out):
+def image_pair_kernel(scalars, own, first, second, gy, gy_out, unit_out, part):
+    part[...] = second[: part.shape[0]]
     unit = rounded_unit(widened(second))
     unit_out[...] = unit
     grad_a, _ = meet(scalars, own[...], rounded_unit(widened(first)))
@@ -136,9 +137,8 @@
     return jnp.where(scalars[2] > 0.5, widened(outer), widened(inner)).astype(outer.dtype)
 
 
-def pick_kernel(scalars, outer, inner, whole, out, part):
+def pick_kernel(scalars, outer, inner, out):
     out[...] = chosen(scalars, outer, inner)
-    part[...] = whole[: part.shape[0]]
 
 
 def pick_half_kernel(scalars, outer, inner, out):
@@ -227,10 +227,12 @@
     img_y, gx = tied(img_y, gx)
     img_z = send(img_y, beyond)
     txt_z, img_x, img_y = tied(txt_z, img_x, img_y)
-    txt_v, img_h = run(pick_kernel, 1, [txt_y, txt_z, img_x], unit, part)
+    (txt_v,) = run(pick_kernel, 1, [txt_y, txt_z], unit)
     txt_w = send(txt_v, beside)
     txt_v, gy = tied(txt_v, gy)
-    gy, unit_x = run(image_pair_kernel, 2, [txt_unit, img_y, img_x, gy], tile, unit)
+    gy, unit_x, img_h = run(
+        image_pair_kernel, 2, [txt_unit, img_y, img_x, gy], tile, unit, part
+    )
     gx, sums = run(
         text_far_kernel, 2, [img_unit, txt_z, unit_x, unit_y, gx, stats], tile, spread
     )

time: 62.6 us -> 62.4 us (level)
  waiting for transfers between devices: 18.6 us -> 17.8 us
  local copies, waits for them, and re-layouts: 3.21 us -> 3.85 us
    ppermute x9, waiting for transfers between devices: 18.6 us -> 17.8 us  [send(): return lax.ppermute(block, 'blk', route)]
    unnamed x24, local copies, waits for them, and re-layouts: 3.21 us -> 3.85 us
where the time goes in v7:
time: 62.4 us; the launch traced here: 62.1 us
  Pallas kernels  20.1 us (32%)
  waiting for transfers between devices  17.8 us (29%)
  starting transfers between devices  17.5 us (28%)
  local copies, waits for them, and re-layouts  3.85 us (6%)
  between operations  2.14 us (3%)
  other arithmetic  0.64 us (1%)
    pallas_call x9, Pallas kernels, call(): pl.pallas_call(kernel, out_shape=shapes, in_specs=[IN_SMEM] + [IN_VMEM] *...  20.1 us
    ppermute x9, waiting for transfers between devices, send(): return lax.ppermute(block, 'blk', route)  17.8 us
    ppermute x9, starting transfers between devices, send(): return lax.ppermute(block, 'blk', route)  12.9 us
    all_to_all x1, starting transfers between devices, on_device(): seen = lax.all_to_all(sums, ('blk', 'grp'), 0, 0)  4.64 us
    unnamed x24, local copies, waits for them, and re-layouts  3.85 us
  transfers between devices with their start and end apart: 10, of which 4 were waited for; matrix products, arithmetic and copies ran while one was open for 0% of the time, Pallas kernels for 32%

profile of v7, /device:TPU:0, one launch (start us, length us, event | category | flops | bytes accessed | tf_op | source)
XLA Modules:
  0.0 62.1 jit_solution(13818596649445168480)
XLA Ops:
  0.6 3.0 %collective-permute-start.1 = (bf16[256,1152]{1,0:T(8,128)(2,1)}, bf16[256,1152]{1,0:T(8,128)(2,1)S(1)}, u32[]{:S(2)}, u32[]{:S(2)}) collective-permute-start(bf16[256,1152]{1,0:T(8,128)(2,1)} %refs_4_.1), channel_id=1, source_target_pairs={{0,4},{2,6},{4,0},{6,2},{8,12},{10,14},{12,8},{14,10},{16,20},{18,... | collective-permute-start | bytes 1769480 | tf_op jit(solution)/shard_map/ppermute | solution.py:193
  3.7 1.5 %collective-permute-start.2 = (bf16[256,1152]{1,0:T(8,128)(2,1)}, bf16[256,1152]{1,0:T(8,128)(2,1)S(1)}, u32[]{:S(2)}, u32[]{:S(2)}) collective-permute-start(bf16[256,1152]{1,0:T(8,128)(2,1)} %refs_4_.1), channel_id=1, source_target_pairs={{0,2},{2,0},{4,6},{6,4},{8,10},{10,8},{12,14},{14,12},{16,18},{18,... | collective-permute-start | bytes 1769480 | tf_op jit(solution)/shard_map/ppermute | solution.py:193
  5.2 0.5 collective-permute-start
  5.7 0.1 collective-permute-start.5
  7.1 0.1 pad_maximum_fusion.scalars
  7.2 1.1 %copy-done.4 = bf16[256,1152]{1,0:T(8,128)(2,1)S(1)} copy-done((bf16[256,1152]{1,0:T(8,128)(2,1)S(1)}, bf16[256,1152]{1,0:T(8,128)(2,1)}, u32[]{:S(2)}) %copy-start.4) | copy-done | bytes 589848
  8.3 1.1 %copy-done.6 = bf16[256,1152]{1,0:T(8,128)(2,1)S(1)} copy-done((bf16[256,1152]{1,0:T(8,128)(2,1)S(1)}, bf16[256,1152]{1,0:T(8,128)(2,1)}, u32[]{:S(2)}) %copy-start.6) | copy-done | bytes 589848
  9.3 2.7 %shard_map.67 = (bf16[256,1152]{1,0:T(8,128)(2,1)S(1)}, bf16[256,1152]{1,0:T(8,128)(2,1)S(1)}, f32[256,128]{1,0:T(8,128)S(1)}, f32[256,128]{1,0:T(8,128)S(1)}, f...) custom-call(f32[4]{0:T(128)S(1)} %pad_maximum_fusion.scalars, ...), custom_call_target="tpu_custom_call" | custom-call | flops 603979776 | bytes 7077888 | tf_op jit(solution)/shard_map/pallas_call | solution.py:170
  12.1 0.0 copy-start.10
  12.1 0.6 %copy-done.10 = f32[256,128]{1,0:T(8,128)} copy-done((f32[256,128]{1,0:T(8,128)}, f32[256,128]{1,0:T(8,128)S(1)}, u32[]{:S(2)}) %copy-start.10) | copy-done | bytes 131096
  12.7 5.3 %collective-permute-done.1.first.outer = bf16[256,1152]{1,0:T(8,128)(2,1)S(1)} collective-permute-done((bf16[256,1152]{1,0:T(8,128)(2,1)}, bf16[256,1152]{1,0:T(8,128)(2,1)S(1)}, u32[]{:S(2)}, u32[]{:S(2)}) %collective-permute-start.1) | collective-permute-done | bytes 589856 | tf_op jit(solution)/shard_map/ppermute | solution.py:193
  18.0 2.1 %collective-permute-start.4 = (bf16[256,1152]{1,0:T(8,128)(2,1)S(1)}, bf16[256,1152]{1,0:T(8,128)(2,1)S(1)}, u32[]{:S(2)}, u32[]{:S(2)}) collective-permute-start(bf16[256,1152]{1,0:T(8,128)(2,1)S(1)} %collective-permute-done.1.first.outer), channel_id=1, source_target_pairs={{0,8},{2,10},{4,28},{6,30},{8,16},{10,18},{12,4},{14,6},{16,24},{1... | collective-permute-start | bytes 1769480 | tf_op jit(solution)/shard_map/ppermute | solution.py:193
  20.1 0.0 collective-permute-done.2.second
  20.1 2.5 %shard_map.68 = (f32[256,1152]{1,0:T(8,128)S(1)}, f32[24,128]{1,0:T(8,128)S(1)}, bf16[256,1152]{1,0:T(8,128)(2,1)S(1)}) custom-call(f32[4]{0:T(128)S(1)} %pad_maximum_fusion.scalars, bf16[256,1152]{1,0:T(8,128)(2,1)S(1)} %get-tuple-element.38.own, bf16[256,1152]{1,0:T(8,128)(2,1)S(1)} %collective-permute-done.1.first.outer, ...), custom_call_target="tpu_custom_call" | custom-call | flops 603979776 | bytes 7077888 | tf_op jit(solution)/shard_map/pallas_call | solution.py:170
  22.7 0.0 copy-done.8
  22.7 7.2 %collective-permute-done.first.outer = bf16[256,1152]{1,0:T(8,128)(2,1)S(1)} collective-permute-done((bf16[256,1152]{1,0:T(8,128)(2,1)}, bf16[256,1152]{1,0:T(8,128)(2,1)S(1)}, u32[]{:S(2)}, u32[]{:S(2)}) %collective-permute-start) | collective-permute-done | bytes 589856 | tf_op jit(solution)/shard_map/ppermute | solution.py:193
  29.8 1.8 %collective-permute-start.3 = (bf16[256,1152]{1,0:T(8,128)(2,1)S(1)}, bf16[256,1152]{1,0:T(8,128)(2,1)S(1)}, u32[]{:S(2)}, u32[]{:S(2)}) collective-permute-start(bf16[256,1152]{1,0:T(8,128)(2,1)S(1)} %collective-permute-done.first.outer), channel_id=1, source_target_pairs={{0,8},{2,10},{4,28},{6,30},{8,16},{10,18},{12,4},{14,6},{16,24},{1... | collective-permute-start | bytes 1769480 | tf_op jit(solution)/shard_map/ppermute | solution.py:193
  31.6 0.0 collective-permute-done.5.second
  31.6 1.9 %collective-permute-done.4.inner.far = bf16[256,1152]{1,0:T(8,128)(2,1)S(1)} collective-permute-done((bf16[256,1152]{1,0:T(8,128)(2,1)S(1)}, bf16[256,1152]{1,0:T(8,128)(2,1)S(1)}, u32[]{:S(2)}, u32[]{:S(2)}) %collective-permute-start.4) | collective-permute-done | bytes 589856 | tf_op jit(solution)/shard_map/ppermute | solution.py:193
  33.5 0.7 %shard_map.69 = bf16[256,1152]{1,0:T(8,128)(2,1)S(1)} custom-call(f32[4]{0:T(128)S(1)} %pad_maximum_fusion.scalars, bf16[256,1152]{1,0:T(8,128)(2,1)S(1)} %collective-permute-done.1.first.outer, bf16[256,1152]{1,0:T(8,128)(2,1)S(1)} %collective-permute-done.4.inner.far), custom_call_target="tpu_custom_call" | custom-call | flops 301989888 | bytes 3538944 | tf_op jit(solution)/shard_map/pallas_call | solution.py:170
  34.2 1.5 %collective-permute-start.6 = (bf16[256,1152]{1,0:T(8,128)(2,1)S(1)}, bf16[256,1152]{1,0:T(8,128)(2,1)S(1)}, u32[]{:S(2)}, u32[]{:S(2)}) collective-permute-start(bf16[256,1152]{1,0:T(8,128)(2,1)S(1)} %shard_map.69), channel_id=1, source_target_pairs={{0,2},{2,0},{4,6},{6,4},{8,10},{10,8},{12,14},{14,12},{16,18},{18,... | collective-permute-start | bytes 1769480 | tf_op jit(solution)/shard_map/ppermute | solution.py:193
  35.7 3.0 %shard_map.70 = (f32[256,1152]{1,0:T(8,128)S(1)}, bf16[256,1152]{1,0:T(8,128)(2,1)S(1)}, bf16[128,1152]{1,0:T(8,128)(2,1)}) custom-call(f32[4]{0:T(128)S(1)} %pad_maximum_fusion.scalars, bf16[256,1152]{1,0:T(8,128)(2,1)S(1)} %get-tuple-element.46.own, bf16[256,1152]{1,0:T(8,128)(2,1)S(1)} %collective-permute-done.first.outer, ...), custom_call_target="tpu_custom_call" | custom-call | flops 603979776 | bytes 7077888 | tf_op jit(solution)/shard_map/pallas_call | solution.py:170
  38.7 1.0 %copy-done = f32[256,1152]{1,0:T(8,128)} copy-done((f32[256,1152]{1,0:T(8,128)}, f32[256,1152]{1,0:T(8,128)S(1)}, u32[]{:S(2)}) %copy-start) | copy-done | bytes 1179672
  39.7 2.9 %shard_map.71 = (f32[256,1152]{1,0:T(8,128)S(1)}, f32[32,4,128]{2,1,0:T(4,128)}) custom-call(f32[4]{0:T(128)S(1)} %pad_maximum_fusion.scalars, bf16[256,1152]{1,0:T(8,128)(2,1)S(1)} %get-tuple-element.38.own, bf16[256,1152]{1,0:T(8,128)(2,1)S(1)} %collective-permute-done.4.inner.far, bf16[256,1152]{1,0:T(8,128)(2,1)S(1)} %get-tuple-element.53.near_image, ...), custom_call_target="tpu_custom_call" | custom-call | flops 603979776 | bytes 7077888 | tf_op jit(solution)/shard_map/pallas_call | solution.py:170
  42.7 3.5 %collective-permute-done.3.far.inner = bf16[256,1152]{1,0:T(8,128)(2,1)S(1)} collective-permute-done((bf16[256,1152]{1,0:T(8,128)(2,1)S(1)}, bf16[256,1152]{1,0:T(8,128)(2,1)S(1)}, u32[]{:S(2)}, u32[]{:S(2)}) %collective-permute-start.3) | collective-permute-done | bytes 589856 | tf_op jit(solution)/shard_map/ppermute | solution.py:193
  46.2 0.6 shard_map.74
  46.8 0.0 copy-done.2
  46.8 1.5 %collective-permute-start.8 = (bf16[128,1152]{1,0:T(8,128)(2,1)S(1)}, bf16[128,1152]{1,0:T(8,128)(2,1)S(1)}, u32[]{:S(2)}, u32[]{:S(2)}) collective-permute-start(bf16[128,1152]{1,0:T(8,128)(2,1)S(1)} %shard_map.74), channel_id=1, source_target_pairs={{0,2},{2,0},{4,6},{6,4},{8,10},{10,8},{12,14},{14,12},{16,18},{18,... | collective-permute-start | bytes 884744 | tf_op jit(solution)/shard_map/ppermute | solution.py:193
  48.3 0.8 %collective-permute-start.7 = (bf16[128,1152]{1,0:T(8,128)(2,1)}, bf16[128,1152]{1,0:T(8,128)(2,1)S(1)}, u32[]{:S(2)}, u32[]{:S(2)}) collective-permute-start(bf16[128,1152]{1,0:T(8,128)(2,1)} %get-tuple-element.68), channel_id=1, source_target_pairs={{0,4},{2,30},{4,8},{6,2},{8,12},{10,6},{12,16},{14,10},{16,20},{18... | collective-permute-start | bytes 884744 | tf_op jit(solution)/shard_map/ppermute | solution.py:193
  49.1 0.0 collective-permute-done.6.refs_0_
  49.1 4.6 %all-to-all-start = ((f32[32,4,128]{2,1,0:T(4,128)}), f32[32,4,128]{2,1,0:T(4,128)S(1)}, u32[]{:S(2)}, u32[]{:S(2)}) async-start(f32[32,4,128]{2,1,0:T(4,128)} %get-tuple-element.72), calls=%async_computation | async-start | bytes 131072 | tf_op jit(solution)/shard_map/all_to_all | solution.py:245
  53.7 0.0 copy-start.3
  53.8 0.0 copy-start.5
  53.8 0.0 copy-start.11
  53.8 1.6 %shard_map.72.refs_3_ = f32[256,1152]{1,0:T(8,128)S(1)} custom-call(f32[4]{0:T(128)S(1)} %pad_maximum_fusion.scalars, bf16[256,1152]{1,0:T(8,128)(2,1)S(1)} %get-tuple-element.46.own, bf16[256,1152]{1,0:T(8,128)(2,1)S(1)} %collective-permute-done.3.far.inner), custom_call_target="tpu_custom_call" | custom-call | flops 301989888 | bytes 3538944 | tf_op jit(solution)/shard_map/pallas_call | solution.py:170
  55.4 0.0 copy-done.3
  55.4 0.0 copy-done.5
  55.4 0.0 copy-done.11
  55.5 0.0 copy-start.1
  55.5 0.0 copy-start.7
  55.5 0.0 copy-start.9
  55.5 2.8 %shard_map.73 = f32[256,1152]{1,0:T(8,128)} custom-call(f32[4]{0:T(128)S(1)} %pad_maximum_fusion.scalars, bf16[256,1152]{1,0:T(8,128)(2,1)S(1)} %get-tuple-element.38.own, bf16[256,1152]{1,0:T(8,128)(2,1)S(1)} %collective-permute-done.6.refs_0_, f32[256,1152]{1,0:T(8,128)S(1)} %copy-done.3, bf16[256,1152]{1,0:T(8,128)(2,1)S(1)} %copy-done.5, ...), custom_call_target="tpu_custom_call" | custom-call | flops 301989888 | bytes 3538944 | tf_op jit(solution)/shard_map/pallas_call | solution.py:170
  58.3 0.0 collective-permute-done.8.refs_1_
  58.3 0.0 collective-permute-done.7.refs_0_
  58.3 0.0 copy-done.1
  58.4 3.2 %shard_map.75 = f32[256,1152]{1,0:T(8,128)} custom-call(f32[4]{0:T(128)S(1)} %pad_maximum_fusion.scalars, bf16[256,1152]{1,0:T(8,128)(2,1)S(1)} %get-tuple-element.46.own, bf16[128,1152]{1,0:T(8,128)(2,1)S(1)} %collective-permute-done.7.refs_0_, bf16[128,1152]{1,0:T(8,128)(2,1)S(1)} %collective-permute-done.8.refs_1_, f32[256,1152]{1,0:T(8,128)S(1)} %copy-done.1, ...), custom_call_target="tpu_custom_call" | custom-call | flops 301989888 | bytes 3538944 | tf_op jit(solution)/shard_map/pallas_call | solution.py:170
  61.5 0.0 all-to-all-done
  61.5 0.6 slice_reduce_fusion
  (7 shorter events, 0.0 us)
Async XLA Ops:
  0.6 17.4 %collective-permute-start.1 = (bf16[256,1152]{1,0:T(8,128)(2,1)}, bf16[256,1152]{1,0:T(8,128)(2,1)S(1)}, u32[]{:S(2)}, u32[]{:S(2)}) collective-permute-start(bf16[256,1152]{1,0:T(8,128)(2,1)} %refs_4_.1), channel_id=1, source_target_pairs={{0,4},{2,6},{4,0},{6,2},{8,12},{10,14},{12,8},{14,10},{16,20},{18,... | collective-permute-start | bytes 1769480 | tf_op jit(solution)/shard_map/ppermute | solution.py:193
  3.7 16.5 %collective-permute-start.2 = (bf16[256,1152]{1,0:T(8,128)(2,1)}, bf16[256,1152]{1,0:T(8,128)(2,1)S(1)}, u32[]{:S(2)}, u32[]{:S(2)}) collective-permute-start(bf16[256,1152]{1,0:T(8,128)(2,1)} %refs_4_.1), channel_id=1, source_target_pairs={{0,2},{2,0},{4,6},{6,4},{8,10},{10,8},{12,14},{14,12},{16,18},{18,... | collective-permute-start | bytes 1769480 | tf_op jit(solution)/shard_map/ppermute | solution.py:193
  5.2 24.7 %collective-permute-start = (bf16[256,1152]{1,0:T(8,128)(2,1)}, bf16[256,1152]{1,0:T(8,128)(2,1)S(1)}, u32[]{:S(2)}, u32[]{:S(2)}) collective-permute-start(bf16[256,1152]{1,0:T(8,128)(2,1)} %refs_2_.1), channel_id=1, source_target_pairs={{0,4},{2,6},{4,0},{6,2},{8,12},{10,14},{12,8},{14,10},{16,20},{18,... | collective-permute-start | bytes 1769480 | tf_op jit(solution)/shard_map/ppermute | solution.py:193
  5.7 26.0 %collective-permute-start.5 = (bf16[256,1152]{1,0:T(8,128)(2,1)}, bf16[256,1152]{1,0:T(8,128)(2,1)S(1)}, u32[]{:S(2)}, u32[]{:S(2)}) collective-permute-start(bf16[256,1152]{1,0:T(8,128)(2,1)} %refs_2_.1), channel_id=1, source_target_pairs={{0,2},{2,0},{4,6},{6,4},{8,10},{10,8},{12,14},{14,12},{16,18},{18,... | collective-permute-start | bytes 1769480 | tf_op jit(solution)/shard_map/ppermute | solution.py:193
  7.2 1.1 %copy-start.4 = (bf16[256,1152]{1,0:T(8,128)(2,1)S(1)}, bf16[256,1152]{1,0:T(8,128)(2,1)}, u32[]{:S(2)}) copy-start(bf16[256,1152]{1,0:T(8,128)(2,1)} %refs_2_.1) | copy-start | bytes 1769476
  8.3 1.1 %copy-start.6 = (bf16[256,1152]{1,0:T(8,128)(2,1)S(1)}, bf16[256,1152]{1,0:T(8,128)(2,1)}, u32[]{:S(2)}) copy-start(bf16[256,1152]{1,0:T(8,128)(2,1)} %refs_4_.1) | copy-start | bytes 1769476
  12.1 0.7 %copy-start.10 = (f32[256,128]{1,0:T(8,128)}, f32[256,128]{1,0:T(8,128)S(1)}, u32[]{:S(2)}) copy-start(f32[256,128]{1,0:T(8,128)S(1)} %get-tuple-element.66.refs_3_) | copy-start | bytes 393220
  12.7 9.9 %copy-start.8 = (f32[256,128]{1,0:T(8,128)}, f32[256,128]{1,0:T(8,128)S(1)}, u32[]{:S(2)}) copy-start(f32[256,128]{1,0:T(8,128)S(1)} %get-tuple-element.71.refs_5_) | copy-start | bytes 393220
  18.0 15.5 %collective-permute-start.4 = (bf16[256,1152]{1,0:T(8,128)(2,1)S(1)}, bf16[256,1152]{1,0:T(8,128)(2,1)S(1)}, u32[]{:S(2)}, u32[]{:S(2)}) collective-permute-start(bf16[256,1152]{1,0:T(8,128)(2,1)S(1)} %collective-permute-done.1.first.outer), channel_id=1, source_target_pairs={{0,8},{2,10},{4,28},{6,30},{8,16},{10,18},{12,4},{14,6},{16,24},{1... | collective-permute-start | bytes 1769480 | tf_op jit(solution)/shard_map/ppermute | solution.py:193
  29.8 16.3 %collective-permute-start.3 = (bf16[256,1152]{1,0:T(8,128)(2,1)S(1)}, bf16[256,1152]{1,0:T(8,128)(2,1)S(1)}, u32[]{:S(2)}, u32[]{:S(2)}) collective-permute-start(bf16[256,1152]{1,0:T(8,128)(2,1)S(1)} %collective-permute-done.first.outer), channel_id=1, source_target_pairs={{0,8},{2,10},{4,28},{6,30},{8,16},{10,18},{12,4},{14,6},{16,24},{1... | collective-permute-start | bytes 1769480 | tf_op jit(solution)/shard_map/ppermute | solution.py:193
  34.2 14.9 %collective-permute-start.6 = (bf16[256,1152]{1,0:T(8,128)(2,1)S(1)}, bf16[256,1152]{1,0:T(8,128)(2,1)S(1)}, u32[]{:S(2)}, u32[]{:S(2)}) collective-permute-start(bf16[256,1152]{1,0:T(8,128)(2,1)S(1)} %shard_map.69), channel_id=1, source_target_pairs={{0,2},{2,0},{4,6},{6,4},{8,10},{10,8},{12,14},{14,12},{16,18},{18,... | collective-permute-start | bytes 1769480 | tf_op jit(solution)/shard_map/ppermute | solution.py:193
  38.7 1.0 %copy-start = (f32[256,1152]{1,0:T(8,128)}, f32[256,1152]{1,0:T(8,128)S(1)}, u32[]{:S(2)}) copy-start(f32[256,1152]{1,0:T(8,128)S(1)} %get-tuple-element.69.refs_2_) | copy-start | bytes 3538948
  42.7 4.1 %copy-start.2 = (f32[256,1152]{1,0:T(8,128)}, f32[256,1152]{1,0:T(8,128)S(1)}, u32[]{:S(2)}) copy-start(f32[256,1152]{1,0:T(8,128)S(1)} %get-tuple-element.65.refs_1_) | copy-start | bytes 3538948
  46.8 11.6 %collective-permute-start.8 = (bf16[128,1152]{1,0:T(8,128)(2,1)S(1)}, bf16[128,1152]{1,0:T(8,128)(2,1)S(1)}, u32[]{:S(2)}, u32[]{:S(2)}) collective-permute-start(bf16[128,1152]{1,0:T(8,128)(2,1)S(1)} %shard_map.74), channel_id=1, source_target_pairs={{0,2},{2,0},{4,6},{6,4},{8,10},{10,8},{12,14},{14,12},{16,18},{18,... | collective-permute-start | bytes 884744 | tf_op jit(solution)/shard_map/ppermute | solution.py:193
  48.3 10.0 %collective-permute-start.7 = (bf16[128,1152]{1,0:T(8,128)(2,1)}, bf16[128,1152]{1,0:T(8,128)(2,1)S(1)}, u32[]{:S(2)}, u32[]{:S(2)}) collective-permute-start(bf16[128,1152]{1,0:T(8,128)(2,1)} %get-tuple-element.68), channel_id=1, source_target_pairs={{0,4},{2,30},{4,8},{6,2},{8,12},{10,6},{12,16},{14,10},{16,20},{18... | collective-permute-start | bytes 884744 | tf_op jit(solution)/shard_map/ppermute | solution.py:193
  49.1 12.4 %all-to-all-start = ((f32[32,4,128]{2,1,0:T(4,128)}), f32[32,4,128]{2,1,0:T(4,128)S(1)}, u32[]{:S(2)}, u32[]{:S(2)}) async-start(f32[32,4,128]{2,1,0:T(4,128)} %get-tuple-element.72), calls=%async_computation | async-start | bytes 131072 | tf_op jit(solution)/shard_map/all_to_all | solution.py:245
  53.7 1.7 %copy-start.3 = (f32[256,1152]{1,0:T(8,128)S(1)}, f32[256,1152]{1,0:T(8,128)}, u32[]{:S(2)}) copy-start(f32[256,1152]{1,0:T(8,128)} %copy-done.2) | copy-start | bytes 3538948
  53.8 1.7 %copy-start.5 = (bf16[256,1152]{1,0:T(8,128)(2,1)S(1)}, bf16[256,1152]{1,0:T(8,128)(2,1)}, u32[]{:S(2)}) copy-start(bf16[256,1152]{1,0:T(8,128)(2,1)} %refs_2_.1) | copy-start | bytes 1769476
  53.8 1.7 %copy-start.11 = (f32[256,128]{1,0:T(8,128)S(1)}, f32[256,128]{1,0:T(8,128)}, u32[]{:S(2)}) copy-start(f32[256,128]{1,0:T(8,128)} %copy-done.10) | copy-start | bytes 393220
  55.5 2.9 %copy-start.1 = (f32[256,1152]{1,0:T(8,128)S(1)}, f32[256,1152]{1,0:T(8,128)}, u32[]{:S(2)}) copy-start(f32[256,1152]{1,0:T(8,128)} %copy-done) | copy-start | bytes 3538948
  55.5 2.9 %copy-start.7 = (bf16[256,1152]{1,0:T(8,128)(2,1)S(1)}, bf16[256,1152]{1,0:T(8,128)(2,1)}, u32[]{:S(2)}) copy-start(bf16[256,1152]{1,0:T(8,128)(2,1)} %refs_4_.1) | copy-start | bytes 1769476
  55.5 2.9 %copy-start.9 = (f32[256,128]{1,0:T(8,128)S(1)}, f32[256,128]{1,0:T(8,128)}, u32[]{:S(2)}) copy-start(f32[256,128]{1,0:T(8,128)} %copy-done.8) | copy-start | bytes 393220

commit v8 on v7

--- a/solution.py
+++ b/solution.py
@@ -149,8 +149,8 @@
 def last_kernel(count, scalars, own, *refs):
     pieces, (*sums, raw, inverse, out) = refs[:count], refs[count:]
     grad = sum(held[...] for held in sums)
-    for piece in pieces:
-        grad += meet(scalars, own[...], rounded_unit(widened(piece)))[0]
+    block = jnp.concatenate([widened(piece) for piece in pieces], axis=0)
+    grad += meet(scalars, own[...], rounded_unit(block))[0]
     finish(out, grad, raw, inverse)
 
 

time: 62.4 us -> 62.1 us (level)
  no operation moved by 1% of the time
where the time goes in v8:
time: 62.1 us; the launch traced here: 61.8 us
  Pallas kernels  19.8 us (32%)
  waiting for transfers between devices  17.8 us (29%)
  starting transfers between devices  17.5 us (28%)
  local copies, waits for them, and re-layouts  3.85 us (6%)
  between operations  2.14 us (3%)
  other arithmetic  0.64 us (1%)
    pallas_call x9, Pallas kernels, call(): pl.pallas_call(kernel, out_shape=shapes, in_specs=[IN_SMEM] + [IN_VMEM] *...  19.8 us
    ppermute x9, waiting for transfers between devices, send(): return lax.ppermute(block, 'blk', route)  17.8 us
    ppermute x9, starting transfers between devices, send(): return lax.ppermute(block, 'blk', route)  12.9 us
    all_to_all x1, starting transfers between devices, on_device(): seen = lax.all_to_all(sums, ('blk', 'grp'), 0, 0)  4.64 us
    unnamed x24, local copies, waits for them, and re-layouts  3.85 us
  transfers between devices with their start and end apart: 10, of which 4 were waited for; matrix products, arithmetic and copies ran while one was open for 0% of the time, Pallas kernels for 32%

profile of v8, /device:TPU:0, one launch (start us, length us, event | category | flops | bytes accessed | tf_op | source)
XLA Modules:
  0.0 61.8 jit_solution(10585740008241245214)
XLA Ops:
  0.6 3.0 %collective-permute-start.1 = (bf16[256,1152]{1,0:T(8,128)(2,1)}, bf16[256,1152]{1,0:T(8,128)(2,1)S(1)}, u32[]{:S(2)}, u32[]{:S(2)}) collective-permute-start(bf16[256,1152]{1,0:T(8,128)(2,1)} %refs_4_.1), channel_id=1, source_target_pairs={{0,4},{2,6},{4,0},{6,2},{8,12},{10,14},{12,8},{14,10},{16,20},{18,... | collective-permute-start | bytes 1769480 | tf_op jit(solution)/shard_map/ppermute | solution.py:193
  3.7 1.5 %collective-permute-start.2 = (bf16[256,1152]{1,0:T(8,128)(2,1)}, bf16[256,1152]{1,0:T(8,128)(2,1)S(1)}, u32[]{:S(2)}, u32[]{:S(2)}) collective-permute-start(bf16[256,1152]{1,0:T(8,128)(2,1)} %refs_4_.1), channel_id=1, source_target_pairs={{0,2},{2,0},{4,6},{6,4},{8,10},{10,8},{12,14},{14,12},{16,18},{18,... | collective-permute-start | bytes 1769480 | tf_op jit(solution)/shard_map/ppermute | solution.py:193
  5.2 0.5 collective-permute-start
  5.7 0.1 collective-permute-start.5
  7.1 0.1 pad_maximum_fusion.scalars
  7.2 1.1 %copy-done.4 = bf16[256,1152]{1,0:T(8,128)(2,1)S(1)} copy-done((bf16[256,1152]{1,0:T(8,128)(2,1)S(1)}, bf16[256,1152]{1,0:T(8,128)(2,1)}, u32[]{:S(2)}) %copy-start.4) | copy-done | bytes 589848
  8.3 1.1 %copy-done.6 = bf16[256,1152]{1,0:T(8,128)(2,1)S(1)} copy-done((bf16[256,1152]{1,0:T(8,128)(2,1)S(1)}, bf16[256,1152]{1,0:T(8,128)(2,1)}, u32[]{:S(2)}) %copy-start.6) | copy-done | bytes 589848
  9.3 2.7 %shard_map.67 = (bf16[256,1152]{1,0:T(8,128)(2,1)S(1)}, bf16[256,1152]{1,0:T(8,128)(2,1)S(1)}, f32[256,128]{1,0:T(8,128)S(1)}, f32[256,128]{1,0:T(8,128)S(1)}, f...) custom-call(f32[4]{0:T(128)S(1)} %pad_maximum_fusion.scalars, ...), custom_call_target="tpu_custom_call" | custom-call | flops 603979776 | bytes 7077888 | tf_op jit(solution)/shard_map/pallas_call | solution.py:170
  12.1 0.0 copy-start.10
  12.1 0.6 %copy-done.10 = f32[256,128]{1,0:T(8,128)} copy-done((f32[256,128]{1,0:T(8,128)}, f32[256,128]{1,0:T(8,128)S(1)}, u32[]{:S(2)}) %copy-start.10) | copy-done | bytes 131096
  12.7 5.3 %collective-permute-done.1.first.outer = bf16[256,1152]{1,0:T(8,128)(2,1)S(1)} collective-permute-done((bf16[256,1152]{1,0:T(8,128)(2,1)}, bf16[256,1152]{1,0:T(8,128)(2,1)S(1)}, u32[]{:S(2)}, u32[]{:S(2)}) %collective-permute-start.1) | collective-permute-done | bytes 589856 | tf_op jit(solution)/shard_map/ppermute | solution.py:193
  18.0 2.1 %collective-permute-start.4 = (bf16[256,1152]{1,0:T(8,128)(2,1)S(1)}, bf16[256,1152]{1,0:T(8,128)(2,1)S(1)}, u32[]{:S(2)}, u32[]{:S(2)}) collective-permute-start(bf16[256,1152]{1,0:T(8,128)(2,1)S(1)} %collective-permute-done.1.first.outer), channel_id=1, source_target_pairs={{0,8},{2,10},{4,28},{6,30},{8,16},{10,18},{12,4},{14,6},{16,24},{1... | collective-permute-start | bytes 1769480 | tf_op jit(solution)/shard_map/ppermute | solution.py:193
  20.1 0.0 collective-permute-done.2.second
  20.1 2.5 %shard_map.68 = (f32[256,1152]{1,0:T(8,128)S(1)}, f32[24,128]{1,0:T(8,128)S(1)}, bf16[256,1152]{1,0:T(8,128)(2,1)S(1)}) custom-call(f32[4]{0:T(128)S(1)} %pad_maximum_fusion.scalars, bf16[256,1152]{1,0:T(8,128)(2,1)S(1)} %get-tuple-element.38.own, bf16[256,1152]{1,0:T(8,128)(2,1)S(1)} %collective-permute-done.1.first.outer, ...), custom_call_target="tpu_custom_call" | custom-call | flops 603979776 | bytes 7077888 | tf_op jit(solution)/shard_map/pallas_call | solution.py:170
  22.7 0.0 copy-done.8
  22.7 7.2 %collective-permute-done.first.outer = bf16[256,1152]{1,0:T(8,128)(2,1)S(1)} collective-permute-done((bf16[256,1152]{1,0:T(8,128)(2,1)}, bf16[256,1152]{1,0:T(8,128)(2,1)S(1)}, u32[]{:S(2)}, u32[]{:S(2)}) %collective-permute-start) | collective-permute-done | bytes 589856 | tf_op jit(solution)/shard_map/ppermute | solution.py:193
  29.8 1.8 %collective-permute-start.3 = (bf16[256,1152]{1,0:T(8,128)(2,1)S(1)}, bf16[256,1152]{1,0:T(8,128)(2,1)S(1)}, u32[]{:S(2)}, u32[]{:S(2)}) collective-permute-start(bf16[256,1152]{1,0:T(8,128)(2,1)S(1)} %collective-permute-done.first.outer), channel_id=1, source_target_pairs={{0,8},{2,10},{4,28},{6,30},{8,16},{10,18},{12,4},{14,6},{16,24},{1... | collective-permute-start | bytes 1769480 | tf_op jit(solution)/shard_map/ppermute | solution.py:193
  31.6 0.0 collective-permute-done.5.second
  31.6 1.9 %collective-permute-done.4.inner.far = bf16[256,1152]{1,0:T(8,128)(2,1)S(1)} collective-permute-done((bf16[256,1152]{1,0:T(8,128)(2,1)S(1)}, bf16[256,1152]{1,0:T(8,128)(2,1)S(1)}, u32[]{:S(2)}, u32[]{:S(2)}) %collective-permute-start.4) | collective-permute-done | bytes 589856 | tf_op jit(solution)/shard_map/ppermute | solution.py:193
  33.5 0.7 %shard_map.69 = bf16[256,1152]{1,0:T(8,128)(2,1)S(1)} custom-call(f32[4]{0:T(128)S(1)} %pad_maximum_fusion.scalars, bf16[256,1152]{1,0:T(8,128)(2,1)S(1)} %collective-permute-done.1.first.outer, bf16[256,1152]{1,0:T(8,128)(2,1)S(1)} %collective-permute-done.4.inner.far), custom_call_target="tpu_custom_call" | custom-call | flops 301989888 | bytes 3538944 | tf_op jit(solution)/shard_map/pallas_call | solution.py:170
  34.2 1.5 %collective-permute-start.6 = (bf16[256,1152]{1,0:T(8,128)(2,1)S(1)}, bf16[256,1152]{1,0:T(8,128)(2,1)S(1)}, u32[]{:S(2)}, u32[]{:S(2)}) collective-permute-start(bf16[256,1152]{1,0:T(8,128)(2,1)S(1)} %shard_map.69), channel_id=1, source_target_pairs={{0,2},{2,0},{4,6},{6,4},{8,10},{10,8},{12,14},{14,12},{16,18},{18,... | collective-permute-start | bytes 1769480 | tf_op jit(solution)/shard_map/ppermute | solution.py:193
  35.7 3.0 %shard_map.70 = (f32[256,1152]{1,0:T(8,128)S(1)}, bf16[256,1152]{1,0:T(8,128)(2,1)S(1)}, bf16[128,1152]{1,0:T(8,128)(2,1)}) custom-call(f32[4]{0:T(128)S(1)} %pad_maximum_fusion.scalars, bf16[256,1152]{1,0:T(8,128)(2,1)S(1)} %get-tuple-element.46.own, bf16[256,1152]{1,0:T(8,128)(2,1)S(1)} %collective-permute-done.first.outer, ...), custom_call_target="tpu_custom_call" | custom-call | flops 603979776 | bytes 7077888 | tf_op jit(solution)/shard_map/pallas_call | solution.py:170
  38.7 1.0 %copy-done = f32[256,1152]{1,0:T(8,128)} copy-done((f32[256,1152]{1,0:T(8,128)}, f32[256,1152]{1,0:T(8,128)S(1)}, u32[]{:S(2)}) %copy-start) | copy-done | bytes 1179672
  39.7 2.9 %shard_map.71 = (f32[256,1152]{1,0:T(8,128)S(1)}, f32[32,4,128]{2,1,0:T(4,128)}) custom-call(f32[4]{0:T(128)S(1)} %pad_maximum_fusion.scalars, bf16[256,1152]{1,0:T(8,128)(2,1)S(1)} %get-tuple-element.38.own, bf16[256,1152]{1,0:T(8,128)(2,1)S(1)} %collective-permute-done.4.inner.far, bf16[256,1152]{1,0:T(8,128)(2,1)S(1)} %get-tuple-element.53.near_image, ...), custom_call_target="tpu_custom_call" | custom-call | flops 603979776 | bytes 7077888 | tf_op jit(solution)/shard_map/pallas_call | solution.py:170
  42.7 3.5 %collective-permute-done.3.far.inner = bf16[256,1152]{1,0:T(8,128)(2,1)S(1)} collective-permute-done((bf16[256,1152]{1,0:T(8,128)(2,1)S(1)}, bf16[256,1152]{1,0:T(8,128)(2,1)S(1)}, u32[]{:S(2)}, u32[]{:S(2)}) %collective-permute-start.3) | collective-permute-done | bytes 589856 | tf_op jit(solution)/shard_map/ppermute | solution.py:193
  46.2 0.6 shard_map.74
  46.8 0.0 copy-done.2
  46.8 1.5 %collective-permute-start.8 = (bf16[128,1152]{1,0:T(8,128)(2,1)S(1)}, bf16[128,1152]{1,0:T(8,128)(2,1)S(1)}, u32[]{:S(2)}, u32[]{:S(2)}) collective-permute-start(bf16[128,1152]{1,0:T(8,128)(2,1)S(1)} %shard_map.74), channel_id=1, source_target_pairs={{0,2},{2,0},{4,6},{6,4},{8,10},{10,8},{12,14},{14,12},{16,18},{18,... | collective-permute-start | bytes 884744 | tf_op jit(solution)/shard_map/ppermute | solution.py:193
  48.3 0.8 %collective-permute-start.7 = (bf16[128,1152]{1,0:T(8,128)(2,1)}, bf16[128,1152]{1,0:T(8,128)(2,1)S(1)}, u32[]{:S(2)}, u32[]{:S(2)}) collective-permute-start(bf16[128,1152]{1,0:T(8,128)(2,1)} %get-tuple-element.68), channel_id=1, source_target_pairs={{0,4},{2,30},{4,8},{6,2},{8,12},{10,6},{12,16},{14,10},{16,20},{18... | collective-permute-start | bytes 884744 | tf_op jit(solution)/shard_map/ppermute | solution.py:193
  49.1 0.0 collective-permute-done.6.refs_0_
  49.1 4.6 %all-to-all-start = ((f32[32,4,128]{2,1,0:T(4,128)}), f32[32,4,128]{2,1,0:T(4,128)S(1)}, u32[]{:S(2)}, u32[]{:S(2)}) async-start(f32[32,4,128]{2,1,0:T(4,128)} %get-tuple-element.72), calls=%async_computation | async-start | bytes 131072 | tf_op jit(solution)/shard_map/all_to_all | solution.py:245
  53.7 0.0 copy-start.3
  53.8 0.0 copy-start.5
  53.8 0.0 copy-start.11
  53.8 1.6 %shard_map.72.refs_3_ = f32[256,1152]{1,0:T(8,128)S(1)} custom-call(f32[4]{0:T(128)S(1)} %pad_maximum_fusion.scalars, bf16[256,1152]{1,0:T(8,128)(2,1)S(1)} %get-tuple-element.46.own, bf16[256,1152]{1,0:T(8,128)(2,1)S(1)} %collective-permute-done.3.far.inner), custom_call_target="tpu_custom_call" | custom-call | flops 301989888 | bytes 3538944 | tf_op jit(solution)/shard_map/pallas_call | solution.py:170
  55.4 0.0 copy-done.3
  55.4 0.0 copy-done.5
  55.4 0.0 copy-done.11
  55.5 0.0 copy-start.1
  55.5 0.0 copy-start.7
  55.5 0.0 copy-start.9
  55.5 2.8 %shard_map.73 = f32[256,1152]{1,0:T(8,128)} custom-call(f32[4]{0:T(128)S(1)} %pad_maximum_fusion.scalars, bf16[256,1152]{1,0:T(8,128)(2,1)S(1)} %get-tuple-element.38.own, bf16[256,1152]{1,0:T(8,128)(2,1)S(1)} %collective-permute-done.6.refs_0_, f32[256,1152]{1,0:T(8,128)S(1)} %copy-done.3, bf16[256,1152]{1,0:T(8,128)(2,1)S(1)} %copy-done.5, ...), custom_call_target="tpu_custom_call" | custom-call | flops 301989888 | bytes 3538944 | tf_op jit(solution)/shard_map/pallas_call | solution.py:170
  58.3 0.0 collective-permute-done.8.refs_1_
  58.3 0.0 collective-permute-done.7.refs_0_
  58.3 0.0 copy-done.1
  58.4 2.9 %shard_map.75 = f32[256,1152]{1,0:T(8,128)} custom-call(f32[4]{0:T(128)S(1)} %pad_maximum_fusion.scalars, bf16[256,1152]{1,0:T(8,128)(2,1)S(1)} %get-tuple-element.46.own, bf16[128,1152]{1,0:T(8,128)(2,1)S(1)} %collective-permute-done.7.refs_0_, bf16[128,1152]{1,0:T(8,128)(2,1)S(1)} %collective-permute-done.8.refs_1_, f32[256,1152]{1,0:T(8,128)S(1)} %copy-done.1, ...), custom_call_target="tpu_custom_call" | custom-call | flops 301989888 | bytes 3538944 | tf_op jit(solution)/shard_map/pallas_call | solution.py:170
  61.2 0.0 all-to-all-done
  61.2 0.6 slice_reduce_fusion
  (7 shorter events, 0.0 us)
Async XLA Ops:
  0.6 17.4 %collective-permute-start.1 = (bf16[256,1152]{1,0:T(8,128)(2,1)}, bf16[256,1152]{1,0:T(8,128)(2,1)S(1)}, u32[]{:S(2)}, u32[]{:S(2)}) collective-permute-start(bf16[256,1152]{1,0:T(8,128)(2,1)} %refs_4_.1), channel_id=1, source_target_pairs={{0,4},{2,6},{4,0},{6,2},{8,12},{10,14},{12,8},{14,10},{16,20},{18,... | collective-permute-start | bytes 1769480 | tf_op jit(solution)/shard_map/ppermute | solution.py:193
  3.7 16.5 %collective-permute-start.2 = (bf16[256,1152]{1,0:T(8,128)(2,1)}, bf16[256,1152]{1,0:T(8,128)(2,1)S(1)}, u32[]{:S(2)}, u32[]{:S(2)}) collective-permute-start(bf16[256,1152]{1,0:T(8,128)(2,1)} %refs_4_.1), channel_id=1, source_target_pairs={{0,2},{2,0},{4,6},{6,4},{8,10},{10,8},{12,14},{14,12},{16,18},{18,... | collective-permute-start | bytes 1769480 | tf_op jit(solution)/shard_map/ppermute | solution.py:193
  5.2 24.7 %collective-permute-start = (bf16[256,1152]{1,0:T(8,128)(2,1)}, bf16[256,1152]{1,0:T(8,128)(2,1)S(1)}, u32[]{:S(2)}, u32[]{:S(2)}) collective-permute-start(bf16[256,1152]{1,0:T(8,128)(2,1)} %refs_2_.1), channel_id=1, source_target_pairs={{0,4},{2,6},{4,0},{6,2},{8,12},{10,14},{12,8},{14,10},{16,20},{18,... | collective-permute-start | bytes 1769480 | tf_op jit(solution)/shard_map/ppermute | solution.py:193
  5.7 26.0 %collective-permute-start.5 = (bf16[256,1152]{1,0:T(8,128)(2,1)}, bf16[256,1152]{1,0:T(8,128)(2,1)S(1)}, u32[]{:S(2)}, u32[]{:S(2)}) collective-permute-start(bf16[256,1152]{1,0:T(8,128)(2,1)} %refs_2_.1), channel_id=1, source_target_pairs={{0,2},{2,0},{4,6},{6,4},{8,10},{10,8},{12,14},{14,12},{16,18},{18,... | collective-permute-start | bytes 1769480 | tf_op jit(solution)/shard_map/ppermute | solution.py:193
  7.2 1.1 %copy-start.4 = (bf16[256,1152]{1,0:T(8,128)(2,1)S(1)}, bf16[256,1152]{1,0:T(8,128)(2,1)}, u32[]{:S(2)}) copy-start(bf16[256,1152]{1,0:T(8,128)(2,1)} %refs_2_.1) | copy-start | bytes 1769476
  8.3 1.1 %copy-start.6 = (bf16[256,1152]{1,0:T(8,128)(2,1)S(1)}, bf16[256,1152]{1,0:T(8,128)(2,1)}, u32[]{:S(2)}) copy-start(bf16[256,1152]{1,0:T(8,128)(2,1)} %refs_4_.1) | copy-start | bytes 1769476
  12.1 0.7 %copy-start.10 = (f32[256,128]{1,0:T(8,128)}, f32[256,128]{1,0:T(8,128)S(1)}, u32[]{:S(2)}) copy-start(f32[256,128]{1,0:T(8,128)S(1)} %get-tuple-element.66.refs_3_) | copy-start | bytes 393220
  12.7 9.9 %copy-start.8 = (f32[256,128]{1,0:T(8,128)}, f32[256,128]{1,0:T(8,128)S(1)}, u32[]{:S(2)}) copy-start(f32[256,128]{1,0:T(8,128)S(1)} %get-tuple-element.71.refs_5_) | copy-start | bytes 393220
  18.0 15.5 %collective-permute-start.4 = (bf16[256,1152]{1,0:T(8,128)(2,1)S(1)}, bf16[256,1152]{1,0:T(8,128)(2,1)S(1)}, u32[]{:S(2)}, u32[]{:S(2)}) collective-permute-start(bf16[256,1152]{1,0:T(8,128)(2,1)S(1)} %collective-permute-done.1.first.outer), channel_id=1, source_target_pairs={{0,8},{2,10},{4,28},{6,30},{8,16},{10,18},{12,4},{14,6},{16,24},{1... | collective-permute-start | bytes 1769480 | tf_op jit(solution)/shard_map/ppermute | solution.py:193
  29.8 16.3 %collective-permute-start.3 = (bf16[256,1152]{1,0:T(8,128)(2,1)S(1)}, bf16[256,1152]{1,0:T(8,128)(2,1)S(1)}, u32[]{:S(2)}, u32[]{:S(2)}) collective-permute-start(bf16[256,1152]{1,0:T(8,128)(2,1)S(1)} %collective-permute-done.first.outer), channel_id=1, source_target_pairs={{0,8},{2,10},{4,28},{6,30},{8,16},{10,18},{12,4},{14,6},{16,24},{1... | collective-permute-start | bytes 1769480 | tf_op jit(solution)/shard_map/ppermute | solution.py:193
  34.2 14.9 %collective-permute-start.6 = (bf16[256,1152]{1,0:T(8,128)(2,1)S(1)}, bf16[256,1152]{1,0:T(8,128)(2,1)S(1)}, u32[]{:S(2)}, u32[]{:S(2)}) collective-permute-start(bf16[256,1152]{1,0:T(8,128)(2,1)S(1)} %shard_map.69), channel_id=1, source_target_pairs={{0,2},{2,0},{4,6},{6,4},{8,10},{10,8},{12,14},{14,12},{16,18},{18,... | collective-permute-start | bytes 1769480 | tf_op jit(solution)/shard_map/ppermute | solution.py:193
  38.7 1.0 %copy-start = (f32[256,1152]{1,0:T(8,128)}, f32[256,1152]{1,0:T(8,128)S(1)}, u32[]{:S(2)}) copy-start(f32[256,1152]{1,0:T(8,128)S(1)} %get-tuple-element.69.refs_2_) | copy-start | bytes 3538948
  42.7 4.1 %copy-start.2 = (f32[256,1152]{1,0:T(8,128)}, f32[256,1152]{1,0:T(8,128)S(1)}, u32[]{:S(2)}) copy-start(f32[256,1152]{1,0:T(8,128)S(1)} %get-tuple-element.65.refs_1_) | copy-start | bytes 3538948
  46.8 11.6 %collective-permute-start.8 = (bf16[128,1152]{1,0:T(8,128)(2,1)S(1)}, bf16[128,1152]{1,0:T(8,128)(2,1)S(1)}, u32[]{:S(2)}, u32[]{:S(2)}) collective-permute-start(bf16[128,1152]{1,0:T(8,128)(2,1)S(1)} %shard_map.74), channel_id=1, source_target_pairs={{0,2},{2,0},{4,6},{6,4},{8,10},{10,8},{12,14},{14,12},{16,18},{18,... | collective-permute-start | bytes 884744 | tf_op jit(solution)/shard_map/ppermute | solution.py:193
  48.3 10.0 %collective-permute-start.7 = (bf16[128,1152]{1,0:T(8,128)(2,1)}, bf16[128,1152]{1,0:T(8,128)(2,1)S(1)}, u32[]{:S(2)}, u32[]{:S(2)}) collective-permute-start(bf16[128,1152]{1,0:T(8,128)(2,1)} %get-tuple-element.68), channel_id=1, source_target_pairs={{0,4},{2,30},{4,8},{6,2},{8,12},{10,6},{12,16},{14,10},{16,20},{18... | collective-permute-start | bytes 884744 | tf_op jit(solution)/shard_map/ppermute | solution.py:193
  49.1 12.2 %all-to-all-start = ((f32[32,4,128]{2,1,0:T(4,128)}), f32[32,4,128]{2,1,0:T(4,128)S(1)}, u32[]{:S(2)}, u32[]{:S(2)}) async-start(f32[32,4,128]{2,1,0:T(4,128)} %get-tuple-element.72), calls=%async_computation | async-start | bytes 131072 | tf_op jit(solution)/shard_map/all_to_all | solution.py:245
  53.7 1.7 %copy-start.3 = (f32[256,1152]{1,0:T(8,128)S(1)}, f32[256,1152]{1,0:T(8,128)}, u32[]{:S(2)}) copy-start(f32[256,1152]{1,0:T(8,128)} %copy-done.2) | copy-start | bytes 3538948
  53.8 1.7 %copy-start.5 = (bf16[256,1152]{1,0:T(8,128)(2,1)S(1)}, bf16[256,1152]{1,0:T(8,128)(2,1)}, u32[]{:S(2)}) copy-start(bf16[256,1152]{1,0:T(8,128)(2,1)} %refs_2_.1) | copy-start | bytes 1769476
  53.8 1.7 %copy-start.11 = (f32[256,128]{1,0:T(8,128)S(1)}, f32[256,128]{1,0:T(8,128)}, u32[]{:S(2)}) copy-start(f32[256,128]{1,0:T(8,128)} %copy-done.10) | copy-start | bytes 393220
  55.5 2.9 %copy-start.1 = (f32[256,1152]{1,0:T(8,128)S(1)}, f32[256,1152]{1,0:T(8,128)}, u32[]{:S(2)}) copy-start(f32[256,1152]{1,0:T(8,128)} %copy-done) | copy-start | bytes 3538948
  55.5 2.9 %copy-start.7 = (bf16[256,1152]{1,0:T(8,128)(2,1)S(1)}, bf16[256,1152]{1,0:T(8,128)(2,1)}, u32[]{:S(2)}) copy-start(bf16[256,1152]{1,0:T(8,128)(2,1)} %refs_4_.1) | copy-start | bytes 1769476
  55.5 2.9 %copy-start.9 = (f32[256,128]{1,0:T(8,128)S(1)}, f32[256,128]{1,0:T(8,128)}, u32[]{:S(2)}) copy-start(f32[256,128]{1,0:T(8,128)} %copy-done.8) | copy-start | bytes 393220
